TPU v7x, 32 devices: a whole 2x2x4 slice. The times are simulated.
32 devices in a mesh: clip: 8 (over z, x), frame: 4 (over y, core).
Axes of the slice: x: 2, y: 2, z: 4, core: 2. Of those that a mesh axis runs over, the one named last changes fastest.
Arguments:
- clips_in: bfloat16 [32, 16, 196, 768], P('clip', 'frame'), may hold values from -6 to 6
- teacher: bfloat16 [32, 16, 196, 768], P('clip', 'frame'), may hold values from -6 to 6
- valid: int32 [32, 16, 196], P('clip', 'frame'), may hold values from 0 to 1, as said below
- norm_gain: bfloat16 [768, 3], P(('clip', 'frame')), may hold values from 0.5 to 1.5
- norm_shift: bfloat16 [768, 3], P(('clip', 'frame')), may hold values from -1.796875 to 1.796875
- w_space: bfloat16 [768, 2304], P(('clip', 'frame')), may hold values from -0.21875 to 0.21875
- qv_bias: bfloat16 [768, 4], P(('clip', 'frame')), may hold values from -1.796875 to 1.796875
- w_space_out: bfloat16 [768, 768], P(('clip', 'frame')), may hold values from -1.75 to 1.75
- mix_bias: bfloat16 [768, 3], P(('clip', 'frame')), may hold values from -1.796875 to 1.796875
- w_time: bfloat16 [768, 2304], P(('clip', 'frame')), may hold values from -0.21875 to 0.21875
- w_time_out: bfloat16 [768, 768], P(('clip', 'frame')), may hold values from -0.875 to 0.875
- w_up: bfloat16 [768, 3072], P(('clip', 'frame')), may hold values from -0.21875 to 0.21875
- up_bias: bfloat16 [3072], P(('clip', 'frame')), may hold values from -3 to 3
- w_down: bfloat16 [3072, 768], P(('clip', 'frame')), may hold values from -0.109375 to 0.109375
Outputs:
- layer_out: bfloat16 [32, 16, 196, 768], P('clip', 'frame')
- loss_value: float32 [], replicated
- input_grad: bfloat16 [32, 16, 196, 768], P('clip', 'frame')
- gain_grad: float32 [768, 3], P(('clip', 'frame'))
- shift_grad: float32 [768, 3], P(('clip', 'frame'))
- w_space_grad: float32 [768, 2304], P(('clip', 'frame'))
- qv_bias_grad: float32 [768, 3], P(('clip', 'frame'))
- time_query_bias_grad: float32 [768], P(('clip', 'frame'))
- w_space_out_grad: float32 [768, 768], P(('clip', 'frame'))
- mix_bias_grad: float32 [768, 3], P(('clip', 'frame'))
- w_time_grad: float32 [768, 2304], P(('clip', 'frame'))
- w_time_out_grad: float32 [768, 768], P(('clip', 'frame'))
- w_up_grad: float32 [768, 3072], P(('clip', 'frame'))
- up_bias_grad: float32 [3072], P(('clip', 'frame'))
- w_down_grad: float32 [3072, 768], P(('clip', 'frame'))
Inputs may be any that keep to these rules, and one draw needn't show every extreme that they name: The first place of the first frame of every clip is valid.
All inputs are finite; a program needn't handle non-finite values.
Results may differ from a plain program's by a relative error of at most 0.009.
Values may be sent and summed in bfloat16 or wider, within the bound.
A program may use at most 640 MiB of HBM per device.

v0:
```python
import jax
import jax.numpy as jnp
from jax import lax
from jax.sharding import PartitionSpec as P

D = 768
HEADS = 12
HEAD = 64
MICRO = 2


EPS = 1e-06


def matmul(left, right):
    return jnp.dot(left, right, preferred_element_type=jnp.float32)


def matmul_tn(left, right):
    return lax.dot_general(
        left, right, (((0,), (0,)), ((), ())), preferred_element_type=jnp.float32
    )


def matmul_nt(left, right):
    return lax.dot_general(
        left, right, (((1,), (1,)), ((), ())), preferred_element_type=jnp.float32
    )


def norm_apply(inputs, gain, shift):
    center = inputs - jnp.mean(inputs, -1, keepdims=True)
    inverse = lax.rsqrt(jnp.mean(center * center, -1, keepdims=True) + EPS)
    normed = center * inverse
    return (normed * gain + shift, normed, inverse)


def norm_back(grad_out, normed, inverse, gain):
    grad_hat = grad_out * gain
    grad_in = inverse * (
        grad_hat
        - jnp.mean(grad_hat, -1, keepdims=True)
        - normed * jnp.mean(grad_hat * normed, -1, keepdims=True)
    )
    return (grad_in, jnp.sum(grad_out * normed, 0), jnp.sum(grad_out, 0))


def softmax_stats(scores):
    top = jnp.max(scores, -1, keepdims=True)
    expo = jnp.exp(scores - top)
    total = jnp.sum(expo, -1, keepdims=True)
    return (expo / total, top + jnp.log(total))


def space_scores(q_rows, k_rows, groups):
    shape = (groups, -1, HEADS, HEAD)
    return jnp.einsum(
        "gphe,gqhe->ghpq",
        q_rows.reshape(shape),
        k_rows.reshape(shape),
        preferred_element_type=jnp.float32,
    ) * HEAD ** (-0.5)


def space_forward(q_rows, k_rows, v_rows, groups):
    probs, log_total = softmax_stats(space_scores(q_rows, k_rows, groups))
    mixed = jnp.einsum(
        "ghpq,gqhe->gphe",
        probs.astype(jnp.bfloat16),
        v_rows.reshape((groups, -1, HEADS, HEAD)),
        preferred_element_type=jnp.float32,
    )
    return (mixed.reshape(q_rows.shape).astype(jnp.bfloat16), log_total)


def space_back(q_rows, k_rows, v_rows, log_total, grad_mix, groups):
    shape = (groups, -1, HEADS, HEAD)
    probs = jnp.exp(space_scores(q_rows, k_rows, groups) - log_total)
    grad_heads = grad_mix.reshape(shape)
    grad_v = jnp.einsum(
        "ghpq,gphe->gqhe",
        probs.astype(jnp.bfloat16),
        grad_heads,
        preferred_element_type=jnp.float32,
    )
    grad_p = jnp.einsum(
        "gphe,gqhe->ghpq", grad_heads, v_rows.reshape(shape), preferred_element_type=jnp.float32
    )
    grad_s = (probs * (grad_p - jnp.sum(probs * grad_p, -1, keepdims=True))).astype(jnp.bfloat16)
    grad_q = jnp.einsum(
        "ghpq,gqhe->gphe", grad_s, k_rows.reshape(shape), preferred_element_type=jnp.float32
    )
    grad_k = jnp.einsum(
        "ghpq,gphe->gqhe", grad_s, q_rows.reshape(shape), preferred_element_type=jnp.float32
    )
    factor = HEAD ** (-0.5)
    return (
        grad_q.reshape(q_rows.shape) * factor,
        grad_k.reshape(q_rows.shape) * factor,
        grad_v.reshape(q_rows.shape),
    )


def split_heads(block):
    return block.reshape(block.shape[:3] + (HEADS, HEAD))


def time_scores(q_block, keys_full):
    return jnp.einsum(
        "bfphe,btphe->bphft",
        split_heads(q_block),
        split_heads(keys_full),
        preferred_element_type=jnp.float32,
    ) * HEAD ** (-0.5)


def time_forward(q_block, keys_full, values_full):
    probs, log_total = softmax_stats(time_scores(q_block, keys_full))
    mixed = jnp.einsum(
        "bphft,btphe->bfphe",
        probs.astype(jnp.bfloat16),
        split_heads(values_full),
        preferred_element_type=jnp.float32,
    )
    return (mixed.reshape(q_block.shape).astype(jnp.bfloat16), log_total)


def time_back(q_block, keys_full, values_full, log_total, grad_mix):
    probs = jnp.exp(time_scores(q_block, keys_full) - log_total)
    grad_heads = split_heads(grad_mix)
    grad_v = jnp.einsum(
        "bphft,bfphe->btphe",
        probs.astype(jnp.bfloat16),
        grad_heads,
        preferred_element_type=jnp.float32,
    )
    grad_p = jnp.einsum(
        "bfphe,btphe->bphft",
        grad_heads,
        split_heads(values_full),
        preferred_element_type=jnp.float32,
    )
    grad_s = (probs * (grad_p - jnp.sum(probs * grad_p, -1, keepdims=True))).astype(jnp.bfloat16)
    grad_q = jnp.einsum(
        "bphft,btphe->bfphe", grad_s, split_heads(keys_full), preferred_element_type=jnp.float32
    )
    grad_k = jnp.einsum(
        "bphft,bfphe->btphe", grad_s, split_heads(q_block), preferred_element_type=jnp.float32
    )
    factor = HEAD ** (-0.5)
    return (
        grad_q.reshape(q_block.shape) * factor,
        grad_k.reshape(keys_full.shape) * factor,
        grad_v.reshape(keys_full.shape),
    )


def forward(inputs, params):
    (
        gain,
        shift,
        w_space,
        qv_bias,
        w_space_out,
        mix_bias,
        w_time,
        w_time_out,
        w_up,
        up_bias,
        w_down,
    ) = params
    gain = gain.astype(jnp.float32)
    shift = shift.astype(jnp.float32)
    qv_float = qv_bias.astype(jnp.float32)
    mix_float = mix_bias.astype(jnp.float32)
    batch, frames, places, width = inputs.shape
    groups = batch * frames
    rows = inputs.reshape(-1, width)
    normed_a, hat_a, inv_a = norm_apply(rows, gain[:, 0], shift[:, 0])
    in_a = normed_a.astype(jnp.bfloat16)
    proj_a = matmul(in_a, w_space)
    q_a = (proj_a[:, :width] + qv_float[:, 0]).astype(jnp.bfloat16)
    k_a = proj_a[:, width : 2 * width].astype(jnp.bfloat16)
    v_a = (proj_a[:, 2 * width :] + qv_float[:, 1]).astype(jnp.bfloat16)
    mix_a, lse_a = space_forward(q_a, k_a, v_a, groups)
    after_a = rows + matmul(mix_a, w_space_out) + mix_float[:, 0]
    normed_b, hat_b, inv_b = norm_apply(after_a, gain[:, 1], shift[:, 1])
    in_b = normed_b.astype(jnp.bfloat16)
    proj_b = matmul(in_b, w_time)
    q_b = (proj_b[:, :width] + qv_float[:, 2]).astype(jnp.bfloat16).reshape(inputs.shape)
    k_b = proj_b[:, width : 2 * width].astype(jnp.bfloat16).reshape(inputs.shape)
    v_b = (proj_b[:, 2 * width :] + qv_float[:, 3]).astype(jnp.bfloat16).reshape(inputs.shape)
    keys_full, values_full = (
        lax.all_gather(k_b, "frame", axis=1, tiled=True),
        lax.all_gather(v_b, "frame", axis=1, tiled=True),
    )
    mix_b, lse_b = time_forward(q_b, keys_full, values_full)
    time_saved = (q_b, keys_full, values_full)
    mix_b = mix_b.reshape(-1, width)
    after_b = after_a + matmul(mix_b, w_time_out) + mix_float[:, 1]
    normed_c, hat_c, inv_c = norm_apply(after_b, gain[:, 2], shift[:, 2])
    in_c = normed_c.astype(jnp.bfloat16)
    pre_act = matmul(in_c, w_up) + up_bias.astype(jnp.float32)
    hidden = jax.nn.gelu(pre_act, approximate=False).astype(jnp.bfloat16)
    result = after_b + matmul(hidden, w_down) + mix_float[:, 2]
    saved = (
        in_a,
        hat_a,
        inv_a,
        q_a,
        k_a,
        v_a,
        lse_a,
        mix_a,
        in_b,
        hat_b,
        inv_b,
        time_saved,
        lse_b,
        mix_b,
        in_c,
        hat_c,
        inv_c,
        pre_act,
        hidden,
        groups,
        inputs.shape,
    )
    return (result, saved)


def backward(params, saved, grad_rows):
    (
        gain,
        shift,
        w_space,
        qv_bias,
        w_space_out,
        mix_bias,
        w_time,
        w_time_out,
        w_up,
        up_bias,
        w_down,
    ) = params
    gain = gain.astype(jnp.float32)
    (
        in_a,
        hat_a,
        inv_a,
        q_a,
        k_a,
        v_a,
        lse_a,
        mix_a,
        in_b,
        hat_b,
        inv_b,
        time_saved,
        lse_b,
        mix_b,
        in_c,
        hat_c,
        inv_c,
        pre_act,
        hidden,
        groups,
        block_shape,
    ) = saved
    width = in_a.shape[1]
    grad_z3 = grad_rows.astype(jnp.bfloat16)
    down_grad = matmul_tn(hidden, grad_z3)
    bias_c = jnp.sum(grad_z3.astype(jnp.float32), 0)
    grad_hidden = matmul_nt(grad_z3, w_down)
    slope = (
        0.5 * (1.0 + lax.erf(pre_act * 0.7071067811865476))
        + pre_act * jnp.exp(-0.5 * pre_act * pre_act) * 0.3989422804014327
    )
    grad_pre = (grad_hidden * slope).astype(jnp.bfloat16)
    up_grad = matmul_tn(in_c, grad_pre)
    up_bias_grad = jnp.sum(grad_pre.astype(jnp.float32), 0)
    back_c, gain_c, shift_c = norm_back(matmul_nt(grad_pre, w_up), hat_c, inv_c, gain[:, 2])
    grad_after_b = grad_rows + back_c
    grad_z2 = grad_after_b.astype(jnp.bfloat16)
    time_out_grad = matmul_tn(mix_b, grad_z2)
    bias_b = jnp.sum(grad_z2.astype(jnp.float32), 0)
    grad_mix_b = matmul_nt(grad_z2, w_time_out).astype(jnp.bfloat16).reshape(block_shape)
    q_keep, k_keep, v_keep = time_saved
    grad_q_b, grad_k_full, grad_v_full = time_back(q_keep, k_keep, v_keep, lse_b, grad_mix_b)
    grad_k_b, grad_v_b = (
        lax.psum_scatter(
            grad_k_full.astype(jnp.bfloat16), "frame", scatter_dimension=1, tiled=True
        ).astype(jnp.float32),
        lax.psum_scatter(
            grad_v_full.astype(jnp.bfloat16), "frame", scatter_dimension=1, tiled=True
        ).astype(jnp.float32),
    )
    grad_proj_b = jnp.concatenate(
        [
            grad_q_b.reshape(-1, width).astype(jnp.bfloat16),
            grad_k_b.reshape(-1, width).astype(jnp.bfloat16),
            grad_v_b.reshape(-1, width).astype(jnp.bfloat16),
        ],
        -1,
    )
    time_grad = matmul_tn(in_b, grad_proj_b)
    sums_b = jnp.sum(grad_proj_b.astype(jnp.float32), 0)
    back_b, gain_b, shift_b = norm_back(matmul_nt(grad_proj_b, w_time), hat_b, inv_b, gain[:, 1])
    grad_after_a = grad_after_b + back_b
    grad_z1 = grad_after_a.astype(jnp.bfloat16)
    space_out_grad = matmul_tn(mix_a, grad_z1)
    bias_a = jnp.sum(grad_z1.astype(jnp.float32), 0)
    grad_mix_a = matmul_nt(grad_z1, w_space_out).astype(jnp.bfloat16)
    grad_q_a, grad_k_a, grad_v_a = space_back(q_a, k_a, v_a, lse_a, grad_mix_a, groups)
    grad_proj_a = jnp.concatenate([grad_q_a, grad_k_a, grad_v_a], -1).astype(jnp.bfloat16)
    space_grad = matmul_tn(in_a, grad_proj_a)
    sums_a = jnp.sum(grad_proj_a.astype(jnp.float32), 0)
    back_a, gain_a, shift_a = norm_back(matmul_nt(grad_proj_a, w_space), hat_a, inv_a, gain[:, 0])
    grad_inputs = grad_after_a + back_a
    grads = (
        jnp.stack([gain_a, gain_b, gain_c], -1),
        jnp.stack([shift_a, shift_b, shift_c], -1),
        space_grad,
        jnp.stack([sums_a[:width], sums_a[2 * width :], sums_b[2 * width :]], -1),
        sums_b[:width],
        space_out_grad,
        jnp.stack([bias_a, bias_b, bias_c], -1),
        time_grad,
        time_out_grad,
        up_grad,
        up_bias_grad,
        down_grad,
    )
    return (grads, grad_inputs)


def shards(
    clips_in,
    teacher,
    valid,
    norm_gain,
    norm_shift,
    w_space,
    qv_bias,
    w_space_out,
    mix_bias,
    w_time,
    w_time_out,
    w_up,
    up_bias,
    w_down,
):
    count = lax.psum(jnp.sum(valid.astype(jnp.float32)), ("clip", "frame"))
    coefficient = 2.0 / (count * D)
    per_micro = clips_in.shape[0] // MICRO
    squares = jnp.zeros((), jnp.float32)
    local_sum = None
    outputs = []
    input_grads = []
    for micro_step in range(MICRO):
        lower = micro_step * per_micro
        gathered = (
            lax.all_gather(norm_gain, ("clip", "frame"), axis=0, tiled=True),
            lax.all_gather(norm_shift, ("clip", "frame"), axis=0, tiled=True),
            lax.all_gather(w_space, ("clip", "frame"), axis=0, tiled=True),
            lax.all_gather(qv_bias, ("clip", "frame"), axis=0, tiled=True),
            lax.all_gather(w_space_out, ("clip", "frame"), axis=0, tiled=True),
            lax.all_gather(mix_bias, ("clip", "frame"), axis=0, tiled=True),
            lax.all_gather(w_time, ("clip", "frame"), axis=0, tiled=True),
            lax.all_gather(w_time_out, ("clip", "frame"), axis=0, tiled=True),
            lax.all_gather(w_up, ("clip", "frame"), axis=0, tiled=True),
            lax.all_gather(up_bias, ("clip", "frame"), axis=0, tiled=True),
            lax.all_gather(w_down, ("clip", "frame"), axis=0, tiled=True),
        )
        inputs = clips_in[lower : lower + per_micro].astype(jnp.float32)
        result, saved = forward(inputs, gathered)
        result = result.reshape(inputs.shape)
        diff = result - teacher[lower : lower + per_micro].astype(jnp.float32)
        keep_mask = valid[lower : lower + per_micro].astype(jnp.float32)[..., None]
        squares = squares + jnp.sum(keep_mask * diff * diff)
        grad_rows = (coefficient * keep_mask * diff).reshape(-1, inputs.shape[-1])
        back_weights = (
            lax.all_gather(norm_gain, ("clip", "frame"), axis=0, tiled=True),
            lax.all_gather(norm_shift, ("clip", "frame"), axis=0, tiled=True),
            lax.all_gather(w_space, ("clip", "frame"), axis=0, tiled=True),
            lax.all_gather(qv_bias, ("clip", "frame"), axis=0, tiled=True),
            lax.all_gather(w_space_out, ("clip", "frame"), axis=0, tiled=True),
            lax.all_gather(mix_bias, ("clip", "frame"), axis=0, tiled=True),
            lax.all_gather(w_time, ("clip", "frame"), axis=0, tiled=True),
            lax.all_gather(w_time_out, ("clip", "frame"), axis=0, tiled=True),
            lax.all_gather(w_up, ("clip", "frame"), axis=0, tiled=True),
            lax.all_gather(up_bias, ("clip", "frame"), axis=0, tiled=True),
            lax.all_gather(w_down, ("clip", "frame"), axis=0, tiled=True),
        )
        grads_micro, grad_inputs = backward(back_weights, saved, grad_rows)
        local_sum = (
            grads_micro if local_sum is None else jax.tree.map(jnp.add, local_sum, grads_micro)
        )
        outputs.append(result.astype(jnp.bfloat16))
        input_grads.append(grad_inputs.reshape(inputs.shape).astype(jnp.bfloat16))
    final = lax.psum_scatter(local_sum, ("clip", "frame"), scatter_dimension=0, tiled=True)
    total = lax.psum(squares, ("clip", "frame"))
    loss_value = total / (count * D)
    return (
        jnp.concatenate(outputs, 0),
        loss_value,
        jnp.concatenate(input_grads, 0),
        final[0],
        final[1],
        final[2],
        final[3],
        final[4],
        final[5],
        final[6],
        final[7],
        final[8],
        final[9],
        final[10],
        final[11],
    )


def solution(mesh):
    in_specs = (
        P("clip", "frame", None, None),
        P("clip", "frame", None, None),
        P("clip", "frame", None),
        P(("clip", "frame"), None),
        P(("clip", "frame"), None),
        P(("clip", "frame"), None),
        P(("clip", "frame"), None),
        P(("clip", "frame"), None),
        P(("clip", "frame"), None),
        P(("clip", "frame"), None),
        P(("clip", "frame"), None),
        P(("clip", "frame"), None),
        P(("clip", "frame")),
        P(("clip", "frame"), None),
    )
    out_specs = (
        P("clip", "frame", None, None),
        P(),
        P("clip", "frame", None, None),
        P(("clip", "frame"), None),
        P(("clip", "frame"), None),
        P(("clip", "frame"), None),
        P(("clip", "frame"), None),
        P(("clip", "frame")),
        P(("clip", "frame"), None),
        P(("clip", "frame"), None),
        P(("clip", "frame"), None),
        P(("clip", "frame"), None),
        P(("clip", "frame"), None),
        P(("clip", "frame")),
        P(("clip", "frame"), None),
    )
    return jax.shard_map(shards, mesh=mesh, in_specs=in_specs, out_specs=out_specs, check_vma=False)
```

profile of v0, /device:TPU:0, one launch (start us, length us, event | category | flops | bytes accessed | tf_op | source)
XLA Modules:
  0.0 2816.3 jit_solution(17977950136183633596)
XLA Ops:
  32.2 43.3 %all-gather = bf16[32,24,3]{1,2,0:T(4,128)(2,1)S(1)} all-gather(bf16[1,24,3]{1,2,0:T(4,128)(2,1)S(1)} %bitcast.220), channel_id=1, replica_groups=mesh['clip'=8,'frame'=4] {'clip','frame'}, dimensions={0}, use_global_device_ids=true | all-gather | bytes 4752 | tf_op jit(solution)/shard_map/all_gather | solution.py:363
  76.4 36.6 %all-gather.1 = bf16[32,24,3]{1,2,0:T(4,128)(2,1)S(1)} all-gather(bf16[1,24,3]{1,2,0:T(4,128)(2,1)S(1)} %bitcast.221), channel_id=1, replica_groups=mesh['clip'=8,'frame'=4] {'clip','frame'}, dimensions={0}, use_global_device_ids=true | all-gather | bytes 4752 | tf_op jit(solution)/shard_map/all_gather | solution.py:364
  113.9 38.0 %all-gather.2 = bf16[32,24,4]{1,2,0:T(4,128)(2,1)S(1)} all-gather(bf16[1,24,4]{1,2,0:T(4,128)(2,1)S(1)} %bitcast.222), channel_id=1, replica_groups=mesh['clip'=8,'frame'=4] {'clip','frame'}, dimensions={0}, use_global_device_ids=true | all-gather | bytes 6336 | tf_op jit(solution)/shard_map/all_gather | solution.py:366
  152.1 36.8 %all-gather.3 = bf16[32,24,3]{1,2,0:T(4,128)(2,1)S(1)} all-gather(bf16[1,24,3]{1,2,0:T(4,128)(2,1)S(1)} %bitcast.223), channel_id=1, replica_groups=mesh['clip'=8,'frame'=4] {'clip','frame'}, dimensions={0}, use_global_device_ids=true | all-gather | bytes 4752 | tf_op jit(solution)/shard_map/all_gather | solution.py:368
  489.2 37.6 %psum.15 = f32[]{:T(128)} all-reduce(f32[]{:T(128)} %convert_reduce_fusion.14), channel_id=1, replica_groups=mesh['clip'=8,'frame'=4] {'clip','frame'}, use_global_device_ids=true, to_apply=%region_24.0 | all-reduce | flops 1 | bytes 8 | tf_op jit(solution)/shard_map/psum | solution.py:353
  527.0 43.1 %all-reduce = bf16[3072]{0:T(1024)(128)(2,1)S(1)} all-reduce(bf16[3072]{0:T(1024)(128)(2,1)S(1)} %dynamic-update-slice), channel_id=1, replica_groups=mesh['clip'=8,'frame'=4] {'clip','frame'}, use_global_device_ids=true, to_apply=%add | all-reduce | flops 3072 | bytes 12288
  592.6 14.8 copy.287
  607.4 26.7 copy.289
  634.2 14.8 copy.306
  649.0 26.4 copy.308
  675.4 14.8 copy.304
  690.2 26.4 copy.309
  716.6 14.7 copy.285
  731.3 26.4 copy.290
  757.7 17.2 multiply_reduce_fusion.6
  774.9 14.3 fusion.49
  790.9 15.7 convert_bitcast_fusion.2
  827.6 17.9 multiply_reduce_fusion.7
  845.4 14.0 fusion.48
  861.2 15.7 convert_bitcast_fusion.3
  898.8 15.1 fusion.123
  914.0 96.5 %fusion.2 = (bf16[1568,3072]{1,0:T(8,128)(2,1)}, bf16[1568,3072]{1,0:T(8,128)(2,1)}, f32[1568,3072]{1,0:T(8,128)}) fusion(f32[3072]{0:T(1024)S(1)} %copy-done.100, f32[1568,3072]{1,0:T(8,128)} %fusion.123, bf16[768,3072]{1,0:T(8,128)(2,1)S(1)} %copy-done.141, f32[1568,768]{1,0:T(8,128)S(1)} %copy-done.17, f32[768]{0:T(1024)S(1)} %copy-done.71, ...), kind=kOutput, calls=%fused_computation.18 | convolution fusion | flops 8040603648 | bytes 67369216 | tf_op jit(solution)/shard_map/dot_general | solution.py:16
  1016.7 13.7 add_add_fusion.3
  1035.6 13.9 add_add_fusion
  1082.7 20.6 convert_reduce_fusion
  1103.3 16.7 multiply_reduce_fusion.8
  1120.0 19.3 convert_reduce_fusion.1
  1139.4 21.2 convert_reduce_fusion.8
  1174.8 21.3 multiply_reduce_fusion.4
  1196.1 26.9 convert_bitcast_fusion
  1243.8 21.5 multiply_reduce_fusion.5
  1265.3 27.3 convert_bitcast_fusion.1
  1292.6 26.2 copy.350
  1318.7 30.6 %copy.351 = bf16[2,16,196,768]{3,0,2,1:T(2,128)(2,1)} copy(bf16[2,16,196,768]{2,3,1,0:T(8,128)(2,1)} %bitcast.194) | data formatting | bytes 19267584 | tf_op jit(solution)/shard_map/convert_element_type | solution.py:295
  1349.4 14.9 multiply_convert_fusion.7
  1379.2 26.5 copy.323
  1405.7 30.7 %copy.324 = bf16[2,16,196,768]{3,0,2,1:T(2,128)(2,1)} copy(bf16[2,16,196,768]{2,3,1,0:T(8,128)(2,1)} %bitcast.195) | data formatting | bytes 19267584 | tf_op jit(solution)/shard_map/convert_element_type | solution.py:295
  1436.4 26.4 copy.319
  1462.8 30.9 %copy.320 = bf16[2,16,196,768]{3,0,2,1:T(2,128)(2,1)} copy(bf16[2,16,196,768]{2,3,1,0:T(8,128)(2,1)} %bitcast.196) | data formatting | bytes 19267584 | tf_op jit(solution)/shard_map/convert_element_type | solution.py:292
  1493.8 14.7 multiply_convert_fusion.5
  1523.5 26.2 copy.346
  1549.7 30.6 %copy.347 = bf16[2,16,196,768]{3,0,2,1:T(2,128)(2,1)} copy(bf16[2,16,196,768]{2,3,1,0:T(8,128)(2,1)} %bitcast.197) | data formatting | bytes 19267584 | tf_op jit(solution)/shard_map/convert_element_type | solution.py:292
  1593.0 13.3 fusion.96
  1606.3 15.3 convolution_add_fusion.2
  1635.3 14.0 fusion.55
  1662.2 13.0 fusion.54
  1695.5 16.7 fusion.119
  1712.3 14.4 convolution_add_fusion.3
  1744.4 321.6 %all-reduce.18.cloned.1.call-done = (bf16[2,16,196,768]{3,0,2,1:T(2,128)(2,1)}, bf16[2,16,196,768]{3,0,2,1:T(2,128)(2,1)}, bf16[2,16,196,768]{3,0,2,1:T(2,128)(2,1)}) async-done(((bf16[2,16,196,768]{3,0,2,1:T(2,128)(2,1)}, bf16[2,16,196,768]{3,0,2,1:T(2,128)(2,1)}, bf16[2,16,196,768]{3,0,2,1:T(2,128)(2,1)}), (bf16[2,16,196,768]{3,0,2,1:T(2,128)(2,1)}, bf16[2,16,196,768]{3,0,2,1:T(2,128)(2,1)}, ...) | async-done | bytes 28901392
  2153.6 19.3 convert_reduce_fusion.9
  2199.2 12.8 convert_bitcast_fusion.4
  2247.4 13.2 convert_bitcast_fusion.5
  2272.5 16.0 multiply_reduce_fusion.1
  2288.5 14.7 multiply_convert_fusion.3
  2351.0 14.2 fusion.117
  2365.3 15.6 multiply_reduce_fusion
  2380.8 14.9 convolution_add_fusion
  2395.8 15.2 multiply_convert_fusion.2
  2465.5 14.6 convolution_add_fusion.1
  2485.7 13.4 multiply_reduce_fusion.13
  2503.6 19.0 multiply_reduce_fusion.10
  2522.9 41.4 %all-reduce.11 = (f32[]{:T(128)}, f32[768,3]{0,1:T(4,128)S(1)}, f32[768,3]{0,1:T(4,128)S(1)}, f32[768,3]{0,1:T(4,128)S(1)}, f32[768]{0:T(1024)S(1)}, /*index=5*/f32[768,3]{0,1:T(4,128)S(1)}, f32[3072]{0:T(1024)S(1)}) all-reduce(f32[]{:T(128)S(6)} %add.434, ...), channel_id=1, replica_groups=mesh['clip'=8,'frame'=4] {'clip','frame'}, use_global_device_ids=true, to_apply=%region_22.0 | all-reduce | flops 13057 | bytes 104456 | tf_op jit(solution)/shard_map/psum | solution.py:402
  2589.4 94.2 %reduce-scatter.15.cloned.1.call-done = f32[24,2304]{1,0:T(8,128)} async-done(((f32[768,2304]{1,0:T(8,128)}), f32[24,2304]{1,0:T(8,128)}) %reduce-scatter.15.cloned.1.call-update) | async-done | bytes 221200 | tf_op jit(solution)/shard_map/reduce_scatter | solution.py:401
  2683.6 124.5 %reduce-scatter.11.cloned.1.call-done = f32[24,2304]{1,0:T(8,128)} async-done(((f32[768,2304]{1,0:T(8,128)}), f32[24,2304]{1,0:T(8,128)}) %reduce-scatter.11.cloned.1.call-update) | async-done | bytes 221200 | tf_op jit(solution)/shard_map/reduce_scatter | solution.py:401
  (643 shorter events, 876.9 us)
Async XLA Ops:
  7.2 205.8 %all-gather.15.cloned.1.call-start = ((), (), s32[]{:S(2)}) async-start(), calls=%async_computation.6 | async-start | bytes 3649536 | tf_op jit(solution)/shard_map/all_gather | solution.py:365
  7.9 320.5 %all-gather.17.cloned.1.call-start = ((), (), s32[]{:S(2)}) async-start(), calls=%async_computation.7 | async-start | bytes 1216512 | tf_op jit(solution)/shard_map/all_gather | solution.py:367
  8.7 328.4 %all-gather.19.cloned.1.call-start = ((), (), s32[]{:S(2)}) async-start(), calls=%async_computation.8 | async-start | bytes 3649536 | tf_op jit(solution)/shard_map/all_gather | solution.py:369
  9.4 583.3 %all-gather.23.cloned.1.call-start = ((), (), s32[]{:S(2)}) async-start(), calls=%async_computation.10 | async-start | bytes 12288000 | tf_op jit(solution)/shard_map/all_gather | solution.py:194
  26.5 49.9 %copy-start.138 = (bf16[24,3]{0,1:T(4,128)(2,1)S(1)}, bf16[24,3]{0,1:T(4,128)(2,1)}, u32[]{:S(2)}) copy-start(bf16[24,3]{0,1:T(4,128)(2,1)} %param.18) | copy-start | bytes 436
  26.5 87.4 %copy-start.139 = (bf16[24,4]{0,1:T(4,128)(2,1)S(1)}, bf16[24,4]{0,1:T(4,128)(2,1)}, u32[]{:S(2)}) copy-start(bf16[24,4]{0,1:T(4,128)(2,1)} %param.20) | copy-start | bytes 580
  26.5 125.5 %copy-start.140 = (bf16[24,3]{0,1:T(4,128)(2,1)S(1)}, bf16[24,3]{0,1:T(4,128)(2,1)}, u32[]{:S(2)}) copy-start(bf16[24,3]{0,1:T(4,128)(2,1)} %param.22) | copy-start | bytes 436
  76.4 145.9 %copy-start.98 = (f32[768]{0:T(1024)}, f32[768]{0:T(1024)S(1)}, u32[]{:S(2)}) copy-start(f32[768]{0:T(1024)S(1)} %get-tuple-element.93) | copy-start | bytes 9220
  76.4 374.6 %copy-start.94 = (f32[768]{0:T(1024)}, f32[768]{0:T(1024)S(1)}, u32[]{:S(2)}) copy-start(f32[768]{0:T(1024)S(1)} %get-tuple-element.92) | copy-start | bytes 9220
  113.9 108.4 %copy-start.131 = (f32[768]{0:T(1024)}, f32[768]{0:T(1024)S(1)}, u32[]{:S(2)}) copy-start(f32[768]{0:T(1024)S(1)} %get-tuple-element.96) | copy-start | bytes 9220
  113.9 337.1 %copy-start.133 = (f32[768]{0:T(1024)}, f32[768]{0:T(1024)S(1)}, u32[]{:S(2)}) copy-start(f32[768]{0:T(1024)S(1)} %get-tuple-element.95) | copy-start | bytes 9220
  190.7 22.3 copy-start.78
  190.8 31.6 %copy-start.119 = (f32[1568]{0:T(1024)}, f32[1568]{0:T(1024)S(1)}, u32[]{:S(2)}) copy-start(f32[1568]{0:T(1024)S(1)} %div.115) | copy-start | bytes 18820
  191.1 31.3 %copy-start.121 = (f32[1568]{0:T(1024)}, f32[1568]{0:T(1024)S(1)}, u32[]{:S(2)}) copy-start(f32[1568]{0:T(1024)S(1)} %rsqrt.55) | copy-start | bytes 18820
  191.3 21.6 copy-start.80
  254.9 34.3 %copy-start.7 = (bf16[8,196,12,64]{1,3,2,0:T(8,128)(2,1)}, bf16[8,196,12,64]{1,3,2,0:T(8,128)(2,1)S(1)}, u32[]{:S(2)}) copy-start(bf16[8,196,12,64]{1,3,2,0:T(8,128)(2,1)S(1)} %copy.279) | copy-start | bytes 7225348
  354.3 279.8 %all-gather.33.cloned.1.call-start = ((), (), s32[]{:S(2)}) async-start(), calls=%async_computation.15 | async-start | bytes 12288000 | tf_op jit(solution)/shard_map/all_gather | solution.py:194
  370.8 34.1 %copy-start.5 = (bf16[8,196,12,64]{1,3,2,0:T(8,128)(2,1)}, bf16[8,196,12,64]{1,3,2,0:T(8,128)(2,1)S(1)}, u32[]{:S(2)}) copy-start(bf16[8,196,12,64]{1,3,2,0:T(8,128)(2,1)S(1)} %copy.300) | copy-start | bytes 7225348
  467.8 207.6 %all-gather.31.cloned.1.call-start = ((), (), s32[]{:S(2)}) async-start(), calls=%async_computation.14 | async-start | bytes 12288000 | tf_op jit(solution)/shard_map/all_gather | solution.py:195
  483.5 43.3 %copy-start.148 = (bf16[96]{0:T(256)(128)(2,1)S(1)}, bf16[96]{0:T(256)(128)(2,1)}, u32[]{:S(2)}) copy-start(bf16[96]{0:T(256)(128)(2,1)} %param.26) | copy-start | bytes 580
  483.5 233.1 %all-gather.21.cloned.1.call-start = ((), (), s32[]{:S(2)}) async-start(), calls=%async_computation.9 | async-start | bytes 12288000 | tf_op jit(solution)/shard_map/all_gather | solution.py:195
  485.8 333.8 %all-gather.25.cloned.1.call-start = ((), (), s32[]{:S(2)}) async-start(), calls=%async_computation.11 | async-start | bytes 1216512 | tf_op jit(solution)/shard_map/all_gather | solution.py:370
  486.6 412.2 %all-gather.27.cloned.1.call-start = ((), (), s32[]{:S(2)}) async-start(), calls=%async_computation.12 | async-start | bytes 4866048 | tf_op jit(solution)/shard_map/all_gather | solution.py:371
  487.3 529.4 %all-gather.29.cloned.1.call-start = ((), (), s32[]{:S(2)}) async-start(), calls=%async_computation.13 | async-start | bytes 4866048 | tf_op jit(solution)/shard_map/all_gather | solution.py:373
  487.9 1238.9 %all-reduce.16.cloned.1.call-start = ((), (), s32[]{:S(2)}) async-start(), calls=%async_computation.22 | async-start | bytes 19267584
  825.5 73.3 %copy-start.58 = (f32[1568]{0:T(1024)}, f32[1568]{0:T(1024)S(1)}, u32[]{:S(2)}) copy-start(f32[1568]{0:T(1024)S(1)} %broadcast_multiply_fusion.16) | copy-start | bytes 18820
  827.6 71.2 %copy-start.62 = (f32[1568]{0:T(1024)}, f32[1568]{0:T(1024)S(1)}, u32[]{:S(2)}) copy-start(f32[1568]{0:T(1024)S(1)} %add_rsqrt_fusion.2) | copy-start | bytes 18820
  895.9 327.0 %copy-start.69 = (f32[1568]{0:T(1024)}, f32[1568]{0:T(1024)S(1)}, u32[]{:S(2)}) copy-start(f32[1568]{0:T(1024)S(1)} %broadcast_multiply_fusion.18) | copy-start | bytes 18820
  898.7 324.2 %copy-start.87 = (f32[1568]{0:T(1024)}, f32[1568]{0:T(1024)S(1)}, u32[]{:S(2)}) copy-start(f32[1568]{0:T(1024)S(1)} %add_rsqrt_fusion.4) | copy-start | bytes 18820
  913.9 96.5 %copy-start.10 = (f32[2,196,12,4]{3,2,1,0:T(8,128)S(1)}, f32[2,196,12,4]{3,2,1,0:T(8,128)}, u32[]{:S(2)}) copy-start(f32[2,196,12,4]{3,2,1,0:T(8,128)} %copy-done.9) | copy-start | bytes 225796
  913.9 96.5 %copy-start.24 = (f32[2,196,12,4]{3,2,1,0:T(8,128)S(1)}, f32[2,196,12,4]{3,2,1,0:T(8,128)}, u32[]{:S(2)}) copy-start(f32[2,196,12,4]{3,2,1,0:T(8,128)} %copy-done.23) | copy-start | bytes 225796
  1077.4 25.9 slice-start.4
  1082.7 20.6 slice-start.5
  1082.7 20.6 copy-start.59
  1082.7 20.6 copy-start.63
  1139.4 21.2 copy-start.146
  1349.3 716.6 %all-reduce.18.cloned.1.call-start = ((), (), s32[]{:S(2)}) async-start(), calls=%async_computation.23 | async-start | bytes 57802752
  1462.8 48.0 %slice-start = ((s8[6422528]{0:T(1024)(128)(4,1)}), s8[2228224]{0:T(1024)(128)(4,1)S(1)}, s32[]{:S(2)}) async-start(s8[6422528]{0:T(1024)(128)(4,1)} %bitcast.198), calls=%async_computation.24 | async-start | bytes 4456448
  1580.3 1009.0 %reduce-scatter.17.cloned.1.call-start = ((), (), s32[]{:S(2)}) async-start(), calls=%async_computation.19 | async-start | bytes 2433024 | tf_op jit(solution)/shard_map/reduce_scatter | solution.py:401
  1592.7 996.6 %reduce-scatter.21.cloned.1.call-start = ((), (), s32[]{:S(2)}) async-start(), calls=%async_computation.21 | async-start | bytes 9732096 | tf_op jit(solution)/shard_map/reduce_scatter | solution.py:401
  1621.7 967.6 %reduce-scatter.19.cloned.1.call-start = ((), (), s32[]{:S(2)}) async-start(), calls=%async_computation.20 | async-start | bytes 9732096 | tf_op jit(solution)/shard_map/reduce_scatter | solution.py:401
  1690.2 22.0 slice-start.6
  1690.2 22.0 slice-start.10
  1726.7 862.7 %reduce-scatter.13.cloned.1.call-start = ((), (), s32[]{:S(2)}) async-start(), calls=%async_computation.17 | async-start | bytes 2433024 | tf_op jit(solution)/shard_map/reduce_scatter | solution.py:401
  2365.2 318.4 %reduce-scatter.15.cloned.1.call-start = ((), (), s32[]{:S(2)}) async-start(), calls=%async_computation.18 | async-start | bytes 7299072 | tf_op jit(solution)/shard_map/reduce_scatter | solution.py:401
  2395.8 412.3 %reduce-scatter.11.cloned.1.call-start = ((), (), s32[]{:S(2)}) async-start(), calls=%async_computation.16 | async-start | bytes 7299072 | tf_op jit(solution)/shard_map/reduce_scatter | solution.py:401
  2503.4 19.2 copy-start.104
  2503.4 19.2 copy-start.105
  2503.4 19.2 copy-start.109
  2503.4 19.2 copy-start.110
  2503.4 19.2 copy-start.117
  2503.5 19.2 copy-start.118
  2503.5 19.2 copy-start.107
  2503.5 19.2 copy-start.108
  2503.5 19.2 copy-start.114
  2503.5 19.2 copy-start.116
  2503.5 19.2 copy-start.103
  2503.5 19.2 copy-start.106
  2503.5 19.2 copy-start.113
  2503.5 19.2 copy-start.115
  2503.5 19.3 copy-start.111
  2503.6 19.3 copy-start.112
  2503.6 19.3 copy-start.73
  2503.6 19.3 copy-start.97
  (127 other events, 985.6 us)
Sparse Core Ops, SparseCore 0:
  10.9 62.8 all-gather.14
  76.8 52.8 all-gather.16
  132.6 59.1 all-gather.18
  354.4 63.9 all-gather.22
  467.9 65.6 all-gather.32
  535.6 67.1 all-gather.30
  604.4 66.4 all-gather.20
  673.8 54.0 all-gather.24
  730.8 62.5 all-gather.26
  796.1 62.3 all-gather.28
  1349.5 172.0 all-reduce.15
  1580.5 485.4 all-reduce.17
  2072.6 98.9 reduce-scatter.16
  2178.0 134.5 reduce-scatter.20
  2319.9 134.6 reduce-scatter.18
  2460.3 98.1 reduce-scatter.12
  2565.5 118.0 reduce-scatter.14
  2689.7 118.3 reduce-scatter.10
where the time goes:
time: 2840 us; the launch traced here: 2820 us
  local copies, waits for them, and re-layouts  917 us (32%)
  matrix products  830 us (29%)
  waiting for transfers between devices  545 us (19%)
  blocking collectives  277 us (10%)
  other arithmetic  226 us (8%)
    unnamed x20, waiting for transfers between devices  326 us
    reduce_scatter x6, waiting for transfers between devices, shards(): lax.psum_scatter(local_sum, ('clip', 'frame'), scatter_dimension=0, tiled...  219 us
    dot_general x12, matrix products, matmul(): return jnp.dot(left, right, preferred_element_type=jnp.float32)  197 us
    dot_general x12, matrix products, matmul_nt(): lax.dot_general(left, right, (((1,), (1,)), ((), ())), preferred_element_...  158 us
    dot_general x12, matrix products, matmul_tn(): lax.dot_general(left, right, (((0,), (0,)), ((), ())), preferred_element_...  138 us
    convert_element_type x4, local copies, waits for them, and re-layouts, backward(): grad_k_full.astype(jnp.bfloat16)  114 us
    convert_element_type x4, local copies, waits for them, and re-layouts, backward(): grad_v_full.astype(jnp.bfloat16)  114 us
    reshape x4, local copies, waits for them, and re-layouts, split_heads(): return block.reshape(block.shape[:3] + (HEADS, HEAD))  106 us
  transfers between devices with their start and end apart: 18, of which 3 were waited for; matrix products, arithmetic and copies ran while one was open for 56% of the time, Pallas kernels for 0%

commit v1 on v0

v1 whole, which is shorter than its diff:
```python
import functools

import jax
import jax.numpy as jnp
from jax import lax
from jax.experimental import pallas as pl
from jax.experimental.pallas import tpu as pltpu
from jax.sharding import PartitionSpec as P

D = 768
HEADS = 12
HEAD = 64
FF = 3072
EPS = 1e-06
F32 = jnp.float32
BF16 = jnp.bfloat16
PARAMS = pltpu.CompilerParams(vmem_limit_bytes=60 << 20)

GAIN, SHIFT, QV, MIX, UP = 0, 3, 6, 10, 13


def dot(left, right):
    return jnp.dot(left, right, preferred_element_type=F32)


def dot_nt(left, right):
    return lax.dot_general(left, right, (((1,), (1,)), ((), ())), preferred_element_type=F32)


def dot_tn(left, right):
    return lax.dot_general(left, right, (((0,), (0,)), ((), ())), preferred_element_type=F32)


def normalize(rows):
    center = rows - jnp.mean(rows, -1, keepdims=True)
    inverse = lax.rsqrt(jnp.mean(center * center, -1, keepdims=True) + EPS)
    return center * inverse, inverse


def normalize_back(grad_out, hat, inverse, gain):
    grad_hat = grad_out * gain
    return inverse * (
        grad_hat
        - jnp.mean(grad_hat, -1, keepdims=True)
        - hat * jnp.mean(grad_hat * hat, -1, keepdims=True)
    )


def column_sum(rows):
    return jnp.sum(rows, 0, keepdims=True)


def first_lanes(shape):
    return lax.broadcasted_iota(jnp.int32, shape, 1) < HEAD


def halves(block):
    low = first_lanes(block.shape)
    zero = jnp.zeros_like(block)
    return jnp.where(low, block, zero), jnp.where(low, zero, block)


def pair(index):
    return slice(2 * HEAD * index, 2 * HEAD * (index + 1))


def attention(query, key, value, keep_probs, mask=None):
    outs = []
    for p in range(HEADS // 2):
        key_pair, value_pair = key[:, pair(p)], value[:, pair(p)]
        mixed = []
        for side, one in enumerate(halves(query[:, pair(p)])):
            scores = dot_nt(one, key_pair)
            if mask is not None:
                scores = jnp.where(mask, scores, -1e30)
            expo = jnp.exp(scores - jnp.max(scores, -1, keepdims=True))
            probs = (expo * (1.0 / jnp.sum(expo, -1, keepdims=True))).astype(BF16)
            keep_probs(2 * p + side, probs)
            mixed.append(dot(probs, value_pair))
        outs.append(jnp.where(first_lanes(mixed[0].shape), mixed[0], mixed[1]).astype(BF16))
    return jnp.concatenate(outs, 1)


def attention_back(query, key, value, grad_mix, probs_of):
    grad_q, grad_k, grad_v = [], [], []
    for p in range(HEADS // 2):
        query_pair, key_pair = query[:, pair(p)], key[:, pair(p)]
        value_pair, grad_pair = value[:, pair(p)], grad_mix[:, pair(p)]
        parts = []
        for side, one in enumerate(halves(grad_pair)):
            probs = probs_of(2 * p + side)
            wide = probs.astype(F32)
            grad_p = dot_nt(one, value_pair)
            term = wide * grad_p
            grad_s = (term - wide * jnp.sum(term, -1, keepdims=True)).astype(BF16)
            parts.append((dot(grad_s, key_pair), dot_tn(grad_s, query_pair), dot_tn(probs, grad_pair)))
        low = first_lanes(parts[0][0].shape)
        grad_q.append((jnp.where(low, parts[0][0], parts[1][0]) * HEAD ** (-0.5)).astype(BF16))
        grad_k.append(jnp.where(low, parts[0][1], parts[1][1]).astype(BF16))
        grad_v.append(jnp.where(low, parts[0][2], parts[1][2]).astype(BF16))
    return jnp.concatenate(grad_q + grad_k + grad_v, 1)


def project(rows, weights, table, query_row):
    proj = dot(rows, weights)
    query = (proj[:, :D] + table[query_row : query_row + 1, :]).astype(BF16)
    key = proj[:, D : 2 * D].astype(BF16)
    value = (proj[:, 2 * D :] + table[query_row + 1 : query_row + 2, :]).astype(BF16)
    return (query.astype(F32) * HEAD ** (-0.5)).astype(BF16), key, value


def fixed(shape):
    return pl.BlockSpec(shape, lambda *_: (0,) * len(shape), pipeline_mode=pl.Buffered(1))


def accumulate(ref, value, first):
    @pl.when(first)
    def _():
        ref[...] = value

    @pl.when(jnp.logical_not(first))
    def _():
        ref[...] += value


def space_kernel(clip, x_ref, table, w_ref, in_ref, q_ref, k_ref, v_ref, mix_ref, p_ref, out_ref):
    rows = x_ref[0, 0].astype(F32)
    hat, _ = normalize(rows)
    normed = (hat * table[GAIN : GAIN + 1, :] + table[SHIFT : SHIFT + 1, :]).astype(BF16)
    in_ref[0] = normed
    query, key, value = project(normed, w_ref[:, : 3 * D], table, QV)
    q_ref[0], k_ref[0], v_ref[0] = query, key, value

    def keep(head, probs):
        p_ref[0, head] = probs

    mixed = attention(query, key, value, keep)
    mix_ref[0] = mixed
    after = rows + dot(mixed, w_ref[:, 3 * D : 4 * D]) + table[MIX : MIX + 1, :]
    out_ref[0] = after.astype(BF16)


def space_forward(clip, inputs, table, weights):
    _, frames, places, _ = inputs.shape

    def frame(*tail):
        return pl.BlockSpec((1,) + tail, lambda i, c: (i,) + (0,) * len(tail))

    def shape(*tail):
        return jax.ShapeDtypeStruct((frames,) + tail, BF16)

    return pl.pallas_call(
        space_kernel,
        grid_spec=pltpu.PrefetchScalarGridSpec(
            num_scalar_prefetch=1,
            grid=(frames,),
            in_specs=[
                pl.BlockSpec((1, 1, places, D), lambda i, c: (c[0], i, 0, 0)),
                fixed(table.shape),
                fixed((D, 4 * D)),
            ],
            out_specs=[frame(places, D)] * 5 + [frame(HEADS, places, places), frame(places, D)],
        ),
        out_shape=[shape(places, D)] * 5 + [shape(HEADS, places, places), shape(places, D)],
        compiler_params=PARAMS,
        name="space_forward",
    )(clip, inputs, table, weights)


def largest_divisor(number, limit):
    return max(n for n in range(1, limit + 1) if number % n == 0)


def time_kernel(frames, group, a_ref, table, w_ref, in_ref, q_ref, k_ref, v_ref, mix_ref, p_ref, out_ref):
    rows = a_ref[...].astype(F32)
    hat, _ = normalize(rows)
    normed = (hat * table[GAIN + 1 : GAIN + 2, :] + table[SHIFT + 1 : SHIFT + 2, :]).astype(BF16)
    in_ref[...] = normed
    query, key, value = project(normed, w_ref[:, : 3 * D], table, QV + 2)
    q_ref[...], k_ref[...], v_ref[...] = query, key, value
    place = lax.broadcasted_iota(jnp.int32, (group, group), 0) // frames
    mask = place == lax.broadcasted_iota(jnp.int32, (group, group), 1) // frames

    def one_group(g, carry):
        span = pl.ds(pl.multiple_of(g * group, group), group)

        def keep(head, probs):
            p_ref[g, head] = probs

        mix_ref[span, :] = attention(q_ref[span, :], k_ref[span, :], v_ref[span, :], keep, mask)
        return carry

    lax.fori_loop(0, rows.shape[0] // group, one_group, 0)
    out_ref[...] = rows + dot(mix_ref[...], w_ref[:, 3 * D :]) + table[MIX + 1 : MIX + 2, :]


def time_tiles(places, frames):
    per_group = largest_divisor(places, 128 // frames)
    per_tile = per_group * largest_divisor(places // per_group, 4)
    return per_tile * frames, per_group * frames


def time_forward(after_a, table, weights, frames):
    tokens = after_a.shape[0]
    tile, group = time_tiles(tokens // frames, frames)
    rows = pl.BlockSpec((tile, D), lambda i: (i, 0))
    return pl.pallas_call(
        functools.partial(time_kernel, frames, group),
        grid=(tokens // tile,),
        in_specs=[rows, fixed(table.shape), fixed((D, 4 * D))],
        out_specs=[rows] * 5
        + [pl.BlockSpec((tile // group, HEADS, group, group), lambda i: (i, 0, 0, 0)), rows],
        out_shape=[jax.ShapeDtypeStruct((tokens, D), BF16)] * 5
        + [
            jax.ShapeDtypeStruct((tokens // group, HEADS, group, group), BF16),
            jax.ShapeDtypeStruct((tokens, D), F32),
        ],
        compiler_params=PARAMS,
        name="time_forward",
    )(after_a, table, weights)


def gelu_parts(u):
    bell = jnp.exp(-0.5 * u * u)
    base = 1.0 + 0.2316418886 * jnp.abs(u)
    t = 1.0 / base
    poly = t * (
        0.127414796 + t * (-0.142248368 + t * (0.7107068705 + t * (-0.7265760135 + t * 0.5307027145)))
    )
    tail = poly * bell
    area = jnp.where(u >= 0, 1.0 - tail, tail)
    return u * area, area + 0.3989422804014327 * (u * bell)


FF_CHUNK = 768


def feed_kernel(
    a_ref, t_ref, valid_ref, scale_ref, table, up_bias, up_ref, down_ref,
    out_ref, g_ref, d_up_ref, d_down_ref, rows_ref, bias_ref, square_ref,
    hidden, slope, d_up, d_down, stage, sems,
):
    step, last = pl.program_id(0), pl.num_programs(0) - 1
    first = step == 0
    after = a_ref[...]
    hat, inverse = normalize(after)
    normed = (hat * table[GAIN + 2 : GAIN + 3, :] + table[SHIFT + 2 : SHIFT + 3, :]).astype(BF16)
    total = after + table[MIX + 2 : MIX + 3, :]
    chunks = [slice(c, c + FF_CHUNK) for c in range(0, FF, FF_CHUNK)]
    for c in chunks:
        act, rise = gelu_parts(dot(normed, up_ref[:, c]) + up_bias[:, c])
        act = act.astype(BF16)
        hidden[:, c] = act
        slope[:, c] = rise.astype(BF16)
        total = total + dot(act, down_ref[c, :])
    out_ref[...] = total.astype(BF16)
    diff = (total - t_ref[...].astype(F32)) * valid_ref[...]
    accumulate(square_ref, column_sum(diff * diff), first)
    grad = diff * scale_ref[0, 0]
    grad_low = grad.astype(BF16)
    bias_c = column_sum(grad_low.astype(F32))
    back = jnp.zeros_like(grad)
    for c in chunks:
        grad_pre = dot_nt(grad_low, down_ref[c, :]) * slope[:, c].astype(F32)
        grad_pre = grad_pre.astype(BF16)
        accumulate(bias_ref.at[:, c], column_sum(grad_pre.astype(F32)), first)
        accumulate(d_down.at[c, :], dot_tn(hidden[:, c], grad_low), first)
        accumulate(d_up.at[:, c], dot_tn(normed, grad_pre), first)
        back = back + dot_nt(grad_pre, up_ref[:, c])
    accumulate(
        rows_ref, jnp.concatenate([column_sum(back * hat), column_sum(back), bias_c], 0), first
    )
    g_ref[...] = grad + normalize_back(back, hat, inverse, table[GAIN + 2 : GAIN + 3, :])

    @pl.when(step == last)
    def _():
        flush([(d_up.at[:, c], d_up_ref.at[:, c]) for c in chunks], stage, sems)
        flush([(d_down.at[c, :], d_down_ref.at[c, :]) for c in chunks], stage, sems)


def flush(moves, stage, sems):
    copies = []
    for i, (source, target) in enumerate(moves):
        if i >= 2:
            copies[i - 2].wait()
        stage[i % 2] = source[...].astype(BF16)
        copies.append(pltpu.make_async_copy(stage.at[i % 2], target, sems.at[i % 2]))
        copies[i].start()
    for copy in copies[-2:]:
        copy.wait()


def feed_forward(after_b, teacher, valid, scale, table, up_bias, w_up, w_down, tile):
    tokens = after_b.shape[0]
    rows = pl.BlockSpec((tile, D), lambda i: (i, 0))
    hbm = pl.BlockSpec(memory_space=pl.ANY)
    return pl.pallas_call(
        feed_kernel,
        grid=(tokens // tile,),
        in_specs=[
            rows,
            rows,
            pl.BlockSpec((tile, 1), lambda i: (i, 0)),
            pl.BlockSpec(memory_space=pltpu.SMEM),
            fixed(table.shape),
            fixed((1, FF)),
            fixed((D, FF)),
            fixed((FF, D)),
        ],
        out_specs=[rows, rows, hbm, hbm, fixed((3, D)), fixed((1, FF)), fixed((1, D))],
        out_shape=[
            jax.ShapeDtypeStruct((tokens, D), BF16),
            jax.ShapeDtypeStruct((tokens, D), F32),
            jax.ShapeDtypeStruct((D, FF), BF16),
            jax.ShapeDtypeStruct((FF, D), BF16),
            jax.ShapeDtypeStruct((3, D), F32),
            jax.ShapeDtypeStruct((1, FF), F32),
            jax.ShapeDtypeStruct((1, D), F32),
        ],
        scratch_shapes=[
            pltpu.VMEM((tile, FF), BF16),
            pltpu.VMEM((tile, FF), BF16),
            pltpu.VMEM((D, FF), F32),
            pltpu.VMEM((FF, D), F32),
            pltpu.VMEM((2, D, FF_CHUNK), BF16),
            pltpu.SemaphoreType.DMA((2,)),
        ],
        compiler_params=PARAMS,
        name="feed_forward",
    )(after_b, teacher, valid, scale, table, up_bias, w_up, w_down)


def time_back_kernel(
    group, g_ref, a_ref, in_ref, q_ref, k_ref, v_ref, mix_ref, p_ref, table, w_ref,
    out_ref, d_ref, rows_ref, grad_mix, grad_proj, d_proj, d_out, stage, sems,
):
    step, last = pl.program_id(0), pl.num_programs(0) - 1
    first = step == 0
    grad = g_ref[...]
    grad_low = grad.astype(BF16)
    accumulate(d_out, dot_tn(mix_ref[...], grad_low), first)
    grad_mix[...] = dot_nt(grad_low, w_ref[:, 3 * D :]).astype(BF16)

    def one_group(g, carry):
        span = pl.ds(pl.multiple_of(g * group, group), group)
        grad_proj[span, :] = attention_back(
            q_ref[span, :], k_ref[span, :], v_ref[span, :], grad_mix[span, :], lambda h: p_ref[g, h]
        )
        return carry

    lax.fori_loop(0, grad.shape[0] // group, one_group, 0)
    proj = grad_proj[...]
    accumulate(d_proj, dot_tn(in_ref[...], proj), first)
    sums = column_sum(proj.astype(F32))
    back = dot_nt(proj, w_ref[:, : 3 * D])
    hat, inverse = normalize(a_ref[...].astype(F32))
    accumulate(
        rows_ref,
        jnp.concatenate(
            [
                column_sum(back * hat),
                column_sum(back),
                sums[:, :D],
                sums[:, 2 * D :],
                column_sum(grad_low.astype(F32)),
            ],
            0,
        ),
        first,
    )
    out_ref[...] = (grad + normalize_back(back, hat, inverse, table[GAIN + 1 : GAIN + 2, :])).astype(BF16)

    @pl.when(step == last)
    def _():
        moves = [(d_proj.at[:, pl.ds(c * D, D)], d_ref.at[:, pl.ds(c * D, D)]) for c in range(3)]
        flush(moves + [(d_out, d_ref.at[:, pl.ds(3 * D, D)])], stage, sems)


def time_back(grad, after_a, saved, table, weights, frames):
    tokens = grad.shape[0]
    tile, group = time_tiles(tokens // frames, frames)
    rows = pl.BlockSpec((tile, D), lambda i: (i, 0))
    return pl.pallas_call(
        functools.partial(time_back_kernel, group),
        grid=(tokens // tile,),
        in_specs=[rows] * 7
        + [
            pl.BlockSpec((tile // group, HEADS, group, group), lambda i: (i, 0, 0, 0)),
            fixed(table.shape),
            fixed((D, 4 * D)),
        ],
        out_specs=[rows, pl.BlockSpec(memory_space=pl.ANY), fixed((5, D))],
        out_shape=[
            jax.ShapeDtypeStruct((tokens, D), BF16),
            jax.ShapeDtypeStruct((D, 4 * D), BF16),
            jax.ShapeDtypeStruct((5, D), F32),
        ],
        scratch_shapes=[
            pltpu.VMEM((tile, D), BF16),
            pltpu.VMEM((tile, 3 * D), BF16),
            pltpu.VMEM((D, 3 * D), F32),
            pltpu.VMEM((D, D), F32),
            pltpu.VMEM((2, D, D), BF16),
            pltpu.SemaphoreType.DMA((2,)),
        ],
        compiler_params=PARAMS,
        name="time_back",
    )(grad, after_a, *saved, table, weights)


def space_back_kernel(g_ref, q_ref, k_ref, v_ref, mix_ref, p_ref, w_ref, out_ref, d_ref, bias_ref):
    first = pl.program_id(0) == 0
    grad = g_ref[0]
    accumulate(d_ref, dot_tn(mix_ref[0], grad), first)
    accumulate(bias_ref, column_sum(grad.astype(F32)), first)
    grad_mix = dot_nt(grad, w_ref[...]).astype(BF16)
    out_ref[0] = attention_back(q_ref[0], k_ref[0], v_ref[0], grad_mix, lambda h: p_ref[0, h])


def space_back(grad, saved, weights):
    frames, places, _ = grad.shape

    def frame(*tail):
        return pl.BlockSpec((1,) + tail, lambda i: (i,) + (0,) * len(tail))

    return pl.pallas_call(
        space_back_kernel,
        grid=(frames,),
        in_specs=[frame(places, D)] * 5
        + [
            frame(HEADS, places, places),
            pl.BlockSpec((D, D), lambda i: (0, 3), pipeline_mode=pl.Buffered(1)),
        ],
        out_specs=[frame(places, 3 * D), fixed((D, D)), fixed((1, D))],
        out_shape=[
            jax.ShapeDtypeStruct((frames, places, 3 * D), BF16),
            jax.ShapeDtypeStruct((D, D), F32),
            jax.ShapeDtypeStruct((1, D), F32),
        ],
        compiler_params=PARAMS,
        name="space_back",
    )(grad, *saved, weights)


def space_weight_kernel(parts, frames, *refs):
    ins, projs, outs = refs[:parts], refs[parts : 2 * parts], refs[2 * parts : 3 * parts]
    d_ref, rows_ref, d_proj, stage, sems = refs[3 * parts :]
    step, last = pl.program_id(0), pl.num_programs(0) - 1

    @pl.when(step == 0)
    def _():
        d_proj[...] = jnp.zeros_like(d_proj)
        rows_ref[...] = jnp.zeros_like(rows_ref)

    for part in range(parts):

        @pl.when(step // frames == part)
        def _():
            proj = projs[part][0]
            d_proj[...] += dot_tn(ins[part][0], proj)
            rows_ref[...] += column_sum(proj.astype(F32))

    @pl.when(step == last)
    def _():
        total = outs[0][...]
        for ref in outs[1:]:
            total = total + ref[...]
        outs_sum = total
        stage[0] = outs_sum.astype(BF16)
        copy = pltpu.make_async_copy(stage.at[0], d_ref.at[:, pl.ds(3 * D, D)], sems.at[0])
        copy.start()
        copy.wait()
        flush(
            [(d_proj.at[:, pl.ds(c * D, D)], d_ref.at[:, pl.ds(c * D, D)]) for c in range(3)], stage, sems
        )


def space_weights(ins, projs, outs):
    parts = len(ins)
    frames, places, _ = ins[0].shape

    def frame(part, width):
        return pl.BlockSpec(
            (1, places, width), lambda i: (jnp.clip(i - part * frames, 0, frames - 1), 0, 0)
        )

    return pl.pallas_call(
        functools.partial(space_weight_kernel, parts, frames),
        grid=(parts * frames,),
        in_specs=[frame(p, D) for p in range(parts)]
        + [frame(p, 3 * D) for p in range(parts)]
        + [fixed((D, D))] * parts,
        out_specs=[pl.BlockSpec(memory_space=pl.ANY), fixed((1, 3 * D))],
        out_shape=[jax.ShapeDtypeStruct((D, 4 * D), BF16), jax.ShapeDtypeStruct((1, 3 * D), F32)],
        scratch_shapes=[
            pltpu.VMEM((D, 3 * D), F32),
            pltpu.VMEM((2, D, D), BF16),
            pltpu.SemaphoreType.DMA((2,)),
        ],
        compiler_params=PARAMS,
        name="space_weights",
    )(*ins, *projs, *outs)


def input_kernel(parts, frames, clips, *refs):
    grads, projs = refs[:parts], refs[parts : 2 * parts]
    x_ref, table, w_ref, out_ref, rows_ref = refs[2 * parts :]
    step = pl.program_id(0)

    @pl.when(step == 0)
    def _():
        rows_ref[...] = jnp.zeros_like(rows_ref)

    for part in range(parts):

        @pl.when(step // frames == part)
        def _():
            back = dot_nt(projs[part][0], w_ref[...])
            hat, inverse = normalize(x_ref[0, 0].astype(F32))
            rows_ref[...] += jnp.concatenate([column_sum(back * hat), column_sum(back)], 0)
            grad = grads[part][0].astype(F32) + normalize_back(
                back, hat, inverse, table[GAIN : GAIN + 1, :]
            )
            out_ref[0, 0] = grad.astype(BF16)


def input_grads(clips, grads, projs, inputs, table, weights):
    parts = len(grads)
    frames, places, _ = grads[0].shape

    def frame(part, width):
        return pl.BlockSpec(
            (1, places, width), lambda i, c: (jnp.clip(i - part * frames, 0, frames - 1), 0, 0)
        )

    clip = pl.BlockSpec((1, 1, places, D), lambda i, c: (c[i // frames], i % frames, 0, 0))
    return pl.pallas_call(
        functools.partial(input_kernel, parts, frames),
        grid_spec=pltpu.PrefetchScalarGridSpec(
            num_scalar_prefetch=1,
            grid=(parts * frames,),
            in_specs=[frame(p, D) for p in range(parts)]
            + [frame(p, 3 * D) for p in range(parts)]
            + [
                clip,
                fixed(table.shape),
                pl.BlockSpec((D, 3 * D), lambda *_: (0, 0), pipeline_mode=pl.Buffered(1)),
            ],
            out_specs=[clip, fixed((2, D))],
        ),
        out_shape=[jax.ShapeDtypeStruct(inputs.shape, BF16), jax.ShapeDtypeStruct((2, D), F32)],
        compiler_params=PARAMS,
        name="input_grads",
    )(clips, *grads, *projs, inputs, table, weights)


AXES = ("clip", "frame")


def gather(block):
    return lax.all_gather(block, AXES, axis=0, tiled=True)


def scatter(block):
    return lax.psum_scatter(block, AXES, scatter_dimension=0, tiled=True)


def shards(
    clips_in, teacher, valid, norm_gain, norm_shift, w_space, qv_bias, w_space_out, mix_bias,
    w_time, w_time_out, w_up, up_bias, w_down,
):
    batch, frames, places, _ = clips_in.shape
    ring = lax.axis_size("frame")
    pieces = ring // batch
    chunk = places // pieces
    all_frames = ring * frames
    me = lax.axis_index("frame")
    depth = w_up.shape[0]

    def swap(block, step):
        if step == 0:
            return block
        return lax.ppermute(block, "frame", [(i, i ^ step) for i in range(ring)])

    def clip_of(step):
        return (me // pieces) ^ (step // pieces)

    def place_of(step):
        return ((me % pieces) ^ (step % pieces)) * chunk

    def cut(block, step):
        if pieces == 1:
            return block
        return lax.dynamic_slice_in_dim(block, place_of(step), chunk, 0)

    def spread(block):
        got = []
        for step in range(ring):
            mine = lax.dynamic_index_in_dim(block, clip_of(step), 0, keepdims=False)
            got.append(swap(cut(jnp.swapaxes(mine, 0, 1), step), step))
        return jnp.concatenate(got, 1)

    count = jnp.sum(valid)
    counts = jnp.stack([count // 256, count % 256]).astype(BF16)
    smalls = jnp.concatenate(
        [
            norm_gain, norm_shift, qv_bias, mix_bias, up_bias.reshape(depth, -1),
            jnp.broadcast_to(counts[None], (depth, 2)),
        ],
        1,
    )
    smalls = jnp.pad(smalls, ((0, 0), (0, 128 - smalls.shape[1])))
    first = gather(jnp.concatenate([w_space, w_space_out, smalls], 1))
    second = gather(jnp.concatenate([w_time, w_time_out, w_up], 1))
    third = gather(w_down)
    columns = first[:, 4 * D : 4 * D + 24].astype(F32)
    table = jnp.swapaxes(columns, 0, 1)[:16]
    up_row = columns[:, UP : UP + 4].reshape(1, FF)
    counted = columns[::depth, UP + 4 : UP + 6]
    total_count = jnp.sum(counted[:, 0]) * 256.0 + jnp.sum(counted[:, 1])
    scale = (2.0 / (total_count * D)).reshape(1, 1)

    order = [(me // pieces) ^ j for j in range(batch)]
    clip_ids = [jnp.reshape(c, (1,)).astype(jnp.int32) for c in order]
    saved, sent = [None] * batch, [None] * ring
    for j in list(range(batch))[::-1]:
        *kept, after = space_forward(clip_ids[j], clips_in, table, first)
        saved[j] = kept
        after = jnp.swapaxes(after, 0, 1)
        for r in range(pieces):
            step = j * pieces + r
            sent[step] = swap(cut(after, step), step)
    after_a = jnp.concatenate(sent, 1).reshape(-1, D)
    teach = spread(teacher).reshape(-1, D)
    valid_column = spread(valid).reshape(-1, 1).astype(F32)

    in_b, q_b, k_b, v_b, mix_b, p_b, after_b = time_forward(after_a, table, second, all_frames)
    tile, _ = time_tiles(chunk, all_frames)
    layer_rows, grad_b, d_up, d_down, rows_c, bias_up, squares = feed_forward(
        after_b, teach, valid_column, scale, table, up_row, second[:, 4 * D :], third, tile
    )
    d_up, d_down = scatter(d_up), scatter(d_down)
    grad_a, d_time, rows_b = time_back(
        grad_b, after_a, (in_b, q_b, k_b, v_b, mix_b, p_b), table, second, all_frames
    )
    d_time = scatter(d_time)

    def give_back(rows):
        split = rows.reshape(chunk, ring, frames, D)
        return [swap(split[:, step], step) for step in range(ring)]

    def join(parts, j):
        if pieces == 1:
            return jnp.swapaxes(parts[j], 0, 1)
        whole = jnp.zeros((places, frames, D), BF16)
        for r in range(pieces):
            step = j * pieces + r
            whole = lax.dynamic_update_slice_in_dim(whole, parts[step], place_of(step), 0)
        return jnp.swapaxes(whole, 0, 1)

    layer_parts, grad_parts = give_back(layer_rows), give_back(grad_a)
    grads = [join(grad_parts, j) for j in range(batch)]
    projs, outs, biases = [], [], []
    for j in range(batch):
        proj, d_out, bias = space_back(grads[j], saved[j][1:], first)
        projs.append(proj)
        outs.append(d_out)
        biases.append(bias)
    d_space, sums_a = space_weights([s[0] for s in saved], projs, outs)
    d_space = scatter(d_space)
    input_grad, rows_a = input_grads(
        jnp.stack(order).astype(jnp.int32), grads, projs, clips_in, table, first
    )
    layer_out = jnp.zeros(clips_in.shape, BF16)
    for j in range(batch):
        layer_out = lax.dynamic_update_index_in_dim(layer_out, join(layer_parts, j), order[j], 0)

    small = jnp.concatenate(
        [
            rows_a[0:1], rows_b[0:1], rows_c[0:1],
            rows_a[1:2], rows_b[1:2], rows_c[1:2],
            sums_a[:, :D], sums_a[:, 2 * D :], rows_b[3:4], rows_b[2:3],
            sum(biases), rows_b[4:5], rows_c[2:3],
            jnp.swapaxes(bias_up.reshape(D, 4), 0, 1),
            squares,
        ],
        0,
    )
    small = lax.psum(small, AXES)
    loss_value = jnp.sum(small[17]) / (total_count * D)
    here = lax.dynamic_slice_in_dim(
        jnp.swapaxes(small, 0, 1), (lax.axis_index("clip") * ring + me) * depth, depth, 0
    )
    return (
        layer_out,
        loss_value,
        input_grad,
        here[:, 0:3],
        here[:, 3:6],
        d_space[:, : 3 * D].astype(F32),
        here[:, 6:9],
        here[:, 9],
        d_space[:, 3 * D :].astype(F32),
        here[:, 10:13],
        d_time[:, : 3 * D].astype(F32),
        d_time[:, 3 * D :].astype(F32),
        d_up.astype(F32),
        here[:, 13:17].reshape(-1),
        d_down.astype(F32),
    )


def solution(mesh):
    tokens, rows = P("clip", "frame", None, None), P(AXES, None)
    in_specs = (tokens, tokens, P("clip", "frame", None)) + (rows,) * 9 + (P(AXES), rows)
    out_specs = (
        (tokens, P(), tokens, rows, rows, rows, rows, P(AXES)) + (rows,) * 5 + (P(AXES), rows)
    )
    return jax.shard_map(shards, mesh=mesh, in_specs=in_specs, out_specs=out_specs, check_vma=False)
```

time: 2840 us -> 989 us (0.35)
  matrix products: 830 us -> 0 us
  local copies, waits for them, and re-layouts: 917 us -> 92.5 us
  Pallas kernels: 0 us -> 645 us
  waiting for transfers between devices: 545 us -> 126 us
  blocking collectives: 277 us -> 62.8 us
  other arithmetic: 226 us -> 26.1 us
    dot_general x60 -> x0, matrix products: 830 us -> none  [the longest x12 197 us: matmul(): return jnp.dot(left, right, preferred_element_type=jnp.float32)]
    pallas_call x0 -> x13, Pallas kernels: none -> 645 us  [the longest x1 184 us: feed_forward(): pl.pallas_call(feed_kernel, grid=(tokens // tile,), in_specs=[rows, rows,...]
    convert_element_type x40 -> x2, local copies, waits for them, and re-layouts: 362 us -> 2.12 us  [shards(): valid_column = spread(valid).reshape(-1, 1).astype(F32)]
    unnamed x20 -> x7, waiting for transfers between devices: 326 us -> 1.3 us
    reshape x32 -> x6, local copies, waits for them, and re-layouts: 287 us -> 20.8 us  [the longest x2 18.2 us: give_back(): split = rows.reshape(chunk, ring, frames, D)]
    reduce_scatter x6 -> x4, waiting for transfers between devices: 219 us -> 0.01 us  [scatter(): return lax.psum_scatter(block, AXES, scatter_dimension=0, tiled=True)]
    all_gather x4 -> x0, blocking collectives: 155 us -> none  [the longest x1 43.3 us: shards(): lax.all_gather(norm_gain, ('clip', 'frame'), axis=0, tiled=True)]
    reduce_sum x19 -> x3, other arithmetic: 122 us -> 2.65 us  [the longest x1 1.36 us: shards(): count = jnp.sum(valid)]
  transfers between devices with their start and end apart: 18 -> 22, of which waited for: 3 -> 5; matrix products, arithmetic and copies ran while one was open for 56% -> 11% of each run, Pallas kernels for 0% -> 47%
where the time goes in v1:
time: 989 us; the launch traced here: 984 us
  Pallas kernels  645 us (65%)
  waiting for transfers between devices  126 us (13%)
  local copies, waits for them, and re-layouts  92.5 us (9%)
  blocking collectives  62.8 us (6%)
  other arithmetic  26.1 us (3%)
  between operations  20.4 us (2%)
  starting transfers between devices  11.1 us (1%)
    pallas_call x1, Pallas kernels, feed_forward(): pl.pallas_call(feed_kernel, grid=(tokens // tile,), in_specs=[rows, rows,...  184 us
    pallas_call x1, Pallas kernels, time_back(): pl.pallas_call(functools.partial(time_back_kernel, group), grid=(tokens /...  172 us
    pallas_call x4, Pallas kernels, space_back(): pl.pallas_call(space_back_kernel, grid=(frames,), in_specs=[frame(places,...  104 us
    ppermute x15, waiting for transfers between devices, swap(): return lax.ppermute(block, 'frame', [(i, i ^ step) for i in range(ring)])  63.5 us
    psum x1, blocking collectives, shards(): small = lax.psum(small, AXES)  62.8 us
    pallas_call x4, Pallas kernels, space_forward(): pl.pallas_call(space_kernel, grid_spec=pltpu.PrefetchScalarGridSpec(num_s...  62.4 us
    all_gather x3, waiting for transfers between devices, gather(): return lax.all_gather(block, AXES, axis=0, tiled=True)  61.4 us
    pallas_call x1, Pallas kernels, time_forward(): pl.pallas_call(functools.partial(time_kernel, frames, group), grid=(token...  59.4 us
  transfers between devices with their start and end apart: 22, of which 5 were waited for; matrix products, arithmetic and copies ran while one was open for 11% of the time, Pallas kernels for 47%

profile of v1, /device:TPU:0, one launch (start us, length us, event | category | flops | bytes accessed | tf_op | source)
XLA Modules:
  0.0 983.6 jit_solution(11278435573381112311)
XLA Ops:
  7.2 1.4 reduce_sum.36
  11.2 0.8 copy.148
  12.0 0.8 copy.149
  15.2 1.6 fusion.2
  16.9 1.7 pad_maximum_fusion.2
  19.5 5.6 dynamic-slice_bitcast_fusion.3
  25.6 2.5 collective-permute-start.4
  28.4 1.8 collective-permute-start.7
  30.2 2.9 copy.152.x_ref.refs_8_
  33.2 61.4 %all-gather.4.cloned.1.call-done.w_ref.refs_10_ = bf16[768,3200]{1,0:T(8,128)(2,1)} async-done(((bf16[24,3200]{1,0:T(8,128)(2,1)}), bf16[768,3200]{1,0:T(8,128)(2,1)}) %all-gather.4.cloned.1.call-update) | async-done | bytes 4915216 | tf_op jit(solution)/shard_map/all_gather | solution.py:561
  94.6 1.0 slice_convert_fusion
  96.3 15.8 %space_forward.5 = (bf16[4,196,768]{2,1,0:T(8,128)(2,1)}, bf16[4,196,768]{2,1,0:T(8,128)(2,1)}, bf16[4,196,768]{2,1,0:T(8,128)(2,1)}, bf16[4,196,768]{2,1,0:T(8,...) custom-call(s32[1]{0:T(128)} %bitcast.5.clip, ...), custom_call_target="tpu_custom_call" | custom-call | tf_op jit(solution)/shard_map/space_forward/pallas_call | solution.py:152
  112.1 1.8 copy.156
  113.8 15.6 %space_forward.6 = (bf16[4,196,768]{2,1,0:T(8,128)(2,1)}, bf16[4,196,768]{2,1,0:T(8,128)(2,1)}, bf16[4,196,768]{2,1,0:T(8,128)(2,1)}, bf16[4,196,768]{2,1,0:T(8,...) custom-call(s32[1]{0:T(128)} %bitcast.7.clip, ...), custom_call_target="tpu_custom_call" | custom-call | tf_op jit(solution)/shard_map/space_forward/pallas_call | solution.py:152
  129.4 2.8 copy.159
  132.2 15.5 %space_forward.7 = (bf16[4,196,768]{2,1,0:T(8,128)(2,1)}, bf16[4,196,768]{2,1,0:T(8,128)(2,1)}, bf16[4,196,768]{2,1,0:T(8,128)(2,1)}, bf16[4,196,768]{2,1,0:T(8,...) custom-call(s32[1]{0:T(128)} %bitcast.9.clip, ...), custom_call_target="tpu_custom_call" | custom-call | tf_op jit(solution)/shard_map/space_forward/pallas_call | solution.py:152
  147.7 2.8 copy.162
  150.7 0.9 collective-permute-start.1
  152.5 2.0 convert_element_type.42.valid_ref
  154.5 7.8 pad_maximum_fusion.1
  162.5 0.9 reshape.110.up_bias
  165.4 15.5 %space_forward.4 = (bf16[4,196,768]{2,1,0:T(8,128)(2,1)}, bf16[4,196,768]{2,1,0:T(8,128)(2,1)}, bf16[4,196,768]{2,1,0:T(8,128)(2,1)}, bf16[4,196,768]{2,1,0:T(8,...) custom-call(s32[1]{0:T(128)} %bitcast.clip, ...), custom_call_target="tpu_custom_call" | custom-call | tf_op jit(solution)/shard_map/space_forward/pallas_call | solution.py:152
  180.9 1.4 copy.163
  182.3 9.1 collective-permute-done.1
  191.5 1.4 copy.164
  192.9 25.0 %collective-permute-done.2 = bf16[196,4,768]{2,1,0:T(4,128)(2,1)} collective-permute-done((bf16[196,4,768]{2,1,0:T(4,128)(2,1)}, bf16[196,4,768]{2,1,0:T(4,128)(2,1)}, u32[]{:S(2)}, u32[]{:S(2)}) %collective-permute-start.2) | collective-permute-done | bytes 1204256 | tf_op jit(solution)/shard_map/ppermute | solution.py:583
  217.9 1.4 copy.165
  220.0 3.2 copy.166
  223.1 4.9 slice.157.up_ref
  228.0 59.4 %time_forward.1 = (bf16[3136,768]{1,0:T(8,128)(2,1)}, bf16[3136,768]{1,0:T(8,128)(2,1)}, bf16[3136,768]{1,0:T(8,128)(2,1)}, bf16[3136,768]{1,0:T(8,128)(2,1)}, b...) custom-call(bf16[3136,768]{1,0:T(8,128)(2,1)} %bitcast.107, ...), custom_call_target="tpu_custom_call" | custom-call | tf_op jit(solution)/shard_map/time_forward/pallas_call | solution.py:207
  287.4 184.2 %feed_forward.1 = (bf16[3136,768]{1,0:T(8,128)(2,1)}, f32[3136,768]{1,0:T(8,128)}, bf16[768,3072]{1,0:T(8,128)(2,1)}, bf16[3072,768]{1,0:T(8,128)(2,1)}, f32[3,7...) custom-call(f32[3136,768]{1,0:T(8,128)} %get-tuple-element.80.a_ref, bf16[3136,768]{1,0:T(8,128)(2,1)} %bitcast.109, ...), custom_call_target="tpu_custom_call" | custom-call | tf_op jit(solution)/shard_map/feed_forward/pallas_call | solution.py:297
  472.3 171.9 %time_back.1 = (bf16[3136,768]{1,0:T(8,128)(2,1)}, bf16[768,3072]{1,0:T(8,128)(2,1)}, f32[5,768]{1,0:T(8,128)}) custom-call(f32[3136,768]{1,0:T(8,128)} %get-tuple-element.82.g_ref, bf16[3136,768]{1,0:T(8,128)(2,1)} %bitcast.108, bf16[3136,768]{1,0:T(8,128)(2,1)} %get-tuple-element.83.in_ref, bf16[3136,768]{1,0:T(8,128)(2,1)} %get-tuple-element.84.q_ref, ...), custom_call_target="tpu_custom_call" | custom-call | tf_op jit(solution)/shard_map/time_back/pallas_call | solution.py:383
  644.3 9.2 reshape.112
  653.5 4.4 slice_bitcast_fusion
  657.8 1.7 collective-permute-start.13
  659.7 1.2 copy.194
  660.9 25.8 %space_back.4 = (bf16[4,196,2304]{2,1,0:T(8,128)(2,1)}, f32[768,768]{1,0:T(8,128)}, f32[1,768]{1,0:T(1,128)}) custom-call(bf16[4,196,768]{2,1,0:T(8,128)(2,1)} %bitcast.110, bf16[4,196,768]{2,1,0:T(8,128)(2,1)} %get-tuple-element.90.q_ref, bf16[4,196,768]{2,1,0:T(8,128)(2,1)} %get-tuple-element.91.k_ref, bf16[4,196,768]{2,1,0:T(8,128)(2,1)} %get-tuple-element.92.v_ref, ...), custom_call_target="tpu_custom_call" | custom-call | tf_op jit(solution)/shard_map/space_back/pallas_call | solution.py:426
  686.8 4.7 collective-permute-done.14
  691.4 1.2 copy.195
  692.6 24.7 %collective-permute-done.13 = bf16[196,4,768]{2,1,0:T(4,128)(2,1)S(1)} collective-permute-done((bf16[196,4,768]{2,1,0:T(4,128)(2,1)}, bf16[196,4,768]{2,1,0:T(4,128)(2,1)S(1)}, u32[]{:S(2)}, u32[]{:S(2)}) %collective-permute-start.13) | collective-permute-done | bytes 1204256 | tf_op jit(solution)/shard_map/ppermute | solution.py:583
  717.3 1.2 copy.196
  718.5 1.2 copy.197
  719.6 25.9 %space_back.7 = (bf16[4,196,2304]{2,1,0:T(8,128)(2,1)}, f32[768,768]{1,0:T(8,128)}, f32[1,768]{1,0:T(1,128)}) custom-call(bf16[4,196,768]{2,1,0:T(8,128)(2,1)} %bitcast.112, bf16[4,196,768]{2,1,0:T(8,128)(2,1)} %get-tuple-element.108.q_ref, bf16[4,196,768]{2,1,0:T(8,128)(2,1)} %get-tuple-element.109.k_ref, bf16[4,196,768]{2,1,0:T(8,128)(2,1)} %get-tuple-element.110.v_ref, ...), custom_call_target="tpu_custom_call" | custom-call | tf_op jit(solution)/shard_map/space_back/pallas_call | solution.py:426
  745.5 26.0 %space_back.6 = (bf16[4,196,2304]{2,1,0:T(8,128)(2,1)}, f32[768,768]{1,0:T(8,128)}, f32[1,768]{1,0:T(1,128)}) custom-call(bf16[4,196,768]{2,1,0:T(8,128)(2,1)} %bitcast.114, bf16[4,196,768]{2,1,0:T(8,128)(2,1)} %get-tuple-element.102.q_ref, bf16[4,196,768]{2,1,0:T(8,128)(2,1)} %get-tuple-element.103.k_ref, bf16[4,196,768]{2,1,0:T(8,128)(2,1)} %get-tuple-element.104.v_ref, ...), custom_call_target="tpu_custom_call" | custom-call | tf_op jit(solution)/shard_map/space_back/pallas_call | solution.py:426
  771.5 25.8 %space_back.5 = (bf16[4,196,2304]{2,1,0:T(8,128)(2,1)}, f32[768,768]{1,0:T(8,128)}, f32[1,768]{1,0:T(1,128)}) custom-call(bf16[4,196,768]{2,1,0:T(8,128)(2,1)} %bitcast.116, bf16[4,196,768]{2,1,0:T(8,128)(2,1)} %get-tuple-element.96.q_ref, bf16[4,196,768]{2,1,0:T(8,128)(2,1)} %get-tuple-element.97.k_ref, bf16[4,196,768]{2,1,0:T(8,128)(2,1)} %get-tuple-element.98.v_ref, ...), custom_call_target="tpu_custom_call" | custom-call | tf_op jit(solution)/shard_map/space_back/pallas_call | solution.py:426
  797.4 31.1 %space_weights.1 = (bf16[768,3072]{1,0:T(8,128)(2,1)}, f32[1,2304]{1,0:T(1,128)}) custom-call(bf16[4,196,768]{2,1,0:T(8,128)(2,1)} %get-tuple-element.117.refs_0_, bf16[4,196,768]{2,1,0:T(8,128)(2,1)} %get-tuple-element.118.refs_1_, bf16[4,196,768]{2,1,0:T(8,128)(2,1)} %get-tuple-element.119.refs_2_, bf16[4,196,768]{2,1,0:T(8,128)(2,1)} %get-tuple-element.120.refs_3_, ...), custom_call_target="tpu_custom_call" | custom-call | tf_op jit(solution)/shard_map/space_weights/pallas_call | solution.py:487
  829.1 9.0 reshape.111
  838.1 4.4 slice_bitcast_fusion.3
  842.6 3.5 broadcast_in_dim.22
  846.0 2.8 fusion
  850.9 1.6 collective-permute-start.11
  852.5 32.0 %input_grads.1 = (bf16[4,4,196,768]{3,2,1,0:T(8,128)(2,1)}, f32[2,768]{1,0:T(2,128)}) custom-call(s32[4]{0:T(128)} %pad_add_fusion.clips, bf16[4,196,768]{2,1,0:T(8,128)(2,1)} %bitcast.111, bf16[4,196,768]{2,1,0:T(8,128)(2,1)} %bitcast.117, bf16[4,196,768]{2,1,0:T(8,128)(2,1)} %bitcast.115, bf16[4,196,768]{2,1,0:T(8,128)(2,1)} %bitcast.113, ...), custom_call_target="tpu_custom_call" | custom-call | tf_op jit(solution)/shard_map/input_grads/pallas_call | solution.py:537
  884.5 0.8 fusion.8
  885.5 62.8 %psum.7 = f32[18,768]{1,0:T(8,128)S(1)} all-reduce(f32[18,768]{1,0:T(8,128)S(1)} %concatenate.32), channel_id=1, replica_groups=mesh['clip'=8,'frame'=4] {'clip','frame'}, use_global_device_ids=true, to_apply=%region_3.4 | all-reduce | flops 13824 | bytes 110592 | tf_op jit(solution)/shard_map/psum | solution.py:689
  950.4 6.5 copy.184
  957.9 2.7 bitcast_dynamic-update-slice_fusion.2
  960.7 2.7 bitcast_dynamic-update-slice_fusion.1
  963.4 2.7 bitcast_dynamic-update-slice_fusion
  966.1 1.6 convert_element_type.40
  967.7 1.6 convert_element_type.41
  969.4 1.4 slice_convert_fusion.3
  970.8 1.6 slice_convert_fusion.1
  972.4 1.6 slice_convert_fusion.2
  974.0 1.4 slice_convert_fusion.4
  (98 shorter events, 13.9 us)
Async XLA Ops:
  7.2 87.4 %all-gather.4.cloned.1.call-start = ((), (), s32[]{:S(2)}) async-start(), calls=%async_computation.4 | async-start | bytes 5068800 | tf_op jit(solution)/shard_map/all_gather | solution.py:561
  16.9 206.3 %all-gather.6.cloned.1.call-start = ((), (), s32[]{:S(2)}) async-start(), calls=%async_computation.5 | async-start | bytes 9732096 | tf_op jit(solution)/shard_map/all_gather | solution.py:561
  18.7 268.7 %all-gather.8.cloned.1.call-start = ((), (), s32[]{:S(2)}) async-start(), calls=%async_computation.6 | async-start | bytes 4866048 | tf_op jit(solution)/shard_map/all_gather | solution.py:561
  19.4 946.7 %reduce-scatter.9.cloned.1.call-start = ((), (), s32[]{:S(2)}) async-start(), calls=%async_computation.9 | async-start | bytes 4866048 | tf_op jit(solution)/shard_map/reduce_scatter | solution.py:565
  19.5 10.8 %slice-start = ((s8[4816896]{0:T(1024)(128)(4,1)}), s8[622592]{0:T(1024)(128)(4,1)S(1)}, s32[]{:S(2)}) async-start(s8[4816896]{0:T(1024)(128)(4,1)} %bitcast.118), calls=%async_computation.11 | async-start | bytes 1245184
  19.5 8.7 copy-start.1
  19.5 10.7 %slice-start.1 = ((s8[4816896]{0:T(1024)(128)(4,1)}), s8[4194304]{0:T(1024)(128)(4,1)S(1)}, s32[]{:S(2)}) async-start(s8[4816896]{0:T(1024)(128)(4,1)} %bitcast.118), calls=%async_computation.12 | async-start | bytes 8388608
  25.1 126.6 %collective-permute-start.3 = (bf16[196,4,768]{2,1,0:T(4,128)(2,1)}, bf16[196,4,768]{2,1,0:T(4,128)(2,1)}, u32[]{:S(2)}, u32[]{:S(2)}) collective-permute-start(bf16[196,4,768]{2,1,0:T(4,128)(2,1)} %get-tuple-element.209), channel_id=1, source_target_pairs={{0,1},{1,0},{2,3},{3,2},{4,5},{5,4},{6,7},{7,6},{8,9},{9,8},{10,11... | collective-permute-start | bytes 3612680 | tf_op jit(solution)/shard_map/ppermute | solution.py:583
  25.6 128.9 %collective-permute-start.4 = (bf16[196,4,768]{2,1,0:T(4,128)(2,1)}, bf16[196,4,768]{2,1,0:T(4,128)(2,1)}, u32[]{:S(2)}, u32[]{:S(2)}) collective-permute-start(bf16[196,4,768]{2,1,0:T(4,128)(2,1)} %get-tuple-element.211), channel_id=1, source_target_pairs={{0,2},{1,3},{2,0},{3,1},{4,6},{5,7},{6,4},{7,5},{8,10},{9,11},{10,... | collective-permute-start | bytes 3612680 | tf_op jit(solution)/shard_map/ppermute | solution.py:583
  28.1 126.4 %collective-permute-start.5 = (bf16[196,4,768]{2,1,0:T(4,128)(2,1)}, bf16[196,4,768]{2,1,0:T(4,128)(2,1)}, u32[]{:S(2)}, u32[]{:S(2)}) collective-permute-start(bf16[196,4,768]{2,1,0:T(4,128)(2,1)} %get-tuple-element.210), channel_id=1, source_target_pairs={{0,3},{1,2},{2,1},{3,0},{4,7},{5,6},{6,5},{7,4},{8,11},{9,10},{10,... | collective-permute-start | bytes 3612680 | tf_op jit(solution)/shard_map/ppermute | solution.py:583
  28.2 4.9 collective-permute-start.6
  28.4 122.1 %collective-permute-start.7 = (s32[196,4]{0,1:T(4,128)S(1)}, s32[196,4]{0,1:T(4,128)S(1)}, u32[]{:S(2)}, u32[]{:S(2)}) collective-permute-start(s32[196,4]{0,1:T(4,128)S(1)} %get-tuple-element.220), channel_id=1, source_target_pairs={{0,2},{1,3},{2,0},{3,1},{4,6},{5,7},{6,4},{7,5},{8,10},{9,11},{10,... | collective-permute-start | bytes 9416 | tf_op jit(solution)/shard_map/ppermute | solution.py:583
  33.2 117.6 %collective-permute-start.8 = (s32[196,4]{0,1:T(4,128)S(1)}, s32[196,4]{0,1:T(4,128)S(1)}, u32[]{:S(2)}, u32[]{:S(2)}) collective-permute-start(s32[196,4]{0,1:T(4,128)S(1)} %get-tuple-element.219), channel_id=1, source_target_pairs={{0,3},{1,2},{2,1},{3,0},{4,7},{5,6},{6,5},{7,4},{8,11},{9,10},{10,... | collective-permute-start | bytes 9416 | tf_op jit(solution)/shard_map/ppermute | solution.py:583
  150.5 30.4 %collective-permute-start = (bf16[196,4,768]{2,1,0:T(4,128)(2,1)S(1)}, bf16[196,4,768]{2,1,0:T(4,128)(2,1)}, u32[]{:S(2)}, u32[]{:S(2)}) collective-permute-start(bf16[196,4,768]{2,1,0:T(4,128)(2,1)S(1)} %copy.156), channel_id=1, source_target_pairs={{0,1},{1,0},{2,3},{3,2},{4,5},{5,4},{6,7},{7,6},{8,9},{9,8},{10,11... | collective-permute-start | bytes 3612680 | tf_op jit(solution)/shard_map/ppermute | solution.py:583
  150.7 40.7 %collective-permute-start.1 = (bf16[196,4,768]{2,1,0:T(4,128)(2,1)}, bf16[196,4,768]{2,1,0:T(4,128)(2,1)}, u32[]{:S(2)}, u32[]{:S(2)}) collective-permute-start(bf16[196,4,768]{2,1,0:T(4,128)(2,1)} %copy.159), channel_id=1, source_target_pairs={{0,2},{1,3},{2,0},{3,1},{4,6},{5,7},{6,4},{7,5},{8,10},{9,11},{10,... | collective-permute-start | bytes 3612680 | tf_op jit(solution)/shard_map/ppermute | solution.py:583
  151.7 66.2 %collective-permute-start.2 = (bf16[196,4,768]{2,1,0:T(4,128)(2,1)}, bf16[196,4,768]{2,1,0:T(4,128)(2,1)}, u32[]{:S(2)}, u32[]{:S(2)}) collective-permute-start(bf16[196,4,768]{2,1,0:T(4,128)(2,1)} %copy.162), channel_id=1, source_target_pairs={{0,3},{1,2},{2,1},{3,0},{4,7},{5,6},{6,5},{7,4},{8,11},{9,10},{10,... | collective-permute-start | bytes 3612680 | tf_op jit(solution)/shard_map/ppermute | solution.py:583
  192.9 26.4 %copy-start = (bf16[4,196,768]{2,1,0:T(8,128)(2,1)S(1)}, bf16[4,196,768]{2,1,0:T(8,128)(2,1)}, u32[]{:S(2)}) copy-start(bf16[4,196,768]{2,1,0:T(8,128)(2,1)} %get-tuple-element.76) | copy-start | bytes 3612676
  471.6 496.1 %reduce-scatter.11.cloned.1.call-start = ((), (), s32[]{:S(2)}) async-start(), calls=%async_computation.10 | async-start | bytes 4866048 | tf_op jit(solution)/shard_map/reduce_scatter | solution.py:565
  472.2 497.2 %reduce-scatter.7.cloned.1.call-start = ((), (), s32[]{:S(2)}) async-start(), calls=%async_computation.8 | async-start | bytes 4866048 | tf_op jit(solution)/shard_map/reduce_scatter | solution.py:565
  644.2 328.2 %reduce-scatter.5.cloned.1.call-start = ((), (), s32[]{:S(2)}) async-start(), calls=%async_computation.7 | async-start | bytes 4866048 | tf_op jit(solution)/shard_map/reduce_scatter | solution.py:565
  657.8 33.6 %collective-permute-start.14 = (bf16[196,4,768]{2,1,0:T(4,128)(2,1)}, bf16[196,4,768]{2,1,0:T(4,128)(2,1)S(1)}, u32[]{:S(2)}, u32[]{:S(2)}) collective-permute-start(bf16[196,4,768]{2,1,0:T(4,128)(2,1)} %get-tuple-element.201), channel_id=1, source_target_pairs={{0,3},{1,2},{2,1},{3,0},{4,7},{5,6},{6,5},{7,4},{8,11},{9,10},{10,... | collective-permute-start | bytes 3612680 | tf_op jit(solution)/shard_map/ppermute | solution.py:583
  657.8 59.4 %collective-permute-start.13 = (bf16[196,4,768]{2,1,0:T(4,128)(2,1)}, bf16[196,4,768]{2,1,0:T(4,128)(2,1)S(1)}, u32[]{:S(2)}, u32[]{:S(2)}) collective-permute-start(bf16[196,4,768]{2,1,0:T(4,128)(2,1)} %get-tuple-element.202), channel_id=1, source_target_pairs={{0,2},{1,3},{2,0},{3,1},{4,6},{5,7},{6,4},{7,5},{8,10},{9,11},{10,... | collective-permute-start | bytes 3612680 | tf_op jit(solution)/shard_map/ppermute | solution.py:583
  659.6 58.9 %collective-permute-start.12 = (bf16[196,4,768]{2,1,0:T(4,128)(2,1)}, bf16[196,4,768]{2,1,0:T(4,128)(2,1)S(1)}, u32[]{:S(2)}, u32[]{:S(2)}) collective-permute-start(bf16[196,4,768]{2,1,0:T(4,128)(2,1)} %get-tuple-element.203), channel_id=1, source_target_pairs={{0,1},{1,0},{2,3},{3,2},{4,5},{5,4},{6,7},{7,6},{8,9},{9,8},{10,11... | collective-permute-start | bytes 3612680 | tf_op jit(solution)/shard_map/ppermute | solution.py:583
  838.1 4.5 copy-start.3
  842.5 115.5 %collective-permute-start.9 = (bf16[196,4,768]{2,1,0:T(4,128)(2,1)}, bf16[196,4,768]{2,1,0:T(4,128)(2,1)}, u32[]{:S(2)}, u32[]{:S(2)}) collective-permute-start(bf16[196,4,768]{2,1,0:T(4,128)(2,1)} %get-tuple-element.207), channel_id=1, source_target_pairs={{0,1},{1,0},{2,3},{3,2},{4,5},{5,4},{6,7},{7,6},{8,9},{9,8},{10,11... | collective-permute-start | bytes 3612680 | tf_op jit(solution)/shard_map/ppermute | solution.py:583
  846.0 2.8 copy-start.4
  846.0 3.3 copy-start.2
  850.6 110.1 %collective-permute-start.10 = (bf16[196,4,768]{2,1,0:T(4,128)(2,1)S(1)}, bf16[196,4,768]{2,1,0:T(4,128)(2,1)}, u32[]{:S(2)}, u32[]{:S(2)}) collective-permute-start(bf16[196,4,768]{2,1,0:T(4,128)(2,1)S(1)} %get-tuple-element.206), channel_id=1, source_target_pairs={{0,2},{1,3},{2,0},{3,1},{4,6},{5,7},{6,4},{7,5},{8,10},{9,11},{10,... | collective-permute-start | bytes 3612680 | tf_op jit(solution)/shard_map/ppermute | solution.py:583
  850.9 34.4 %copy-start.5 = (f32[1,2304]{1,0:T(1,128)S(1)}, f32[1,2304]{1,0:T(1,128)}, u32[]{:S(2)}) copy-start(f32[1,2304]{1,0:T(1,128)} %get-tuple-element.125) | copy-start | bytes 27652
  850.9 34.4 %copy-start.6 = (f32[1,768]{1,0:T(1,128)S(1)}, f32[1,768]{1,0:T(1,128)}, u32[]{:S(2)}) copy-start(f32[1,768]{1,0:T(1,128)} %get-tuple-element.126) | copy-start | bytes 9220
  850.9 34.4 %copy-start.7 = (f32[1,768]{1,0:T(1,128)S(1)}, f32[1,768]{1,0:T(1,128)}, u32[]{:S(2)}) copy-start(f32[1,768]{1,0:T(1,128)} %get-tuple-element.129) | copy-start | bytes 9220
  850.9 34.4 %copy-start.8 = (f32[1,768]{1,0:T(1,128)S(1)}, f32[1,768]{1,0:T(1,128)}, u32[]{:S(2)}) copy-start(f32[1,768]{1,0:T(1,128)} %get-tuple-element.128) | copy-start | bytes 9220
  850.9 34.4 %copy-start.9 = (f32[1,768]{1,0:T(1,128)S(1)}, f32[1,768]{1,0:T(1,128)}, u32[]{:S(2)}) copy-start(f32[1,768]{1,0:T(1,128)} %get-tuple-element.127) | copy-start | bytes 9220
  850.9 34.4 %copy-start.10 = (f32[1,768]{1,0:T(1,128)S(1)}, f32[1,768]{1,0:T(1,128)}, u32[]{:S(2)}) copy-start(f32[1,768]{1,0:T(1,128)} %get-tuple-element.131) | copy-start | bytes 9220
  850.9 112.5 %collective-permute-start.11 = (bf16[196,4,768]{2,1,0:T(4,128)(2,1)S(1)}, bf16[196,4,768]{2,1,0:T(4,128)(2,1)}, u32[]{:S(2)}, u32[]{:S(2)}) collective-permute-start(bf16[196,4,768]{2,1,0:T(4,128)(2,1)S(1)} %get-tuple-element.205), channel_id=1, source_target_pairs={{0,3},{1,2},{2,1},{3,0},{4,7},{5,6},{6,5},{7,4},{8,11},{9,10},{10,... | collective-permute-start | bytes 3612680 | tf_op jit(solution)/shard_map/ppermute | solution.py:583
Sparse Core Ops, SparseCore 0:
  17.0 77.5 all-gather.3
  98.0 91.2 all-gather.5
  192.2 64.2 all-gather.7
  471.8 107.1 reduce-scatter.8
  585.2 110.6 reduce-scatter.10
  701.2 105.8 reduce-scatter.6
  828.6 116.8 reduce-scatter.4

commit v2 on v1

v2 whole, which is shorter than its diff:
```python
import functools

import jax
import jax.numpy as jnp
from jax import lax
from jax.experimental import pallas as pl
from jax.experimental.pallas import tpu as pltpu
from jax.sharding import PartitionSpec as P

D = 768
HEADS = 12
HEAD = 64
FF = 3072
EPS = 1e-06
F32 = jnp.float32
BF16 = jnp.bfloat16
PARAMS = pltpu.CompilerParams(vmem_limit_bytes=60 << 20)


def cost(flops, moved=0):
    return pl.CostEstimate(flops=int(flops), bytes_accessed=int(moved), transcendentals=0)


GAIN, SHIFT, QV, MIX, UP = 0, 3, 6, 10, 13


def dot(left, right):
    return jnp.dot(left, right, preferred_element_type=F32)


def dot_nt(left, right):
    return lax.dot_general(left, right, (((1,), (1,)), ((), ())), preferred_element_type=F32)


def dot_tn(left, right):
    return lax.dot_general(left, right, (((0,), (0,)), ((), ())), preferred_element_type=F32)


def normalize(rows):
    center = rows - jnp.mean(rows, -1, keepdims=True)
    inverse = lax.rsqrt(jnp.mean(center * center, -1, keepdims=True) + EPS)
    return center * inverse, inverse


def normalize_back(grad_out, hat, inverse, gain):
    grad_hat = grad_out * gain
    return inverse * (
        grad_hat
        - jnp.mean(grad_hat, -1, keepdims=True)
        - hat * jnp.mean(grad_hat * hat, -1, keepdims=True)
    )


def column_sum(rows):
    return jnp.sum(rows, 0, keepdims=True)


def first_lanes(shape):
    return lax.broadcasted_iota(jnp.int32, shape, 1) < HEAD


def halves(block):
    low = first_lanes(block.shape)
    zero = jnp.zeros_like(block)
    return jnp.where(low, block, zero), jnp.where(low, zero, block)


def pair(index):
    return slice(2 * HEAD * index, 2 * HEAD * (index + 1))


def grow(block, rows):
    if rows == block.shape[0]:
        return block
    return jnp.concatenate([block, jnp.zeros((rows - block.shape[0], block.shape[1]), block.dtype)], 0)


def stack(block):
    return jnp.concatenate(halves(block), 0)


def merge(two):
    rows = two.shape[0] // 2
    return jnp.where(first_lanes((rows, two.shape[1])), two[:rows], two[rows:])


def kept(rows):
    return HEADS // 2, 2 * padded(rows), rows


def padded(rows):
    return -(-rows // 16) * 16


def attention(query, key, value, keep_probs, frames=None):
    rows = query.shape[0]
    full = padded(rows)
    place = lax.broadcasted_iota(jnp.int32, (full, rows), 0)
    if frames is not None:
        mask = place // frames == lax.broadcasted_iota(jnp.int32, (full, rows), 1) // frames
    else:
        mask = place < rows
    outs = []

    def score(p):
        return dot_nt(stack(grow(key[:, pair(p)], full)), query[:, pair(p)])

    scores = score(0)
    for p in range(HEADS // 2):
        now = scores
        if p + 1 < HEADS // 2:
            scores = score(p + 1)
        probs = []
        for one in (now[:full], now[full:]):
            one = jnp.where(mask, one, -1e30)
            expo = jnp.exp(one - jnp.max(one, 0, keepdims=True))
            probs.append((expo * (1.0 / jnp.sum(expo, 0, keepdims=True))).astype(BF16))
        probs = jnp.concatenate(probs, 0)
        keep_probs(p, probs)
        outs.append(dot_tn(probs, stack(grow(value[:, pair(p)], full))).astype(BF16))
    return jnp.concatenate(outs, 1)


def attention_back(query, key, value, grad_mix, probs_of):
    rows = query.shape[0]
    full = padded(rows)
    grad_q, grad_k, grad_v = [], [], []

    def probs_grad(p):
        return dot_nt(stack(grow(value[:, pair(p)], full)), grad_mix[:, pair(p)])

    grad_p = probs_grad(0)
    for p in range(HEADS // 2):
        probs = probs_of(p)
        wide = probs.astype(F32)
        term = wide * grad_p
        grad_s = []
        for head in (slice(0, full), slice(full, 2 * full)):
            grad_s.append((term[head] - wide[head] * column_sum(term[head])).astype(BF16))
        grad_s = jnp.concatenate(grad_s, 0)
        if p + 1 < HEADS // 2:
            grad_p = probs_grad(p + 1)
        to_v = merge(dot(probs, grad_mix[:, pair(p)]))
        to_k = merge(dot(grad_s, query[:, pair(p)]))
        to_q = dot_tn(grad_s, stack(grow(key[:, pair(p)], full)))
        grad_q.append((to_q * HEAD ** (-0.5)).astype(BF16))
        grad_k.append(to_k[:rows].astype(BF16))
        grad_v.append(to_v[:rows].astype(BF16))
    return jnp.concatenate(grad_q + grad_k + grad_v, 1)


def project(rows, weights, table, query_row):
    proj = dot(rows, weights)
    query = (proj[:, :D] + table[query_row : query_row + 1, :]).astype(BF16)
    key = proj[:, D : 2 * D].astype(BF16)
    value = (proj[:, 2 * D :] + table[query_row + 1 : query_row + 2, :]).astype(BF16)
    return (query.astype(F32) * HEAD ** (-0.5)).astype(BF16), key, value


def fixed(shape):
    return pl.BlockSpec(shape, lambda *_: (0,) * len(shape), pipeline_mode=pl.Buffered(1))


def columns_of(width, index):
    return pl.BlockSpec((D, width), lambda *_: (0, index), pipeline_mode=pl.Buffered(1))


def collect(refs, scratch):
    frames = refs[0].shape[1]
    for n, ref in enumerate(refs):
        scratch[:, n * frames : (n + 1) * frames, :] = ref[...].astype(F32)
    return scratch[...].reshape(-1, D)


def deal(rows, scratch, refs):
    frames = refs[0].shape[1]
    scratch[...] = rows.reshape(scratch.shape)
    for n, ref in enumerate(refs):
        ref[...] = scratch[:, n * frames : (n + 1) * frames, :].astype(BF16)


def clear(first, *refs):
    @pl.when(first)
    def _():
        for ref in refs:
            ref[...] = jnp.zeros_like(ref)


def space_kernel(clip, x_ref, table, w_ref, in_ref, q_ref, k_ref, v_ref, mix_ref, p_ref, out_ref):
    rows = x_ref[0, 0].astype(F32)
    hat, _ = normalize(rows)
    normed = (hat * table[GAIN : GAIN + 1, :] + table[SHIFT : SHIFT + 1, :]).astype(BF16)
    in_ref[0] = normed
    query, key, value = project(normed, w_ref[:, : 3 * D], table, QV)
    q_ref[0], k_ref[0], v_ref[0] = query, key, value

    def keep(heads, probs):
        p_ref[0, heads] = probs

    mixed = attention(query, key, value, keep)
    mix_ref[0] = mixed
    after = rows + dot(mixed, w_ref[:, 3 * D : 4 * D]) + table[MIX : MIX + 1, :]
    out_ref[0] = after.astype(BF16)


def space_forward(clip, inputs, table, weights):
    _, frames, places, _ = inputs.shape

    def frame(*tail):
        return pl.BlockSpec((1,) + tail, lambda i, c: (i,) + (0,) * len(tail))

    def shape(*tail):
        return jax.ShapeDtypeStruct((frames,) + tail, BF16)

    return pl.pallas_call(
        space_kernel,
        grid_spec=pltpu.PrefetchScalarGridSpec(
            num_scalar_prefetch=1,
            grid=(frames,),
            in_specs=[
                pl.BlockSpec((1, 1, places, D), lambda i, c: (c[0], i, 0, 0)),
                fixed(table.shape),
                fixed((D, 4 * D)),
            ],
            out_specs=[frame(places, D)] * 5 + [frame(*kept(places)), frame(places, D)],
        ),
        out_shape=[shape(places, D)] * 5 + [shape(*kept(places)), shape(places, D)],
        compiler_params=PARAMS,
        cost_estimate=cost(24 * frames * places * D * D),
        name="space_forward",
    )(clip, inputs, table, weights)


def largest_divisor(number, limit):
    return max(n for n in range(1, limit + 1) if number % n == 0)


def time_kernel(frames, group, ring, *refs):
    parts, (table, w_ref) = refs[:ring], refs[ring : ring + 2]
    a_ref, in_ref, q_ref, k_ref, v_ref, mix_ref, p_ref, out_ref, scratch = refs[ring + 2 :]
    rows = collect(parts, scratch)
    a_ref[...] = rows.astype(BF16)
    hat, _ = normalize(rows)
    normed = (hat * table[GAIN + 1 : GAIN + 2, :] + table[SHIFT + 1 : SHIFT + 2, :]).astype(BF16)
    in_ref[...] = normed
    query, key, value = project(normed, w_ref[:, : 3 * D], table, QV + 2)
    q_ref[...], k_ref[...], v_ref[...] = query, key, value

    def one_group(g):
        span = slice(g * group, (g + 1) * group)

        def keep(heads, probs):
            p_ref[g, heads] = probs

        mix_ref[span, :] = attention(q_ref[span, :], k_ref[span, :], v_ref[span, :], keep, frames)

    for g in range(rows.shape[0] // group):
        one_group(g)
    out_ref[...] = rows + dot(mix_ref[...], w_ref[:, 3 * D :]) + table[MIX + 1 : MIX + 2, :]


def time_tiles(places, frames):
    per_group = largest_divisor(places, 128 // frames)
    per_tile = per_group * largest_divisor(places // per_group, 4)
    return per_tile * frames, per_group * frames


def piece_specs(parts, tile):
    frames = parts[0].shape[1]
    places = tile // (frames * len(parts))
    return [pl.BlockSpec((places, frames, D), lambda i: (i, 0, 0))] * len(parts)


def join_scratch(parts, tile):
    frames = parts[0].shape[1] * len(parts)
    return pltpu.VMEM((tile // frames, frames, D), F32)


def time_forward(parts, table, weights):
    places, frames = parts[0].shape[0], parts[0].shape[1] * len(parts)
    tokens = places * frames
    tile, group = time_tiles(places, frames)
    rows = pl.BlockSpec((tile, D), lambda i: (i, 0))
    return pl.pallas_call(
        functools.partial(time_kernel, frames, group, len(parts)),
        grid=(tokens // tile,),
        in_specs=piece_specs(parts, tile) + [fixed(table.shape), columns_of(4 * D, 0)],
        out_specs=[rows] * 6
        + [pl.BlockSpec((tile // group,) + kept(group), lambda i: (i, 0, 0, 0)), rows],
        out_shape=[jax.ShapeDtypeStruct((tokens, D), BF16)] * 6
        + [
            jax.ShapeDtypeStruct((tokens // group,) + kept(group), BF16),
            jax.ShapeDtypeStruct((tokens, D), F32),
        ],
        scratch_shapes=[join_scratch(parts, tile)],
        compiler_params=PARAMS,
        cost_estimate=cost(24 * tokens * D * D),
        name="time_forward",
    )(*parts, table, weights)


def gelu_parts(u):
    bell = jnp.exp(-0.5 * u * u)
    base = 1.0 + 0.2316418886 * jnp.abs(u)
    t = 1.0 / base
    poly = t * (
        0.127414796 + t * (-0.142248368 + t * (0.7107068705 + t * (-0.7265760135 + t * 0.5307027145)))
    )
    tail = poly * bell
    area = jnp.where(u >= 0, 1.0 - tail, tail)
    return u * area, area + 0.3989422804014327 * (u * bell)


FF_CHUNK = 768


def feed_kernel(ring, *refs):
    teachers, refs = refs[:ring], refs[ring:]
    (a_ref, valid_ref, scale_ref, table, up_bias, up_ref, down_ref), refs = refs[:7], refs[7:]
    outs, refs = refs[:ring], refs[ring:]
    g_ref, d_ref, rows_ref, bias_ref, square_ref, hidden, slope, d_up, d_down, stage, sems, scratch = refs
    step, last = pl.program_id(0), pl.num_programs(0) - 1
    clear(step == 0, d_up, d_down, rows_ref, bias_ref, square_ref)
    after = a_ref[...]
    hat, inverse = normalize(after)
    normed = (hat * table[GAIN + 2 : GAIN + 3, :] + table[SHIFT + 2 : SHIFT + 3, :]).astype(BF16)
    total = after + table[MIX + 2 : MIX + 3, :]
    chunks = [slice(c, c + FF_CHUNK) for c in range(0, FF, FF_CHUNK)]
    for c in chunks:
        act, rise = gelu_parts(dot(normed, up_ref[:, c]) + up_bias[:, c])
        act = act.astype(BF16)
        hidden[:, c] = act
        slope[:, c] = rise.astype(BF16)
        total = total + dot(act, down_ref[:, c])
    deal(total, scratch, outs)
    diff = (total - collect(teachers, scratch)) * valid_ref[...]
    square_ref[...] += column_sum(diff * diff)
    grad = diff * scale_ref[0, 0]
    grad_low = grad.astype(BF16)
    bias_c = column_sum(grad_low.astype(F32))
    back = jnp.zeros_like(grad)
    for c in chunks:
        grad_pre = dot_nt(grad_low, down_ref[:, c]) * slope[:, c].astype(F32)
        grad_pre = grad_pre.astype(BF16)
        bias_ref[:, c] += column_sum(grad_pre.astype(F32))
        d_down[:, c] += dot_tn(hidden[:, c], grad_low)
        d_up[:, c] += dot_tn(normed, grad_pre)
        back = back + dot_nt(grad_pre, up_ref[:, c])
    rows_ref[...] += jnp.concatenate([column_sum(back * hat), column_sum(back), bias_c], 0)
    g_ref[...] = grad + normalize_back(back, hat, inverse, table[GAIN + 2 : GAIN + 3, :])

    @pl.when(step == last)
    def _():
        moves = []
        for source, start in ((d_up, 4 * D), (d_down, 4 * D + FF)):
            moves += [(source.at[:, c], d_ref.at[:, start + c.start : start + c.stop]) for c in chunks]
        flush(moves, stage, sems)


def flush(moves, stage, sems):
    copies = []
    for i, (source, target) in enumerate(moves):
        if i >= 2:
            copies[i - 2].wait()
        stage[i % 2] = source[...].astype(BF16)
        copies.append(pltpu.make_async_copy(stage.at[i % 2], target, sems.at[i % 2]))
        copies[i].start()
    for copy in copies[-2:]:
        copy.wait()


def feed_forward(after_b, teachers, valid, scale, table, up_bias, weights, tile):
    tokens, ring = after_b.shape[0], len(teachers)
    rows = pl.BlockSpec((tile, D), lambda i: (i, 0))
    *outs, grad, d_feed, sums, bias, squares = pl.pallas_call(
        functools.partial(feed_kernel, ring),
        grid=(tokens // tile,),
        in_specs=piece_specs(teachers, tile)
        + [
            rows,
            pl.BlockSpec((tile, 1), lambda i: (i, 0)),
            pl.BlockSpec(memory_space=pltpu.SMEM),
            fixed(table.shape),
            fixed((1, FF)),
            columns_of(FF, 1),
            columns_of(FF, 2),
        ],
        out_specs=piece_specs(teachers, tile)
        + [rows, pl.BlockSpec(memory_space=pl.ANY), fixed((3, D)), fixed((1, FF)), fixed((1, D))],
        out_shape=[jax.ShapeDtypeStruct(t.shape, BF16) for t in teachers]
        + [
            jax.ShapeDtypeStruct((tokens, D), F32),
            jax.ShapeDtypeStruct((D, 4 * D + 2 * FF), BF16),
            jax.ShapeDtypeStruct((3, D), F32),
            jax.ShapeDtypeStruct((1, FF), F32),
            jax.ShapeDtypeStruct((1, D), F32),
        ],
        scratch_shapes=[
            pltpu.VMEM((tile, FF), BF16),
            pltpu.VMEM((tile, FF), BF16),
            pltpu.VMEM((D, FF), F32),
            pltpu.VMEM((D, FF), F32),
            pltpu.VMEM((2, D, FF_CHUNK), BF16),
            pltpu.SemaphoreType.DMA((2,)),
            join_scratch(teachers, tile),
        ],
        compiler_params=PARAMS,
        cost_estimate=cost(80 * tokens * D * D),
        name="feed_forward",
    )(*teachers, after_b, valid, scale, table, up_bias, weights, weights)
    return outs, grad, d_feed, sums, bias, squares


def time_back_kernel(group, ring, *refs):
    (g_ref, a_ref, in_ref, q_ref, k_ref, v_ref, mix_ref, p_ref, table, w_ref), refs = refs[:10], refs[11:]
    outs, refs = refs[:ring], refs[ring:]
    d_ref, rows_ref, grad_mix, grad_proj, d_proj, d_out, stage, sems, scratch = refs
    step, last = pl.program_id(0), pl.num_programs(0) - 1
    clear(step == 0, d_proj, d_out, rows_ref)
    grad = g_ref[...]
    grad_low = grad.astype(BF16)
    d_out[...] += dot_tn(mix_ref[...], grad_low)
    grad_mix[...] = dot_nt(grad_low, w_ref[:, 3 * D :]).astype(BF16)

    def one_group(g):
        span = slice(g * group, (g + 1) * group)
        grad_proj[span, :] = attention_back(
            q_ref[span, :],
            k_ref[span, :],
            v_ref[span, :],
            grad_mix[span, :],
            lambda heads: p_ref[g, heads],
        )

    for g in range(grad.shape[0] // group):
        one_group(g)
    proj = grad_proj[...]
    d_proj[...] += dot_tn(in_ref[...], proj)
    sums = column_sum(proj.astype(F32))
    back = dot_nt(proj, w_ref[:, : 3 * D])
    hat, inverse = normalize(a_ref[...].astype(F32))
    rows_ref[...] += jnp.concatenate(
        [
            column_sum(back * hat),
            column_sum(back),
            sums[:, :D],
            sums[:, 2 * D :],
            column_sum(grad_low.astype(F32)),
        ],
        0,
    )
    deal(grad + normalize_back(back, hat, inverse, table[GAIN + 1 : GAIN + 2, :]), scratch, outs)

    @pl.when(step == last)
    def _():
        moves = [(d_proj.at[:, pl.ds(c * D, D)], d_ref.at[:, pl.ds(c * D, D)]) for c in range(3)]
        flush(moves + [(d_out, d_ref.at[:, pl.ds(3 * D, D)])], stage, sems)


def time_back(grad, saved, like, table, weights, matrix):
    ring, tokens = len(like), grad.shape[0]
    places, frames = like[0].shape[0], like[0].shape[1] * ring
    tile, group = time_tiles(places, frames)
    rows = pl.BlockSpec((tile, D), lambda i: (i, 0))
    *outs, d_time, sums = pl.pallas_call(
        functools.partial(time_back_kernel, group, ring),
        grid=(tokens // tile,),
        in_specs=[rows] * 7
        + [
            pl.BlockSpec((tile // group,) + kept(group), lambda i: (i, 0, 0, 0)),
            fixed(table.shape),
            columns_of(4 * D, 0),
            pl.BlockSpec(memory_space=pl.ANY),
        ],
        out_specs=piece_specs(like, tile) + [pl.BlockSpec(memory_space=pl.ANY), fixed((5, D))],
        out_shape=[jax.ShapeDtypeStruct(t.shape, BF16) for t in like]
        + [jax.ShapeDtypeStruct(matrix.shape, BF16), jax.ShapeDtypeStruct((5, D), F32)],
        input_output_aliases={10: ring},
        scratch_shapes=[
            pltpu.VMEM((tile, D), BF16),
            pltpu.VMEM((tile, 3 * D), BF16),
            pltpu.VMEM((D, 3 * D), F32),
            pltpu.VMEM((D, D), F32),
            pltpu.VMEM((2, D, D), BF16),
            pltpu.SemaphoreType.DMA((2,)),
            join_scratch(like, tile),
        ],
        compiler_params=PARAMS,
        cost_estimate=cost(42 * tokens * D * D),
        name="time_back",
    )(grad, *saved, table, weights, matrix)
    return outs, d_time, sums


def space_back_kernel(g_ref, q_ref, k_ref, v_ref, mix_ref, p_ref, w_ref, out_ref, d_ref, bias_ref):
    clear(pl.program_id(0) == 0, d_ref, bias_ref)
    grad = g_ref[0]
    d_ref[...] += dot_tn(mix_ref[0], grad)
    bias_ref[...] += column_sum(grad.astype(F32))
    grad_mix = dot_nt(grad, w_ref[...]).astype(BF16)
    out_ref[0] = attention_back(
        q_ref[0], k_ref[0], v_ref[0], grad_mix, lambda heads: p_ref[0, heads]
    )


def space_back(grad, saved, weights):
    frames, places, _ = grad.shape

    def frame(*tail):
        return pl.BlockSpec((1,) + tail, lambda i: (i,) + (0,) * len(tail))

    return pl.pallas_call(
        space_back_kernel,
        grid=(frames,),
        in_specs=[frame(places, D)] * 5
        + [
            frame(*kept(places)),
            pl.BlockSpec((D, D), lambda i: (0, 3), pipeline_mode=pl.Buffered(1)),
        ],
        out_specs=[frame(places, 3 * D), fixed((D, D)), fixed((1, D))],
        out_shape=[
            jax.ShapeDtypeStruct((frames, places, 3 * D), BF16),
            jax.ShapeDtypeStruct((D, D), F32),
            jax.ShapeDtypeStruct((1, D), F32),
        ],
        compiler_params=PARAMS,
        cost_estimate=cost(24 * frames * places * D * D),
        name="space_back",
    )(grad, *saved, weights)


SMALL = 128


def space_weight_kernel(parts, steps, *refs):
    ins, projs, outs = refs[:parts], refs[parts : 2 * parts], refs[2 * parts : 3 * parts]
    d_ref, rows_ref, d_proj, d_out, stage, sems = refs[3 * parts :]
    step, last = pl.program_id(0), pl.num_programs(0) - 1
    clear(step == 0, d_proj, rows_ref)
    for part in range(parts):

        @pl.when(step // steps == part)
        def _():
            frames = range(ins[part].shape[0])
            d_proj[...] += sum(dot_tn(ins[part][f], projs[part][f]) for f in frames)
            rows_ref[...] += sum(column_sum(projs[part][f].astype(F32)) for f in frames)

    @pl.when(step == last)
    def _():
        d_out[...] = sum(ref[...] for ref in outs)
        moves = [(d_proj.at[:, pl.ds(c * D, D)], d_ref.at[:, pl.ds(c * D, D)]) for c in range(3)]
        flush(moves + [(d_out, d_ref.at[:, pl.ds(3 * D, D)])], stage, sems)


def space_weights(ins, projs, outs):
    parts = len(ins)
    frames, places, _ = ins[0].shape
    block = largest_divisor(frames, 2)
    steps = frames // block

    def frame(part, width):
        return pl.BlockSpec(
            (block, places, width), lambda i: (jnp.clip(i - part * steps, 0, steps - 1), 0, 0)
        )

    return pl.pallas_call(
        functools.partial(space_weight_kernel, parts, steps),
        grid=(parts * steps,),
        in_specs=[frame(p, D) for p in range(parts)]
        + [frame(p, 3 * D) for p in range(parts)]
        + [fixed((D, D))] * parts,
        out_specs=[pl.BlockSpec(memory_space=pl.ANY), fixed((1, 3 * D))],
        out_shape=[
            jax.ShapeDtypeStruct((D, 4 * D), BF16),
            jax.ShapeDtypeStruct((1, 3 * D), F32),
        ],
        scratch_shapes=[
            pltpu.VMEM((D, 3 * D), F32),
            pltpu.VMEM((D, D), F32),
            pltpu.VMEM((2, D, D), BF16),
            pltpu.SemaphoreType.DMA((2,)),
        ],
        compiler_params=PARAMS,
        cost_estimate=cost(18 * parts * frames * places * D * D),
        name="space_weights",
    )(*ins, *projs, *outs)


def small_kernel(count, *refs):
    rows, (out_ref, table) = refs[:count], refs[count:]
    table[...] = jnp.zeros_like(table)
    at = 0
    for ref in rows:
        table[at : at + ref.shape[0], :] = ref[...]
        at += ref.shape[0]
    out_ref[...] = jnp.swapaxes(table[...], 0, 1)


def as_columns(rows):
    return pl.pallas_call(
        functools.partial(small_kernel, len(rows)),
        out_shape=jax.ShapeDtypeStruct((D, SMALL), F32),
        scratch_shapes=[pltpu.VMEM((SMALL, D), F32)],
        name="as_columns",
    )(*rows)


def input_kernel(clip, g_ref, p_ref, x_ref, table, w_ref, *refs):
    out_ref, rows_ref = refs[-2:]
    clear(pl.program_id(0) == 0, rows_ref)
    back = dot_nt(p_ref[0], w_ref[...])
    hat, inverse = normalize(x_ref[0, 0].astype(F32))
    rows_ref[...] += jnp.concatenate([column_sum(back * hat), column_sum(back)], 0)
    grad = g_ref[0].astype(F32) + normalize_back(back, hat, inverse, table[GAIN : GAIN + 1, :])
    out_ref[0, 0] = grad.astype(BF16)


def input_grads(clip, grad, proj, inputs, table, weights, before):
    frames, places, _ = grad.shape
    frame = pl.BlockSpec((1, places, D), lambda i, c: (i, 0, 0))
    block = pl.BlockSpec((1, 1, places, D), lambda i, c: (c[0], i, 0, 0))
    more = [] if before is None else [before]
    return pl.pallas_call(
        input_kernel,
        grid_spec=pltpu.PrefetchScalarGridSpec(
            num_scalar_prefetch=1,
            grid=(frames,),
            in_specs=[
                frame,
                pl.BlockSpec((1, places, 3 * D), lambda i, c: (i, 0, 0)),
                block,
                fixed(table.shape),
                columns_of(3 * D, 0),
            ]
            + [pl.BlockSpec(memory_space=pl.ANY) for _ in more],
            out_specs=[block, fixed((2, D))],
        ),
        out_shape=[jax.ShapeDtypeStruct(inputs.shape, BF16), jax.ShapeDtypeStruct((2, D), F32)],
        input_output_aliases={6: 0} if more else {},
        compiler_params=PARAMS,
        cost_estimate=cost(18 * frames * places * D * D),
        name="input_grads",
    )(clip, grad, proj, inputs, table, weights, *more)


def place_kernel(order, *refs):
    blocks, out_ref = refs[:-1], refs[-1]
    for n, ref in enumerate(blocks):

        @pl.when(pl.program_id(0) == n)
        def _():
            out_ref[0] = ref[...]


def place_clips(order, blocks):
    shape = blocks[0].shape
    return pl.pallas_call(
        place_kernel,
        grid_spec=pltpu.PrefetchScalarGridSpec(
            num_scalar_prefetch=1,
            grid=(len(blocks),),
            in_specs=[fixed(shape)] * len(blocks),
            out_specs=pl.BlockSpec((1,) + shape, lambda i, order: (order[i], 0, 0, 0)),
        ),
        out_shape=jax.ShapeDtypeStruct((len(blocks),) + shape, BF16),
        compiler_params=PARAMS,
        name="place_clips",
    )(order, *blocks)


AXES = ("clip", "frame")
MESH = pl.DeviceIdType.MESH


def position():
    clip, frame = lax.axis_index("clip"), lax.axis_index("frame")
    return clip // 2, clip % 2, frame // 2, frame % 2


def device(z, x, y, core):
    return (2 * z + x, 2 * y + core)


def greet(partners):
    barrier = pltpu.get_barrier_semaphore()
    for partner in partners:
        pl.semaphore_signal(barrier, inc=1, device_id=partner, device_id_type=MESH)
    pl.semaphore_wait(barrier, len(partners))


def neighbours(depth, height):
    z, x, y, core = position()
    return (
        [device(lax.rem(z + d, depth), x, y, core) for d in range(1, depth)]
        + [device(z, x, lax.rem(y + d, height), core) for d in range(1, height)]
        + [device(z, 1 - x, y, core), device(z, x, y, 1 - core)]
    )


def gather_kernel(depth, height, in_ref, out_ref, local, y_send, y_recv, z_send, z_recv, x_send, x_recv, c_send, c_recv):
    z, x, y, core = position()
    greet(neighbours(depth, height))

    def send(source, target, sems, slot, index, to):
        copy = pltpu.make_async_remote_copy(
            src_ref=source, dst_ref=target, send_sem=sems[0].at[slot], recv_sem=sems[1].at[index],
            device_id=to, device_id_type=MESH,
        )
        copy.start()
        return copy

    def block(zz, xx, cc):
        return out_ref.at[2 * zz + xx, :, cc]

    def arrival(ref, sem):
        return pltpu.make_async_remote_copy(
            src_ref=ref, dst_ref=ref, send_sem=sem, recv_sem=sem, device_id=device(z, 1 - x, y, core), device_id_type=MESH
        )

    sent = []
    own = out_ref.at[2 * z + x, y, core]
    for d in range(1, height):
        sent.append(send(in_ref, own, (y_send, y_recv), d - 1, y, device(z, x, lax.rem(y + d, height), core)))
    mine = pltpu.make_async_copy(in_ref, own, local)
    mine.start()
    mine.wait()
    for d in range(1, height):
        other = lax.rem(y + height - d, height)
        arrival(out_ref.at[2 * z + x, other, core], y_recv.at[other]).wait_recv()
    here = block(z, x, core)
    for d in range(1, depth):
        sent.append(send(here, here, (z_send, z_recv), d - 1, z, device(lax.rem(z + d, depth), x, y, core)))

    def to_x(step, zz):
        sent.append(send(block(zz, x, core), block(zz, x, core), (x_send, x_recv), step, zz, device(z, 1 - x, y, core)))

    def to_core(step, zz, xx):
        sent.append(
            send(block(zz, xx, core), block(zz, xx, core), (c_send, c_recv), step, 2 * zz + xx, device(z, x, y, 1 - core))
        )

    to_x(0, z)
    to_core(0, z, x)
    for d in range(1, depth):
        zz = lax.rem(z + depth - d, depth)
        arrival(block(zz, x, core), z_recv.at[zz]).wait_recv()
        to_x(d, zz)
        to_core(d, zz, x)
    for d in range(depth):
        zz = lax.rem(z + depth - d, depth)
        arrival(block(zz, 1 - x, core), x_recv.at[zz]).wait_recv()
        to_core(depth + d, zz, 1 - x)
    for d in range(depth):
        zz = lax.rem(z + depth - d, depth)
        arrival(block(zz, x, 1 - core), c_recv.at[2 * zz + x]).wait_recv()
        arrival(block(zz, 1 - x, 1 - core), c_recv.at[2 * zz + 1 - x]).wait_recv()
    for copy in sent:
        copy.wait_send()


def gather_rows(block):
    clips, frames = lax.axis_size("clip"), lax.axis_size("frame")
    depth, height = clips // 2, frames // 2
    sems = pltpu.SemaphoreType.DMA
    out = pl.pallas_call(
        functools.partial(gather_kernel, depth, height),
        in_specs=[pl.BlockSpec(memory_space=pl.ANY)],
        out_specs=pl.BlockSpec(memory_space=pl.ANY),
        out_shape=jax.ShapeDtypeStruct((clips, height, 2) + block.shape, block.dtype),
        scratch_shapes=[
            sems,
            sems((max(height - 1, 1),)), sems((height,)),
            sems((depth - 1,)), sems((depth,)),
            sems((depth,)), sems((depth,)),
            sems((clips,)), sems((clips,)),
        ],
        compiler_params=pltpu.CompilerParams(collective_id=0, has_side_effects=True),
        name="gather_rows",
    )(block)
    return out.reshape(-1, block.shape[1])


def reduce_kernel(depth, height, part_ref, small_ref, out_ref, out_small, *refs):
    own, from_core, to_x, from_x, to_z, from_z, to_y, from_y = refs[:8]
    low_core, low_to_x, low_x, low_to_z, low_z, low_to_y, low_y = refs[8:15]
    c_send, c_recv, x_send, x_recv, z_send, z_recv, y_send, y_recv = refs[15:23]
    lc_send, lc_recv, lx_send, lx_recv, lz_send, lz_recv, ly_send, ly_recv, local = refs[23:]
    z, x, y, core = position()
    greet(neighbours(depth, height))

    def remote(source, target, send_sem, recv_sem, to):
        return pltpu.make_async_remote_copy(
            src_ref=source, dst_ref=target, send_sem=send_sem, recv_sem=recv_sem, device_id=to, device_id_type=MESH
        )

    def away(d):
        return lax.rem(z + d, depth)

    order = list(range(1, depth)) + [0]
    core_device, x_device = device(z, x, y, 1 - core), device(z, 1 - x, y, core)
    sent = []

    def start(copy):
        copy.start()
        sent.append(copy)
        return copy

    low_c = start(remote(small_ref.at[:, :, 1 - core], low_core, lc_send, lc_recv, core_device))
    c_copies, mine = [], []
    for side in range(2):
        xx = (1 - x) if side == 0 else x
        for d in order:
            slot, block = side * depth + d, 2 * away(d) + xx
            c_copies.append(
                start(
                    remote(
                        part_ref.at[block, :, 1 - core], from_core.at[slot],
                        c_send.at[slot], c_recv.at[slot], core_device,
                    )
                )
            )
            mine.append(pltpu.make_async_copy(part_ref.at[block, :, core], own.at[slot], local.at[slot]))
            mine[-1].start()

    def pair_sum(slot):
        return own[slot].astype(F32) + from_core[slot].astype(F32)

    x_copies = []
    for n, d in enumerate(order):
        mine[n].wait()
        c_copies[n].wait_recv()
        to_x[d] = pair_sum(d).astype(BF16)
        x_copies.append(start(remote(to_x.at[d], from_x.at[d], x_send.at[d], x_recv.at[d], x_device)))
    low_c.wait_recv()
    for zz in range(depth):
        low_to_x[zz] = small_ref[2 * zz + 1 - x, :, core] + low_core[2 * zz + 1 - x]
    low_xc = start(remote(low_to_x, low_x, lx_send, lx_recv, x_device))
    for n, d in enumerate(order):
        mine[depth + n].wait()
        c_copies[depth + n].wait_recv()
        x_copies[n].wait_recv()
        total = pair_sum(depth + d) + from_x[d].astype(F32)
        if d:
            to_z[d] = total.astype(BF16)
            start(remote(to_z.at[d], from_z.at[z], z_send.at[d], z_recv.at[z], device(away(d), x, y, core)))
        else:
            from_z[z] = total.astype(BF16)
    low_xc.wait_recv()
    for d in order:
        block = 2 * away(d) + x
        total = small_ref[block, :, core] + low_core[block] + low_x[away(d)]
        if d:
            low_to_z[d] = total
            start(remote(low_to_z.at[d], low_z.at[z], lz_send.at[d], lz_recv.at[z], device(away(d), x, y, core)))
        else:
            low_z[z] = total
    for d in range(1, depth):
        zz, to = lax.rem(z + depth - d, depth), device(away(d), x, y, core)
        remote(to_z.at[d], from_z.at[zz], z_send.at[d], z_recv.at[zz], to).wait_recv()
        remote(low_to_z.at[d], low_z.at[zz], lz_send.at[d], lz_recv.at[zz], to).wait_recv()

    def over(ref, *row):
        total = ref[(0,) + row].astype(F32)
        for n in range(1, ref.shape[0]):
            total = total + ref[(n,) + row].astype(F32)
        return total

    for d in range(1, height):
        other = lax.rem(y + d, height)
        to = device(z, x, other, core)
        to_y[d] = over(from_z, other).astype(BF16)
        start(remote(to_y.at[d], from_y.at[y], y_send.at[d], y_recv.at[y], to))
        low_to_y[d] = over(low_z, other)
        start(remote(low_to_y.at[d], low_y.at[y], ly_send.at[d], ly_recv.at[y], to))
    from_y[y] = over(from_z, y).astype(BF16)
    low_y[y] = over(low_z, y)
    for d in range(1, height):
        yy, to = lax.rem(y + height - d, height), device(z, x, lax.rem(y + d, height), core)
        remote(to_y.at[d], from_y.at[yy], y_send.at[d], y_recv.at[yy], to).wait_recv()
        remote(low_to_y.at[d], low_y.at[yy], ly_send.at[d], ly_recv.at[yy], to).wait_recv()
    out_ref[...] = over(from_y)
    out_small[...] = over(low_y)
    for copy in sent:
        copy.wait_send()


def reduce_rows(block, small):
    clips, frames = lax.axis_size("clip"), lax.axis_size("frame")
    depth, height = clips // 2, frames // 2
    rows = block.shape[0] // (clips * frames)
    sems, tail, low = pltpu.SemaphoreType.DMA, (rows, block.shape[1]), (rows, small.shape[1])
    lead = (clips, height, 2)
    return pl.pallas_call(
        functools.partial(reduce_kernel, depth, height),
        in_specs=[pl.BlockSpec(memory_space=pl.ANY), pl.BlockSpec(memory_space=pltpu.VMEM)],
        out_specs=[pl.BlockSpec(memory_space=pltpu.VMEM)] * 2,
        out_shape=[jax.ShapeDtypeStruct(tail, F32), jax.ShapeDtypeStruct(low, F32)],
        scratch_shapes=[
            pltpu.VMEM((2 * depth, height) + tail, BF16),
            pltpu.VMEM((2 * depth, height) + tail, BF16),
            pltpu.VMEM((depth, height) + tail, BF16),
            pltpu.VMEM((depth, height) + tail, BF16),
            pltpu.VMEM((depth, height) + tail, BF16),
            pltpu.VMEM((depth, height) + tail, BF16),
            pltpu.VMEM((height,) + tail, BF16),
            pltpu.VMEM((height,) + tail, BF16),
            pltpu.VMEM((clips, height) + low, F32),
            pltpu.VMEM((depth, height) + low, F32),
            pltpu.VMEM((depth, height) + low, F32),
            pltpu.VMEM((depth, height) + low, F32),
            pltpu.VMEM((depth, height) + low, F32),
            pltpu.VMEM((height,) + low, F32),
            pltpu.VMEM((height,) + low, F32),
            sems((2 * depth,)), sems((2 * depth,)),
            sems((depth,)), sems((depth,)),
            sems((depth,)), sems((depth,)),
            sems((height,)), sems((height,)),
            sems, sems,
            sems, sems,
            sems((depth,)), sems((depth,)),
            sems((height,)), sems((height,)),
            sems((2 * depth,)),
        ],
        compiler_params=pltpu.CompilerParams(
            collective_id=1, has_side_effects=True, vmem_limit_bytes=60 << 20
        ),
        name="reduce_rows",
    )(block.reshape(lead + tail), small.reshape(lead + low))


def gather(block):
    return lax.all_gather(block, AXES, axis=0, tiled=True)


def scatter(block):
    return lax.psum_scatter(block, AXES, scatter_dimension=0, tiled=True)


def shards(
    clips_in, teacher, valid, norm_gain, norm_shift, w_space, qv_bias, w_space_out, mix_bias,
    w_time, w_time_out, w_up, up_bias, w_down,
):
    batch, frames, places, _ = clips_in.shape
    ring = lax.axis_size("frame")
    pieces = ring // batch
    chunk = places // pieces
    all_frames = ring * frames
    me = lax.axis_index("frame")
    depth = w_up.shape[0]

    def swap(block, step):
        if step == 0:
            return block
        return lax.ppermute(block, "frame", [(i, i ^ step) for i in range(ring)])

    def clip_of(step):
        return (me // pieces) ^ (step // pieces)

    def place_of(step):
        return ((me % pieces) ^ (step % pieces)) * chunk

    def cut(block, step):
        if pieces == 1:
            return block
        return lax.dynamic_slice_in_dim(block, place_of(step), chunk, 0)

    def spread(block):
        got = []
        for step in range(ring):
            mine = lax.dynamic_index_in_dim(block, clip_of(step), 0, keepdims=False)
            got.append(swap(cut(jnp.swapaxes(mine, 0, 1), step), step))
        return got

    many = FF // D
    count = jnp.sum(valid)
    counts = jnp.stack([count // 256, count % 256]).astype(BF16)
    smalls = jnp.concatenate(
        [
            norm_gain, norm_shift, qv_bias, mix_bias, up_bias.reshape(depth, many),
            jnp.broadcast_to(counts[None], (depth, 2)),
        ],
        1,
    )
    smalls = jnp.pad(smalls, ((0, 0), (0, SMALL - smalls.shape[1])))
    first = gather_rows(jnp.concatenate([w_space, w_space_out, smalls], 1))
    up_turned = jnp.swapaxes(w_up.reshape(depth, D, many), 1, 2).reshape(depth, FF)
    rest = gather(jnp.concatenate([w_time, w_time_out, up_turned, w_down.reshape(depth, FF)], 1))
    table = jnp.swapaxes(first[:, 4 * D : 4 * D + 24].astype(F32), 0, 1)
    up_row = table[UP : UP + many].reshape(1, FF)
    counted = table[UP + many : UP + many + 2, ::depth]
    total_count = jnp.sum(counted[0]) * 256.0 + jnp.sum(counted[1])
    scale = (2.0 / (total_count * D)).reshape(1, 1)
    table = table[:16]

    order = [((me // pieces) ^ j).astype(jnp.int32) for j in range(batch)]
    clip_ids = [jnp.reshape(c, (1,)) for c in order]
    valid_column = jnp.concatenate(spread(valid), 1).reshape(-1, 1).astype(F32)
    saved, sent = [None] * batch, [None] * ring
    for j in list(range(batch))[::-1]:
        *kept_j, after = space_forward(clip_ids[j], clips_in, table, first)
        saved[j] = kept_j
        after = jnp.swapaxes(after, 0, 1)
        for r in range(pieces):
            step = j * pieces + r
            sent[step] = swap(cut(after, step), step)
        if j == batch // 2:
            teacher, after = lax.optimization_barrier((teacher, after))

    teachers = spread(teacher)
    *saved_b, after_b = time_forward(sent, table, rest)
    tile, _ = time_tiles(chunk, all_frames)
    layer_parts, grad_b, d_feed, rows_c, bias_up, squares = feed_forward(
        after_b, teachers, valid_column, scale, table, up_row, rest, tile
    )
    squares = jnp.broadcast_to(jnp.sum(squares).reshape(1, 1), (1, D))
    grad_parts, d_rest, rows_b = time_back(grad_b, saved_b, sent, table, rest, d_feed)
    d_rest = scatter(d_rest)
    d_time, d_feed = d_rest[:, : 4 * D], d_rest[:, 4 * D :]
    grad_parts = [swap(part, step) for step, part in enumerate(grad_parts)]
    grad_parts[-1], layer_parts = lax.optimization_barrier((grad_parts[-1], layer_parts))
    layer_parts = [swap(part, step) for step, part in enumerate(layer_parts)]

    def join(parts, j):
        if pieces == 1:
            return parts[j]
        whole = jnp.zeros((places, frames, D), BF16)
        for r in range(pieces):
            step = j * pieces + r
            whole = lax.dynamic_update_slice_in_dim(whole, parts[step], place_of(step), 0)
        return whole

    projs, outs, biases, rows_a, input_grad = [], [], [], [], None
    for j in range(batch):
        grad = jnp.swapaxes(join(grad_parts, j), 0, 1)
        proj, d_out, bias = space_back(grad, saved[j][1:], first)
        projs.append(proj)
        outs.append(d_out)
        biases.append(bias)
        input_grad, rows = input_grads(clip_ids[j], grad, proj, clips_in, table, first, input_grad)
        rows_a.append(rows)
    d_space, sums_a = space_weights([kept_j[0] for kept_j in saved], projs, outs)
    rows_a, biases = sum(rows_a), sum(biases)
    columns = as_columns(
        [
            rows_a[0:1], rows_b[0:1], rows_c[0:1],
            rows_a[1:2], rows_b[1:2], rows_c[1:2],
            sums_a[:, :D], sums_a[:, 2 * D :], rows_b[3:4], rows_b[2:3],
            biases, rows_b[4:5], rows_c[2:3],
            bias_up.reshape(many, D), squares,
        ]
    )
    d_space, here = reduce_rows(d_space, columns)
    layer_out = place_clips(jnp.stack(order), [join(layer_parts, j) for j in range(batch)])
    d_up = jnp.swapaxes(d_feed[:, :FF].reshape(depth, many, D), 1, 2).reshape(depth, FF)
    return (
        jnp.swapaxes(layer_out, 1, 2),
        here[0, 13 + many] / (total_count * D),
        input_grad,
        here[:, 0:3],
        here[:, 3:6],
        d_space[:, : 3 * D],
        here[:, 6:9],
        here[:, 9],
        d_space[:, 3 * D : 4 * D],
        here[:, 10:13],
        d_time[:, : 3 * D].astype(F32),
        d_time[:, 3 * D :].astype(F32),
        d_up.astype(F32),
        here[:, 13 : 13 + many].reshape(-1),
        d_feed[:, FF:].reshape(-1, D).astype(F32),
    )


def solution(mesh):
    tokens, rows = P("clip", "frame", None, None), P(AXES, None)
    in_specs = (tokens, tokens, P("clip", "frame", None)) + (rows,) * 9 + (P(AXES), rows)
    out_specs = (
        (tokens, P(), tokens, rows, rows, rows, rows, P(AXES)) + (rows,) * 5 + (P(AXES), rows)
    )
    return jax.shard_map(shards, mesh=mesh, in_specs=in_specs, out_specs=out_specs, check_vma=False)
```

time: 989 us -> 698 us (0.71)
  waiting for transfers between devices: 126 us -> 31 us
  Pallas kernels: 645 us -> 561 us
  blocking collectives: 62.8 us -> 0 us
  local copies, waits for them, and re-layouts: 92.5 us -> 58.8 us
  other arithmetic: 26.1 us -> 11.1 us
    psum x1 -> x0, blocking collectives: 62.8 us -> none  [shards(): small = lax.psum(small, AXES)]
    all_gather x3 -> x1, waiting for transfers between devices: 61.4 us -> 0.02 us  [gather(): return lax.all_gather(block, AXES, axis=0, tiled=True)]
    pallas_call x4, Pallas kernels: 104 us -> 52.7 us  [space_back(): pl.pallas_call(space_back_kernel, grid=(frames,), in_specs=[frame(places,...]
    ppermute x15, waiting for transfers between devices: 63.5 us -> 31 us  [swap(): return lax.ppermute(block, 'frame', [(i, i ^ step) for i in range(ring)])]
    pallas_call x5 -> x12, Pallas kernels: 479 us -> 454 us  [the longest x1 140 us: feed_forward(): pl.pallas_call(functools.partial(feed_kernel, ring), grid=(tokens // tile...]
    reshape x6 -> x4, local copies, waits for them, and re-layouts: 20.8 us -> 2.35 us  [the longest x1 1.04 us: shards(): w_down.reshape(depth, FF)]
    pallas_call x1 -> x6, local copies, waits for them, and re-layouts: 0.51 us -> 11.8 us  [the longest x4 8.83 us: space_forward(): pl.pallas_call(space_kernel, grid_spec=pltpu.PrefetchScalarGridSpec(num_s...]
    dynamic_update_slice x4 -> x0, local copies, waits for them, and re-layouts: 10.9 us -> none  [shards(): lax.dynamic_update_index_in_dim(layer_out, join(layer_parts, j), order[j]...]
  transfers between devices with their start and end apart: 22 -> 17, of which waited for: 5 -> 3; matrix products, arithmetic and copies ran while one was open for 11% -> 8% of each run, Pallas kernels for 47% -> 51%
where the time goes in v2:
time: 698 us; the launch traced here: 694 us
  Pallas kernels  561 us (80%)
  local copies, waits for them, and re-layouts  58.8 us (8%)
  waiting for transfers between devices  31 us (4%)
  between operations  20.7 us (3%)
  starting transfers between devices  11.4 us (2%)
  other arithmetic  11.1 us (2%)
    pallas_call x1, Pallas kernels, feed_forward(): pl.pallas_call(functools.partial(feed_kernel, ring), grid=(tokens // tile...  140 us
    pallas_call x1, Pallas kernels, time_back(): pl.pallas_call(functools.partial(time_back_kernel, group, ring), grid=(to...  69.4 us
    pallas_call x1, Pallas kernels, gather_rows(): pl.pallas_call(functools.partial(gather_kernel, depth, height), in_specs=...  67.6 us
    pallas_call x1, Pallas kernels, reduce_rows(): pl.pallas_call(functools.partial(reduce_kernel, depth, height), in_specs=...  56.8 us
    pallas_call x4, Pallas kernels, space_forward(): pl.pallas_call(space_kernel, grid_spec=pltpu.PrefetchScalarGridSpec(num_s...  54.3 us
    pallas_call x4, Pallas kernels, space_back(): pl.pallas_call(space_back_kernel, grid=(frames,), in_specs=[frame(places,...  52.7 us
    pallas_call x1, Pallas kernels, time_forward(): pl.pallas_call(functools.partial(time_kernel, frames, group, len(parts)),...  42.7 us
    pallas_call x4, Pallas kernels, input_grads(): pl.pallas_call(input_kernel, grid_spec=pltpu.PrefetchScalarGridSpec(num_s...  39 us
  transfers between devices with their start and end apart: 17, of which 3 were waited for; matrix products, arithmetic and copies ran while one was open for 8% of the time, Pallas kernels for 51%

profile of v2, /device:TPU:0, one launch (start us, length us, event | category | flops | bytes accessed | tf_op | source)
XLA Modules:
  0.0 694.2 jit_solution(16781583535170659555)
XLA Ops:
  7.2 1.0 reshape.117
  8.3 1.3 copy.130
  10.3 0.8 pad_maximum_fusion
  11.7 2.6 collective-permute-start.8
  19.0 67.6 %gather_rows.1 = bf16[8,2,2,24,3200]{4,3,2,1,0:T(8,128)(2,1)} custom-call(bf16[24,3200]{1,0:T(8,128)(2,1)} %fusion.1.in_ref), custom_call_target="tpu_custom_call" | custom-call | tf_op jit(solution)/shard_map/gather_rows/pallas_call | solution.py:765
  86.6 1.0 convert_bitcast_fusion
  87.6 0.8 copy.119.table.refs_4_.refs_7_.refs_8_
  88.3 5.3 copy.118.x_ref
  93.6 13.6 %space_forward.7 = (bf16[4,196,768]{2,1,0:T(8,128)(2,1)}, bf16[4,196,768]{2,1,0:T(8,128)(2,1)}, bf16[4,196,768]{2,1,0:T(8,128)(2,1)}, bf16[4,196,768]{2,1,0:T(8,...) custom-call(s32[1]{0:T(128)} %bitcast.3.clip, ...), custom_call_target="tpu_custom_call" | custom-call | flops 11098128384 | tf_op jit(solution)/shard_map/space_forward/pallas_call | solution.py:215
  107.2 1.8 copy.171
  109.0 0.8 collective-permute-start.5
  109.8 13.4 %space_forward.6 = (bf16[4,196,768]{2,1,0:T(8,128)(2,1)}, bf16[4,196,768]{2,1,0:T(8,128)(2,1)}, bf16[4,196,768]{2,1,0:T(8,128)(2,1)}, bf16[4,196,768]{2,1,0:T(8,...) custom-call(s32[1]{0:T(128)} %bitcast.1.clip, ...), custom_call_target="tpu_custom_call" | custom-call | flops 11098128384 | tf_op jit(solution)/shard_map/space_forward/pallas_call | solution.py:215
  123.2 2.8 copy.172
  126.2 13.4 %space_forward.4 = (bf16[4,196,768]{2,1,0:T(8,128)(2,1)}, bf16[4,196,768]{2,1,0:T(8,128)(2,1)}, bf16[4,196,768]{2,1,0:T(8,128)(2,1)}, bf16[4,196,768]{2,1,0:T(8,...) custom-call(s32[1]{0:T(128)} %bitcast.2.clip, ...), custom_call_target="tpu_custom_call" | custom-call | flops 11098128384 | tf_op jit(solution)/shard_map/space_forward/pallas_call | solution.py:215
  139.6 2.8 copy.174
  142.4 1.2 collective-permute-start.4
  143.6 13.8 %space_forward.5 = (bf16[4,196,768]{2,1,0:T(8,128)(2,1)}, bf16[4,196,768]{2,1,0:T(8,128)(2,1)}, bf16[4,196,768]{2,1,0:T(8,128)(2,1)}, bf16[4,196,768]{2,1,0:T(8,...) custom-call(s32[1]{0:T(128)} %bitcast.clip, ...), custom_call_target="tpu_custom_call" | custom-call | flops 11098128384 | tf_op jit(solution)/shard_map/space_forward/pallas_call | solution.py:215
  157.4 5.9 dynamic-slice_bitcast_fusion
  163.4 0.9 collective-permute-start.7
  164.3 0.7 slice_reduce_fusion
  165.9 1.5 copy.173
  168.8 0.8 collective-permute-start.2
  169.6 6.1 collective-permute-done.7
  176.1 2.0 convert_element_type.51.refs_5_
  178.2 42.7 %time_forward.1 = (bf16[3136,768]{1,0:T(8,128)(2,1)}, bf16[3136,768]{1,0:T(8,128)(2,1)}, bf16[3136,768]{1,0:T(8,128)(2,1)}, bf16[3136,768]{1,0:T(8,128)(2,1)}, b...) custom-call(bf16[196,4,768]{2,1,0:T(4,128)(2,1)} %bitcast.110, ...), custom_call_target="tpu_custom_call" | custom-call | flops 44392513536 | tf_op jit(solution)/shard_map/time_forward/pallas_call | solution.py:284
  220.9 6.3 collective-permute-done.1.refs_2_
  227.2 1.1 copy-done.25
  228.3 140.1 %feed_forward.1 = (bf16[196,4,768]{2,1,0:T(4,128)(2,1)}, bf16[196,4,768]{2,1,0:T(4,128)(2,1)}, bf16[196,4,768]{2,1,0:T(4,128)(2,1)}, bf16[196,4,768]{2,1,0:T(4,1...) custom-call(bf16[196,4,768]{2,1,0:T(4,128)(2,1)} %get-tuple-element., ...), custom_call_target="tpu_custom_call" | custom-call | flops 147975045120 | tf_op jit(solution)/shard_map/feed_forward/pallas_call | solution.py:375
  368.5 69.4 %time_back.1 = (bf16[196,4,768]{2,1,0:T(4,128)(2,1)}, bf16[196,4,768]{2,1,0:T(4,128)(2,1)}, bf16[196,4,768]{2,1,0:T(4,128)(2,1)}, bf16[196,4,768]{2,1,0:T(4,128)...) custom-call(f32[3136,768]{1,0:T(8,128)} %get-tuple-element.102.refs_0_, ...), custom_call_target="tpu_custom_call", output_to_operand_aliasing={{4}: (10, {})} | custom-call | flops 77686898688 | tf_op jit(solution)/shard_map/time_back/pallas_call | solution.py:465
  439.0 1.7 collective-permute-start.14
  440.7 2.4 copy.170
  443.2 13.1 %space_back.4 = (bf16[4,196,2304]{2,1,0:T(8,128)(2,1)}, f32[768,768]{1,0:T(8,128)}, f32[1,768]{1,0:T(1,128)}) custom-call(bf16[4,196,768]{2,1,0:T(8,128)(2,1)} %bitcast.103, bf16[4,196,768]{2,1,0:T(8,128)(2,1)} %get-tuple-element.125.q_ref, bf16[4,196,768]{2,1,0:T(8,128)(2,1)} %get-tuple-element.126.k_ref, bf16[4,196,768]{2,1,0:T(8,128)(2,1)} %get-tuple-element.127.v_ref, ...), custom_call_target="tpu_custom_call" | custom-call | flops 11098128384 | tf_op jit(solution)/shard_map/space_back/pallas_call | solution.py:512
  456.8 0.7 reduce.7
  459.3 10.1 %input_grads.4 = (bf16[4,4,196,768]{3,2,1,0:T(8,128)(2,1)}, f32[2,768]{1,0:T(2,128)}) custom-call(s32[1]{0:T(128)} %bitcast.clip, bf16[4,196,768]{2,1,0:T(8,128)(2,1)} %bitcast.104, bf16[4,196,2304]{2,1,0:T(8,128)(2,1)} %get-tuple-element.130.refs_4_.p_ref, bf16[4,4,196,768]{3,2,1,0:T(8,128)(2,1)} %copy.118.x_ref, ...), custom_call_target="tpu_custom_call" | custom-call | flops 8323596288 | tf_op jit(solution)/shard_map/input_grads/pallas_call | solution.py:623
  469.9 1.4 collective-permute-start.12
  471.3 2.6 copy.167
  473.8 1.2 copy.169
  475.0 18.5 %collective-permute-done.14 = bf16[196,4,768]{2,1,0:T(4,128)(2,1)S(1)} collective-permute-done((bf16[196,4,768]{2,1,0:T(4,128)(2,1)}, bf16[196,4,768]{2,1,0:T(4,128)(2,1)S(1)}, u32[]{:S(2)}, u32[]{:S(2)}) %collective-permute-start.14) | collective-permute-done | bytes 1204256 | tf_op jit(solution)/shard_map/ppermute | solution.py:954
  493.5 1.2 copy.168
  494.7 13.5 %space_back.5 = (bf16[4,196,2304]{2,1,0:T(8,128)(2,1)}, f32[768,768]{1,0:T(8,128)}, f32[1,768]{1,0:T(1,128)}) custom-call(bf16[4,196,768]{2,1,0:T(8,128)(2,1)} %bitcast.107, bf16[4,196,768]{2,1,0:T(8,128)(2,1)} %get-tuple-element.132.q_ref, bf16[4,196,768]{2,1,0:T(8,128)(2,1)} %get-tuple-element.133.k_ref, bf16[4,196,768]{2,1,0:T(8,128)(2,1)} %get-tuple-element.134.v_ref, ...), custom_call_target="tpu_custom_call" | custom-call | flops 11098128384 | tf_op jit(solution)/shard_map/space_back/pallas_call | solution.py:512
  508.2 9.5 %input_grads.5 = (bf16[4,4,196,768]{3,2,1,0:T(8,128)(2,1)}, f32[2,768]{1,0:T(2,128)}) custom-call(s32[1]{0:T(128)} %bitcast.1.clip, bf16[4,196,768]{2,1,0:T(8,128)(2,1)} %bitcast.108, bf16[4,196,2304]{2,1,0:T(8,128)(2,1)} %get-tuple-element.137.refs_5_.p_ref, bf16[4,4,196,768]{3,2,1,0:T(8,128)(2,1)} %copy.118.x_ref, ...), custom_call_target="tpu_custom_call", output_to_operand_aliasing={{0}: (6, {})} | custom-call | flops 8323596288 | tf_op jit(solution)/shard_map/input_grads/pallas_call | solution.py:623
  517.7 12.9 %space_back.6 = (bf16[4,196,2304]{2,1,0:T(8,128)(2,1)}, f32[768,768]{1,0:T(8,128)}, f32[1,768]{1,0:T(1,128)}) custom-call(bf16[4,196,768]{2,1,0:T(8,128)(2,1)} %bitcast.105, bf16[4,196,768]{2,1,0:T(8,128)(2,1)} %get-tuple-element.139.q_ref, bf16[4,196,768]{2,1,0:T(8,128)(2,1)} %get-tuple-element.140.k_ref, bf16[4,196,768]{2,1,0:T(8,128)(2,1)} %get-tuple-element.141.v_ref, ...), custom_call_target="tpu_custom_call" | custom-call | flops 11098128384 | tf_op jit(solution)/shard_map/space_back/pallas_call | solution.py:512
  530.7 9.6 %input_grads.6 = (bf16[4,4,196,768]{3,2,1,0:T(8,128)(2,1)}, f32[2,768]{1,0:T(2,128)}) custom-call(s32[1]{0:T(128)} %bitcast.2.clip, bf16[4,196,768]{2,1,0:T(8,128)(2,1)} %bitcast.106, bf16[4,196,2304]{2,1,0:T(8,128)(2,1)} %get-tuple-element.144.refs_6_.p_ref, bf16[4,4,196,768]{3,2,1,0:T(8,128)(2,1)} %copy.118.x_ref, ...), custom_call_target="tpu_custom_call", output_to_operand_aliasing={{0}: (6, {})} | custom-call | flops 8323596288 | tf_op jit(solution)/shard_map/input_grads/pallas_call | solution.py:623
  540.3 13.2 %space_back.7 = (bf16[4,196,2304]{2,1,0:T(8,128)(2,1)}, f32[768,768]{1,0:T(8,128)}, f32[1,768]{1,0:T(1,128)}) custom-call(bf16[4,196,768]{2,1,0:T(8,128)(2,1)} %bitcast.101, bf16[4,196,768]{2,1,0:T(8,128)(2,1)} %get-tuple-element.146.q_ref, bf16[4,196,768]{2,1,0:T(8,128)(2,1)} %get-tuple-element.147.k_ref, bf16[4,196,768]{2,1,0:T(8,128)(2,1)} %get-tuple-element.148.v_ref, ...), custom_call_target="tpu_custom_call" | custom-call | flops 11098128384 | tf_op jit(solution)/shard_map/space_back/pallas_call | solution.py:512
  553.4 31.2 %space_weights.1 = (bf16[768,3072]{1,0:T(8,128)(2,1)}, f32[1,2304]{1,0:T(1,128)}) custom-call(bf16[4,196,768]{2,1,0:T(8,128)(2,1)} %get-tuple-element.120.refs_0_, bf16[4,196,768]{2,1,0:T(8,128)(2,1)} %get-tuple-element.121.refs_1_, bf16[4,196,768]{2,1,0:T(8,128)(2,1)} %get-tuple-element.122.refs_2_, bf16[4,196,768]{2,1,0:T(8,128)(2,1)} %get-tuple-element.123.refs_3_, ...), custom_call_target="tpu_custom_call" | custom-call | flops 33294385152 | tf_op jit(solution)/shard_map/space_weights/pallas_call | solution.py:566
  584.8 9.8 %input_grads.7 = (bf16[4,4,196,768]{3,2,1,0:T(8,128)(2,1)}, f32[2,768]{1,0:T(2,128)}) custom-call(s32[1]{0:T(128)} %bitcast.3.clip, bf16[4,196,768]{2,1,0:T(8,128)(2,1)} %bitcast.102, bf16[4,196,2304]{2,1,0:T(8,128)(2,1)} %get-tuple-element.151.refs_7_.p_ref, bf16[4,4,196,768]{3,2,1,0:T(8,128)(2,1)} %copy.118.x_ref, ...), custom_call_target="tpu_custom_call", output_to_operand_aliasing={{0}: (6, {})} | custom-call | flops 8323596288 | tf_op jit(solution)/shard_map/input_grads/pallas_call | solution.py:623
  594.6 0.7 add_add_fusion
  596.5 1.2 broadcast_in_dim.5.refs_14_
  597.7 1.7 as_columns.1
  599.4 56.8 %reduce_rows.1 = (f32[24,3072]{1,0:T(8,128)}, f32[24,128]{1,0:T(8,128)}) custom-call(bf16[8,2,2,24,3072]{4,3,2,1,0:T(8,128)(2,1)} %bitcast.97, f32[8,2,2,24,128]{4,3,2,1,0:T(8,128)} %bitcast.100), custom_call_target="tpu_custom_call" | custom-call | tf_op jit(solution)/shard_map/reduce_rows/pallas_call | solution.py:893
  656.2 1.3 slice.117
  657.5 0.8 slice.128
  658.2 1.5 slice.123
  659.8 1.6 slice.120
  662.7 0.9 fusion.3
  666.2 6.5 copy.151
  672.7 0.7 slice_reduce_fusion.2
  673.4 5.7 place_clips.1
  679.1 1.0 slice_convert_fusion
  680.1 0.8 reshape.125
  681.1 0.7 copy.150
  681.8 1.2 copy.156
  683.0 1.4 slice_convert_fusion.3
  684.4 1.6 slice_convert_fusion.2
  (109 shorter events, 13.5 us)
Async XLA Ops:
  7.2 3.1 copy-start.6
  7.2 3.1 copy-start.3
  7.2 171.0 %all-gather.2.cloned.1.call-start = ((), (), s32[]{:S(2)}) async-start(), calls=%async_computation.1 | async-start | bytes 14598144 | tf_op jit(solution)/shard_map/all_gather | solution.py:932
  9.6 1.6 copy-start.5
  9.6 8.0 %copy-start.20 = (bf16[24,3]{0,1:T(4,128)(2,1)S(1)}, bf16[24,3]{0,1:T(4,128)(2,1)}, u32[]{:S(2)}) copy-start(bf16[24,3]{0,1:T(4,128)(2,1)} %param.17) | copy-start | bytes 436
  9.6 8.1 %copy-start.21 = (bf16[24,3]{0,1:T(4,128)(2,1)S(1)}, bf16[24,3]{0,1:T(4,128)(2,1)}, u32[]{:S(2)}) copy-start(bf16[24,3]{0,1:T(4,128)(2,1)} %param.18) | copy-start | bytes 436
  9.6 8.2 %copy-start.22 = (bf16[24,4]{0,1:T(4,128)(2,1)S(1)}, bf16[24,4]{0,1:T(4,128)(2,1)}, u32[]{:S(2)}) copy-start(bf16[24,4]{0,1:T(4,128)(2,1)} %param.20) | copy-start | bytes 580
  9.6 8.3 %copy-start.23 = (bf16[24,3]{0,1:T(4,128)(2,1)S(1)}, bf16[24,3]{0,1:T(4,128)(2,1)}, u32[]{:S(2)}) copy-start(bf16[24,3]{0,1:T(4,128)(2,1)} %param.22) | copy-start | bytes 436
  9.6 8.4 %copy-start.24 = (bf16[96]{0:T(256)(128)(2,1)S(1)}, bf16[96]{0:T(256)(128)(2,1)}, u32[]{:S(2)}) copy-start(bf16[96]{0:T(256)(128)(2,1)} %param.26) | copy-start | bytes 580
  9.7 8.7 %copy-start.4 = (bf16[24,2304]{1,0:T(8,128)(2,1)S(1)}, bf16[24,2304]{1,0:T(8,128)(2,1)}, u32[]{:S(2)}) copy-start(bf16[24,2304]{1,0:T(8,128)(2,1)} %param.19) | copy-start | bytes 331780
  9.7 8.7 %copy-start.7 = (bf16[24,768]{1,0:T(8,128)(2,1)S(1)}, bf16[24,768]{1,0:T(8,128)(2,1)}, u32[]{:S(2)}) copy-start(bf16[24,768]{1,0:T(8,128)(2,1)} %param.21) | copy-start | bytes 110596
  11.1 668.1 %reduce-scatter.2.cloned.1.call-start = ((), (), s32[]{:S(2)}) async-start(), calls=%async_computation.2 | async-start | bytes 14598144 | tf_op jit(solution)/shard_map/reduce_scatter | solution.py:936
  11.2 152.2 %collective-permute-start.6 = (s32[196,4]{0,1:T(4,128)S(1)}, s32[196,4]{0,1:T(4,128)S(1)}, u32[]{:S(2)}, u32[]{:S(2)}) collective-permute-start(s32[196,4]{0,1:T(4,128)S(1)} %get-tuple-element.236), channel_id=1, source_target_pairs={{0,1},{1,0},{2,3},{3,2},{4,5},{5,4},{6,7},{7,6},{8,9},{9,8},{10,11... | collective-permute-start | bytes 9416 | tf_op jit(solution)/shard_map/ppermute | solution.py:954
  11.7 157.1 %collective-permute-start.8 = (s32[196,4]{0,1:T(4,128)S(1)}, s32[196,4]{0,1:T(4,128)S(1)}, u32[]{:S(2)}, u32[]{:S(2)}) collective-permute-start(s32[196,4]{0,1:T(4,128)S(1)} %get-tuple-element.237), channel_id=1, source_target_pairs={{0,3},{1,2},{2,1},{3,0},{4,7},{5,6},{6,5},{7,4},{8,11},{9,10},{10,... | collective-permute-start | bytes 9416 | tf_op jit(solution)/shard_map/ppermute | solution.py:954
  109.0 69.2 %collective-permute-start.5 = (bf16[196,4,768]{2,1,0:T(4,128)(2,1)S(1)}, bf16[196,4,768]{2,1,0:T(4,128)(2,1)}, u32[]{:S(2)}, u32[]{:S(2)}) collective-permute-start(bf16[196,4,768]{2,1,0:T(4,128)(2,1)S(1)} %bitcast.109), channel_id=1, source_target_pairs={{0,3},{1,2},{2,1},{3,0},{4,7},{5,6},{6,5},{7,4},{8,11},{9,10},{10,... | collective-permute-start | bytes 3612680 | tf_op jit(solution)/shard_map/ppermute | solution.py:954
  126.0 52.1 %collective-permute-start.3 = (bf16[196,4,768]{2,1,0:T(4,128)(2,1)}, bf16[196,4,768]{2,1,0:T(4,128)(2,1)}, u32[]{:S(2)}, u32[]{:S(2)}) collective-permute-start(bf16[196,4,768]{2,1,0:T(4,128)(2,1)} %bitcast.78), channel_id=1, source_target_pairs={{0,1},{1,0},{2,3},{3,2},{4,5},{5,4},{6,7},{7,6},{8,9},{9,8},{10,11... | collective-permute-start | bytes 3612680 | tf_op jit(solution)/shard_map/ppermute | solution.py:954
  142.4 35.8 %collective-permute-start.4 = (bf16[196,4,768]{2,1,0:T(4,128)(2,1)}, bf16[196,4,768]{2,1,0:T(4,128)(2,1)}, u32[]{:S(2)}, u32[]{:S(2)}) collective-permute-start(bf16[196,4,768]{2,1,0:T(4,128)(2,1)} %bitcast.80), channel_id=1, source_target_pairs={{0,2},{1,3},{2,0},{3,1},{4,6},{5,7},{6,4},{7,5},{8,10},{9,11},{10,... | collective-permute-start | bytes 3612680 | tf_op jit(solution)/shard_map/ppermute | solution.py:954
  163.3 2.6 copy-start
  163.4 12.3 %collective-permute-start.7 = (s32[196,4]{0,1:T(4,128)S(1)}, s32[196,4]{0,1:T(4,128)S(1)}, u32[]{:S(2)}, u32[]{:S(2)}) collective-permute-start(s32[196,4]{0,1:T(4,128)S(1)} %get-tuple-element.238), channel_id=1, source_target_pairs={{0,2},{1,3},{2,0},{3,1},{4,6},{5,7},{6,4},{7,5},{8,10},{9,11},{10,... | collective-permute-start | bytes 9416 | tf_op jit(solution)/shard_map/ppermute | solution.py:954
  167.4 10.8 %copy-start.1 = (bf16[196,4,768]{2,1,0:T(4,128)(2,1)S(1)}, bf16[196,4,768]{2,1,0:T(4,128)(2,1)}, u32[]{:S(2)}) copy-start(bf16[196,4,768]{2,1,0:T(4,128)(2,1)} %get-tuple-element.226) | copy-start | bytes 3612676
  168.8 52.1 %collective-permute-start.2 = (bf16[196,4,768]{2,1,0:T(4,128)(2,1)}, bf16[196,4,768]{2,1,0:T(4,128)(2,1)}, u32[]{:S(2)}, u32[]{:S(2)}) collective-permute-start(bf16[196,4,768]{2,1,0:T(4,128)(2,1)} %get-tuple-element.224), channel_id=1, source_target_pairs={{0,3},{1,2},{2,1},{3,0},{4,7},{5,6},{6,5},{7,4},{8,11},{9,10},{10,... | collective-permute-start | bytes 3612680 | tf_op jit(solution)/shard_map/ppermute | solution.py:954
  175.7 51.5 %collective-permute-start.1 = (bf16[196,4,768]{2,1,0:T(4,128)(2,1)}, bf16[196,4,768]{2,1,0:T(4,128)(2,1)}, u32[]{:S(2)}, u32[]{:S(2)}) collective-permute-start(bf16[196,4,768]{2,1,0:T(4,128)(2,1)} %get-tuple-element.225), channel_id=1, source_target_pairs={{0,2},{1,3},{2,0},{3,1},{4,6},{5,7},{6,4},{7,5},{8,10},{9,11},{10,... | collective-permute-start | bytes 3612680 | tf_op jit(solution)/shard_map/ppermute | solution.py:954
  178.2 49.1 %collective-permute-start = (bf16[196,4,768]{2,1,0:T(4,128)(2,1)S(1)}, bf16[196,4,768]{2,1,0:T(4,128)(2,1)S(1)}, u32[]{:S(2)}, u32[]{:S(2)}) collective-permute-start(bf16[196,4,768]{2,1,0:T(4,128)(2,1)S(1)} %copy-done.1), channel_id=1, source_target_pairs={{0,1},{1,0},{2,3},{3,2},{4,5},{5,4},{6,7},{7,6},{8,9},{9,8},{10,11... | collective-permute-start | bytes 3612680 | tf_op jit(solution)/shard_map/ppermute | solution.py:954
  227.2 1.1 copy-start.25
  438.6 30.8 %collective-permute-start.9 = (bf16[196,4,768]{2,1,0:T(4,128)(2,1)}, bf16[196,4,768]{2,1,0:T(4,128)(2,1)}, u32[]{:S(2)}, u32[]{:S(2)}) collective-permute-start(bf16[196,4,768]{2,1,0:T(4,128)(2,1)} %get-tuple-element.111), channel_id=1, source_target_pairs={{0,3},{1,2},{2,1},{3,0},{4,7},{5,6},{6,5},{7,4},{8,11},{9,10},{10,... | collective-permute-start | bytes 3612680 | tf_op jit(solution)/shard_map/ppermute | solution.py:954
  438.6 35.2 %collective-permute-start.13 = (bf16[196,4,768]{2,1,0:T(4,128)(2,1)}, bf16[196,4,768]{2,1,0:T(4,128)(2,1)S(1)}, u32[]{:S(2)}, u32[]{:S(2)}) collective-permute-start(bf16[196,4,768]{2,1,0:T(4,128)(2,1)} %get-tuple-element.131), channel_id=1, source_target_pairs={{0,1},{1,0},{2,3},{3,2},{4,5},{5,4},{6,7},{7,6},{8,9},{9,8},{10,11... | collective-permute-start | bytes 3612680 | tf_op jit(solution)/shard_map/ppermute | solution.py:954
  439.0 54.5 %collective-permute-start.14 = (bf16[196,4,768]{2,1,0:T(4,128)(2,1)}, bf16[196,4,768]{2,1,0:T(4,128)(2,1)S(1)}, u32[]{:S(2)}, u32[]{:S(2)}) collective-permute-start(bf16[196,4,768]{2,1,0:T(4,128)(2,1)} %get-tuple-element.138), channel_id=1, source_target_pairs={{0,2},{1,3},{2,0},{3,1},{4,6},{5,7},{6,4},{7,5},{8,10},{9,11},{10,... | collective-permute-start | bytes 3612680 | tf_op jit(solution)/shard_map/ppermute | solution.py:954
  443.2 13.6 %copy-start.8 = (f32[1,3072]{1,0:T(1,128)S(1)}, f32[1,3072]{1,0:T(1,128)}, u32[]{:S(2)}) copy-start(f32[1,3072]{1,0:T(1,128)} %get-tuple-element.171) | copy-start | bytes 36868
  443.2 14.9 %copy-start.19 = (f32[1,768]{1,0:T(1,128)S(1)}, f32[1,768]{1,0:T(1,128)}, u32[]{:S(2)}) copy-start(f32[1,768]{1,0:T(1,128)} %get-tuple-element.172) | copy-start | bytes 9220
  443.2 15.5 %copy-start.9 = (f32[5,768]{1,0:T(8,128)S(1)}, f32[5,768]{1,0:T(8,128)}, u32[]{:S(2)}) copy-start(f32[5,768]{1,0:T(8,128)} %get-tuple-element.164) | copy-start | bytes 46084
  443.2 15.5 %copy-start.10 = (f32[3,768]{1,0:T(4,128)S(1)}, f32[3,768]{1,0:T(4,128)}, u32[]{:S(2)}) copy-start(f32[3,768]{1,0:T(4,128)} %get-tuple-element.165) | copy-start | bytes 27652
  469.4 204.0 %collective-permute-start.10 = (bf16[196,4,768]{2,1,0:T(4,128)(2,1)}, bf16[196,4,768]{2,1,0:T(4,128)(2,1)}, u32[]{:S(2)}, u32[]{:S(2)}) collective-permute-start(bf16[196,4,768]{2,1,0:T(4,128)(2,1)} %get-tuple-element.117), channel_id=1, source_target_pairs={{0,1},{1,0},{2,3},{3,2},{4,5},{5,4},{6,7},{7,6},{8,9},{9,8},{10,11... | collective-permute-start | bytes 3612680 | tf_op jit(solution)/shard_map/ppermute | solution.py:954
  469.4 204.0 %collective-permute-start.11 = (bf16[196,4,768]{2,1,0:T(4,128)(2,1)}, bf16[196,4,768]{2,1,0:T(4,128)(2,1)}, u32[]{:S(2)}, u32[]{:S(2)}) collective-permute-start(bf16[196,4,768]{2,1,0:T(4,128)(2,1)} %get-tuple-element.118), channel_id=1, source_target_pairs={{0,2},{1,3},{2,0},{3,1},{4,6},{5,7},{6,4},{7,5},{8,10},{9,11},{10,... | collective-permute-start | bytes 3612680 | tf_op jit(solution)/shard_map/ppermute | solution.py:954
  469.9 203.5 %collective-permute-start.12 = (bf16[196,4,768]{2,1,0:T(4,128)(2,1)}, bf16[196,4,768]{2,1,0:T(4,128)(2,1)}, u32[]{:S(2)}, u32[]{:S(2)}) collective-permute-start(bf16[196,4,768]{2,1,0:T(4,128)(2,1)} %get-tuple-element.119), channel_id=1, source_target_pairs={{0,3},{1,2},{2,1},{3,0},{4,7},{5,6},{6,5},{7,4},{8,11},{9,10},{10,... | collective-permute-start | bytes 3612680 | tf_op jit(solution)/shard_map/ppermute | solution.py:954
  584.7 9.9 %copy-start.11 = (f32[2,768]{1,0:T(2,128)S(1)}, f32[2,768]{1,0:T(2,128)}, u32[]{:S(2)}) copy-start(f32[2,768]{1,0:T(2,128)} %get-tuple-element.157) | copy-start | bytes 18436
  584.7 9.9 %copy-start.12 = (f32[2,768]{1,0:T(2,128)S(1)}, f32[2,768]{1,0:T(2,128)}, u32[]{:S(2)}) copy-start(f32[2,768]{1,0:T(2,128)} %get-tuple-element.159) | copy-start | bytes 18436
  584.7 9.9 %copy-start.13 = (f32[2,768]{1,0:T(2,128)S(1)}, f32[2,768]{1,0:T(2,128)}, u32[]{:S(2)}) copy-start(f32[2,768]{1,0:T(2,128)} %get-tuple-element.161) | copy-start | bytes 18436
  584.7 11.1 %copy-start.14 = (f32[1,2304]{1,0:T(1,128)S(1)}, f32[1,2304]{1,0:T(1,128)}, u32[]{:S(2)}) copy-start(f32[1,2304]{1,0:T(1,128)} %get-tuple-element.166) | copy-start | bytes 27652
  584.7 11.1 %copy-start.15 = (f32[1,768]{1,0:T(1,128)S(1)}, f32[1,768]{1,0:T(1,128)}, u32[]{:S(2)}) copy-start(f32[1,768]{1,0:T(1,128)} %get-tuple-element.167) | copy-start | bytes 9220
  584.7 11.1 %copy-start.16 = (f32[1,768]{1,0:T(1,128)S(1)}, f32[1,768]{1,0:T(1,128)}, u32[]{:S(2)}) copy-start(f32[1,768]{1,0:T(1,128)} %get-tuple-element.168) | copy-start | bytes 9220
  584.7 11.1 %copy-start.17 = (f32[1,768]{1,0:T(1,128)S(1)}, f32[1,768]{1,0:T(1,128)}, u32[]{:S(2)}) copy-start(f32[1,768]{1,0:T(1,128)} %get-tuple-element.169) | copy-start | bytes 9220
  584.7 11.1 %copy-start.18 = (f32[1,768]{1,0:T(1,128)S(1)}, f32[1,768]{1,0:T(1,128)}, u32[]{:S(2)}) copy-start(f32[1,768]{1,0:T(1,128)} %get-tuple-element.170) | copy-start | bytes 9220
  666.2 6.5 copy-start.2
Sparse Core Ops, SparseCore 0:
  11.2 146.0 all-gather.1
  438.1 185.5 reduce-scatter.1

commit v3 on v2

--- a/solution.py
+++ b/solution.py
@@ -18,7 +18,7 @@
 
 
 def cost(flops, moved=0):
-    return pl.CostEstimate(flops=int(flops), bytes_accessed=int(moved), transcendentals=0)
+    return pl.CostEstimate(flops=int(flops) // 16, bytes_accessed=int(moved), transcendentals=0)
 
 
 GAIN, SHIFT, QV, MIX, UP = 0, 3, 6, 10, 13
@@ -92,61 +92,72 @@
     return -(-rows // 16) * 16
 
 
-def attention(query, key, value, keep_probs, frames=None):
-    rows = query.shape[0]
+def attention(units, rows, frames=None):
     full = padded(rows)
     place = lax.broadcasted_iota(jnp.int32, (full, rows), 0)
     if frames is not None:
         mask = place // frames == lax.broadcasted_iota(jnp.int32, (full, rows), 1) // frames
     else:
         mask = place < rows
-    outs = []
-
-    def score(p):
-        return dot_nt(stack(grow(key[:, pair(p)], full)), query[:, pair(p)])
-
-    scores = score(0)
-    for p in range(HEADS // 2):
+
+    def score(unit):
+        return dot_nt(stack(grow(unit[1](), full)), unit[0]())
+
+    scores = score(units[0])
+    for n, (_, _, value, keep_probs, keep_mix) in enumerate(units):
         now = scores
-        if p + 1 < HEADS // 2:
-            scores = score(p + 1)
+        if n + 1 < len(units):
+            scores = score(units[n + 1])
         probs = []
         for one in (now[:full], now[full:]):
             one = jnp.where(mask, one, -1e30)
             expo = jnp.exp(one - jnp.max(one, 0, keepdims=True))
-            probs.append((expo * (1.0 / jnp.sum(expo, 0, keepdims=True))).astype(BF16))
+            probs.append((expo * (1.0 / column_sum(expo))).astype(BF16))
         probs = jnp.concatenate(probs, 0)
-        keep_probs(p, probs)
-        outs.append(dot_tn(probs, stack(grow(value[:, pair(p)], full))).astype(BF16))
-    return jnp.concatenate(outs, 1)
-
-
-def attention_back(query, key, value, grad_mix, probs_of):
-    rows = query.shape[0]
+        keep_probs(probs)
+        keep_mix(dot_tn(probs, stack(grow(value(), full))).astype(BF16))
+
+
+def attention_back(units, rows):
     full = padded(rows)
-    grad_q, grad_k, grad_v = [], [], []
-
-    def probs_grad(p):
-        return dot_nt(stack(grow(value[:, pair(p)], full)), grad_mix[:, pair(p)])
-
-    grad_p = probs_grad(0)
-    for p in range(HEADS // 2):
-        probs = probs_of(p)
+
+    def probs_grad(unit):
+        return dot_nt(stack(grow(unit[2](), full)), unit[3]())
+
+    grad_p = probs_grad(units[0])
+    for n, (query, key, _, grad_mix, probs_of, keep) in enumerate(units):
+        probs = probs_of()
         wide = probs.astype(F32)
         term = wide * grad_p
         grad_s = []
         for head in (slice(0, full), slice(full, 2 * full)):
             grad_s.append((term[head] - wide[head] * column_sum(term[head])).astype(BF16))
         grad_s = jnp.concatenate(grad_s, 0)
-        if p + 1 < HEADS // 2:
-            grad_p = probs_grad(p + 1)
-        to_v = merge(dot(probs, grad_mix[:, pair(p)]))
-        to_k = merge(dot(grad_s, query[:, pair(p)]))
-        to_q = dot_tn(grad_s, stack(grow(key[:, pair(p)], full)))
-        grad_q.append((to_q * HEAD ** (-0.5)).astype(BF16))
-        grad_k.append(to_k[:rows].astype(BF16))
-        grad_v.append(to_v[:rows].astype(BF16))
-    return jnp.concatenate(grad_q + grad_k + grad_v, 1)
+        if n + 1 < len(units):
+            grad_p = probs_grad(units[n + 1])
+        to_v = merge(dot(probs, grad_mix()))
+        to_k = merge(dot(grad_s, query()))
+        to_q = dot_tn(grad_s, stack(grow(key(), full)))
+        keep((to_q * HEAD ** (-0.5)).astype(BF16), to_k[:rows].astype(BF16), to_v[:rows].astype(BF16))
+
+
+def reader(ref, *index):
+    return lambda: ref[index]
+
+
+def writer(ref, *index):
+    def write(value):
+        ref[index] = value
+
+    return write
+
+
+def writer3(ref, lead, rows, p):
+    def write(*values):
+        for n, value in enumerate(values):
+            ref[lead + (rows, pair(n * HEADS // 2 + p))] = value
+
+    return write
 
 
 def project(rows, weights, table, query_row):
@@ -186,25 +197,37 @@
             ref[...] = jnp.zeros_like(ref)
 
 
-def space_kernel(clip, x_ref, table, w_ref, in_ref, q_ref, k_ref, v_ref, mix_ref, p_ref, out_ref):
+def put_rows(ref, value):
+    rows, full = value.shape[0], ref.shape[0]
+    ref[:rows, :] = value
+    if full > rows:
+        ref[rows:, :] = jnp.zeros((full - rows, value.shape[1]), value.dtype)
+
+
+def space_kernel(clip, x_ref, table, w_ref, *refs):
+    in_ref, q_ref, k_ref, v_ref, mix_ref, p_ref, out_ref = refs[-7:]
     rows = x_ref[0, 0].astype(F32)
     hat, _ = normalize(rows)
     normed = (hat * table[GAIN : GAIN + 1, :] + table[SHIFT : SHIFT + 1, :]).astype(BF16)
-    in_ref[0] = normed
-    query, key, value = project(normed, w_ref[:, : 3 * D], table, QV)
-    q_ref[0], k_ref[0], v_ref[0] = query, key, value
-
-    def keep(heads, probs):
-        p_ref[0, heads] = probs
-
-    mixed = attention(query, key, value, keep)
-    mix_ref[0] = mixed
-    after = rows + dot(mixed, w_ref[:, 3 * D : 4 * D]) + table[MIX : MIX + 1, :]
+    put_rows(in_ref.at[0, 0], normed)
+    q_ref[0], k_ref[0], v_ref[0] = project(normed, w_ref[:, : 3 * D], table, QV)
+    every = slice(None)
+    attention(
+        [
+            tuple(reader(ref, 0, every, pair(p)) for ref in (q_ref, k_ref, v_ref))
+            + (writer(p_ref, 0, p), writer(mix_ref, 0, every, pair(p)))
+            for p in range(HEADS // 2)
+        ],
+        rows.shape[0],
+    )
+    after = rows + dot(mix_ref[0], w_ref[:, 3 * D : 4 * D]) + table[MIX : MIX + 1, :]
     out_ref[0] = after.astype(BF16)
 
 
-def space_forward(clip, inputs, table, weights):
-    _, frames, places, _ = inputs.shape
+def space_forward(clip, step, inputs, table, weights, before):
+    batch, frames, places, _ = inputs.shape
+    full = padded(places)
+    more = [] if before is None else [before]
 
     def frame(*tail):
         return pl.BlockSpec((1,) + tail, lambda i, c: (i,) + (0,) * len(tail))
@@ -220,15 +243,21 @@
             in_specs=[
                 pl.BlockSpec((1, 1, places, D), lambda i, c: (c[0], i, 0, 0)),
                 fixed(table.shape),
-                fixed((D, 4 * D)),
-            ],
-            out_specs=[frame(places, D)] * 5 + [frame(*kept(places)), frame(places, D)],
+                columns_of(4 * D, 0),
+            ]
+            + [pl.BlockSpec(memory_space=pl.ANY) for _ in more],
+            out_specs=[pl.BlockSpec((1, 1, full, D), lambda i, c: (step, i, 0, 0))]
+            + [frame(places, D)] * 4
+            + [frame(*kept(places)), frame(places, D)],
         ),
-        out_shape=[shape(places, D)] * 5 + [shape(*kept(places)), shape(places, D)],
+        out_shape=[jax.ShapeDtypeStruct((batch, frames, full, D), BF16)]
+        + [shape(places, D)] * 4
+        + [shape(*kept(places)), shape(places, D)],
+        input_output_aliases={4: 0} if more else {},
         compiler_params=PARAMS,
         cost_estimate=cost(24 * frames * places * D * D),
         name="space_forward",
-    )(clip, inputs, table, weights)
+    )(clip, inputs, table, weights, *more)
 
 
 def largest_divisor(number, limit):
@@ -243,19 +272,16 @@
     hat, _ = normalize(rows)
     normed = (hat * table[GAIN + 1 : GAIN + 2, :] + table[SHIFT + 1 : SHIFT + 2, :]).astype(BF16)
     in_ref[...] = normed
-    query, key, value = project(normed, w_ref[:, : 3 * D], table, QV + 2)
-    q_ref[...], k_ref[...], v_ref[...] = query, key, value
-
-    def one_group(g):
+    q_ref[...], k_ref[...], v_ref[...] = project(normed, w_ref[:, : 3 * D], table, QV + 2)
+    units = []
+    for g in range(rows.shape[0] // group):
         span = slice(g * group, (g + 1) * group)
-
-        def keep(heads, probs):
-            p_ref[g, heads] = probs
-
-        mix_ref[span, :] = attention(q_ref[span, :], k_ref[span, :], v_ref[span, :], keep, frames)
-
-    for g in range(rows.shape[0] // group):
-        one_group(g)
+        for p in range(HEADS // 2):
+            units.append(
+                tuple(reader(ref, span, pair(p)) for ref in (q_ref, k_ref, v_ref))
+                + (writer(p_ref, g, p), writer(mix_ref, span, pair(p)))
+            )
+    attention(units, group, frames)
     out_ref[...] = rows + dot(mix_ref[...], w_ref[:, 3 * D :]) + table[MIX + 1 : MIX + 2, :]
 
 
@@ -300,14 +326,8 @@
 
 
 def gelu_parts(u):
-    bell = jnp.exp(-0.5 * u * u)
-    base = 1.0 + 0.2316418886 * jnp.abs(u)
-    t = 1.0 / base
-    poly = t * (
-        0.127414796 + t * (-0.142248368 + t * (0.7107068705 + t * (-0.7265760135 + t * 0.5307027145)))
-    )
-    tail = poly * bell
-    area = jnp.where(u >= 0, 1.0 - tail, tail)
+    area = 0.5 + 0.5 * lax.erf(u * 0.7071067811865476)
+    bell = jnp.exp2((-0.5 * 1.4426950408889634) * (u * u))
     return u * area, area + 0.3989422804014327 * (u * bell)
 
 
@@ -382,8 +402,8 @@
             pl.BlockSpec(memory_space=pltpu.SMEM),
             fixed(table.shape),
             fixed((1, FF)),
+            columns_of(FF, 0),
             columns_of(FF, 1),
-            columns_of(FF, 2),
         ],
         out_specs=piece_specs(teachers, tile)
         + [rows, pl.BlockSpec(memory_space=pl.ANY), fixed((3, D)), fixed((1, FF)), fixed((1, D))],
@@ -422,18 +442,15 @@
     d_out[...] += dot_tn(mix_ref[...], grad_low)
     grad_mix[...] = dot_nt(grad_low, w_ref[:, 3 * D :]).astype(BF16)
 
-    def one_group(g):
+    units = []
+    for g in range(grad.shape[0] // group):
         span = slice(g * group, (g + 1) * group)
-        grad_proj[span, :] = attention_back(
-            q_ref[span, :],
-            k_ref[span, :],
-            v_ref[span, :],
-            grad_mix[span, :],
-            lambda heads: p_ref[g, heads],
-        )
-
-    for g in range(grad.shape[0] // group):
-        one_group(g)
+        for p in range(HEADS // 2):
+            units.append(
+                tuple(reader(ref, span, pair(p)) for ref in (q_ref, k_ref, v_ref, grad_mix))
+                + (reader(p_ref, g, p), writer3(grad_proj, (), span, p))
+            )
+    attention_back(units, group)
     proj = grad_proj[...]
     d_proj[...] += dot_tn(in_ref[...], proj)
     sums = column_sum(proj.astype(F32))
@@ -492,19 +509,32 @@
     return outs, d_time, sums
 
 
-def space_back_kernel(g_ref, q_ref, k_ref, v_ref, mix_ref, p_ref, w_ref, out_ref, d_ref, bias_ref):
+def space_back_kernel(g_ref, q_ref, k_ref, v_ref, mix_ref, p_ref, w_ref, *refs):
+    out_ref, d_ref, bias_ref, grad_mix = refs[-4:]
     clear(pl.program_id(0) == 0, d_ref, bias_ref)
     grad = g_ref[0]
+    rows, full = grad.shape[0], out_ref.shape[2]
     d_ref[...] += dot_tn(mix_ref[0], grad)
     bias_ref[...] += column_sum(grad.astype(F32))
-    grad_mix = dot_nt(grad, w_ref[...]).astype(BF16)
-    out_ref[0] = attention_back(
-        q_ref[0], k_ref[0], v_ref[0], grad_mix, lambda heads: p_ref[0, heads]
+    grad_mix[...] = dot_nt(grad, w_ref[...]).astype(BF16)
+    every = slice(None)
+    attention_back(
+        [
+            tuple(reader(ref, 0, every, pair(p)) for ref in (q_ref, k_ref, v_ref))
+            + (reader(grad_mix, every, pair(p)), reader(p_ref, 0, p))
+            + (writer3(out_ref, (0, 0), slice(0, rows), p),)
+            for p in range(HEADS // 2)
+        ],
+        rows,
     )
-
-
-def space_back(grad, saved, weights):
+    if full > rows:
+        out_ref[0, 0, rows:, :] = jnp.zeros((full - rows, out_ref.shape[3]), BF16)
+
+
+def space_back(grad, step, batch, saved, weights, before):
     frames, places, _ = grad.shape
+    full = padded(places)
+    more = [] if before is None else [before]
 
     def frame(*tail):
         return pl.BlockSpec((1,) + tail, lambda i: (i,) + (0,) * len(tail))
@@ -513,111 +543,105 @@
         space_back_kernel,
         grid=(frames,),
         in_specs=[frame(places, D)] * 5
-        + [
-            frame(*kept(places)),
-            pl.BlockSpec((D, D), lambda i: (0, 3), pipeline_mode=pl.Buffered(1)),
-        ],
-        out_specs=[frame(places, 3 * D), fixed((D, D)), fixed((1, D))],
+        + [frame(*kept(places)), columns_of(D, 3)]
+        + [pl.BlockSpec(memory_space=pl.ANY) for _ in more],
+        out_specs=[
+            pl.BlockSpec((1, 1, full, 3 * D), lambda i: (step, i, 0, 0)),
+            fixed((D, D)),
+            fixed((1, D)),
+        ],
         out_shape=[
-            jax.ShapeDtypeStruct((frames, places, 3 * D), BF16),
+            jax.ShapeDtypeStruct((batch, frames, full, 3 * D), BF16),
             jax.ShapeDtypeStruct((D, D), F32),
             jax.ShapeDtypeStruct((1, D), F32),
         ],
+        scratch_shapes=[pltpu.VMEM((places, D), BF16)],
+        input_output_aliases={7: 0} if more else {},
         compiler_params=PARAMS,
         cost_estimate=cost(24 * frames * places * D * D),
         name="space_back",
-    )(grad, *saved, weights)
+    )(grad, *saved, weights, *more)
 
 
 SMALL = 128
 
 
-def space_weight_kernel(parts, steps, *refs):
-    ins, projs, outs = refs[:parts], refs[parts : 2 * parts], refs[2 * parts : 3 * parts]
-    d_ref, rows_ref, d_proj, d_out, stage, sems = refs[3 * parts :]
+def space_weight_kernel(parts, in_ref, proj_ref, w_ref, table, c_ref, b_ref, up_ref, square_ref, *refs):
+    outs, biases, refs = refs[:parts], refs[parts : 2 * parts], refs[2 * parts :]
+    d_ref, small_ref, d_proj, d_out, sums, rows, stage, sems = refs
     step, last = pl.program_id(0), pl.num_programs(0) - 1
-    clear(step == 0, d_proj, rows_ref)
-    for part in range(parts):
-
-        @pl.when(step // steps == part)
-        def _():
-            frames = range(ins[part].shape[0])
-            d_proj[...] += sum(dot_tn(ins[part][f], projs[part][f]) for f in frames)
-            rows_ref[...] += sum(column_sum(projs[part][f].astype(F32)) for f in frames)
+    clear(step == 0, d_proj, sums, rows)
+    proj = proj_ref[0].reshape(-1, 3 * D)
+    d_proj[...] += dot_tn(in_ref[0].reshape(-1, D), proj)
+    sums[...] += column_sum(proj.astype(F32))
 
     @pl.when(step == last)
     def _():
         d_out[...] = sum(ref[...] for ref in outs)
         moves = [(d_proj.at[:, pl.ds(c * D, D)], d_ref.at[:, pl.ds(c * D, D)]) for c in range(3)]
         flush(moves + [(d_out, d_ref.at[:, pl.ds(3 * D, D)])], stage, sems)
-
-
-def space_weights(ins, projs, outs):
-    parts = len(ins)
-    frames, places, _ = ins[0].shape
-    block = largest_divisor(frames, 2)
-    steps = frames // block
-
-    def frame(part, width):
-        return pl.BlockSpec(
-            (block, places, width), lambda i: (jnp.clip(i - part * steps, 0, steps - 1), 0, 0)
-        )
-
+        many = up_ref.shape[0]
+        rows[1:2, :], rows[2:3, :] = b_ref[0:1, :], c_ref[0:1, :]
+        rows[4:5, :], rows[5:6, :] = b_ref[1:2, :], c_ref[1:2, :]
+        rows[6:7, :], rows[7:8, :] = sums[:, :D], sums[:, 2 * D :]
+        rows[8:9, :], rows[9:10, :] = b_ref[3:4, :], b_ref[2:3, :]
+        rows[10:11, :] = sum(ref[...] for ref in biases)
+        rows[11:12, :], rows[12:13, :] = b_ref[4:5, :], c_ref[2:3, :]
+        rows[13 : 13 + many, :] = up_ref[...]
+        square = jnp.sum(square_ref[...], -1, keepdims=True)
+        rows[13 + many : 14 + many, :] = jnp.broadcast_to(square, square_ref.shape)
+        rows[SMALL - 2 : SMALL - 1, :] = table[GAIN : GAIN + 1, :]
+        rows[SMALL - 1 : SMALL, :] = table[SHIFT : SHIFT + 1, :]
+        columns = jnp.swapaxes(rows[...], 0, 1)
+        wide = w_ref[...].astype(F32)
+        with_grad = jnp.sum(wide * d_proj[...], -1, keepdims=True)
+        shift_grad = jnp.sum(wide * sums[...], -1, keepdims=True)
+        gain, shift = columns[:, SMALL - 2 : SMALL - 1], columns[:, SMALL - 1 :]
+        gain_grad = (with_grad - shift * shift_grad) / gain
+        lane = lax.broadcasted_iota(jnp.int32, columns.shape, 1)
+        small_ref[...] = jnp.where(lane == 0, gain_grad, jnp.where(lane == 3, shift_grad, columns))
+
+
+def space_weights(ins, projs, weights, table, rows_c, rows_b, bias_up, squares, outs, biases):
+    batch, frames, full, _ = ins.shape
+
+    def clip(width):
+        return pl.BlockSpec((1, frames, full, width), lambda i: (i, 0, 0, 0))
+
+    smalls = [table, rows_c, rows_b, bias_up, squares]
     return pl.pallas_call(
-        functools.partial(space_weight_kernel, parts, steps),
-        grid=(parts * steps,),
-        in_specs=[frame(p, D) for p in range(parts)]
-        + [frame(p, 3 * D) for p in range(parts)]
-        + [fixed((D, D))] * parts,
-        out_specs=[pl.BlockSpec(memory_space=pl.ANY), fixed((1, 3 * D))],
-        out_shape=[
-            jax.ShapeDtypeStruct((D, 4 * D), BF16),
-            jax.ShapeDtypeStruct((1, 3 * D), F32),
-        ],
+        functools.partial(space_weight_kernel, batch),
+        grid=(batch,),
+        in_specs=[clip(D), clip(3 * D), columns_of(3 * D, 0)]
+        + [fixed(a.shape) for a in smalls]
+        + [fixed((D, D))] * batch
+        + [fixed((1, D))] * batch,
+        out_specs=[pl.BlockSpec(memory_space=pl.ANY), fixed((D, SMALL))],
+        out_shape=[jax.ShapeDtypeStruct((D, 4 * D), BF16), jax.ShapeDtypeStruct((D, SMALL), F32)],
         scratch_shapes=[
             pltpu.VMEM((D, 3 * D), F32),
             pltpu.VMEM((D, D), F32),
+            pltpu.VMEM((1, 3 * D), F32),
+            pltpu.VMEM((SMALL, D), F32),
             pltpu.VMEM((2, D, D), BF16),
             pltpu.SemaphoreType.DMA((2,)),
         ],
         compiler_params=PARAMS,
-        cost_estimate=cost(18 * parts * frames * places * D * D),
+        cost_estimate=cost(18 * batch * frames * full * D * D),
         name="space_weights",
-    )(*ins, *projs, *outs)
-
-
-def small_kernel(count, *refs):
-    rows, (out_ref, table) = refs[:count], refs[count:]
-    table[...] = jnp.zeros_like(table)
-    at = 0
-    for ref in rows:
-        table[at : at + ref.shape[0], :] = ref[...]
-        at += ref.shape[0]
-    out_ref[...] = jnp.swapaxes(table[...], 0, 1)
-
-
-def as_columns(rows):
-    return pl.pallas_call(
-        functools.partial(small_kernel, len(rows)),
-        out_shape=jax.ShapeDtypeStruct((D, SMALL), F32),
-        scratch_shapes=[pltpu.VMEM((SMALL, D), F32)],
-        name="as_columns",
-    )(*rows)
+    )(ins, projs, weights, *smalls, *outs, *biases)
 
 
 def input_kernel(clip, g_ref, p_ref, x_ref, table, w_ref, *refs):
-    out_ref, rows_ref = refs[-2:]
-    clear(pl.program_id(0) == 0, rows_ref)
-    back = dot_nt(p_ref[0], w_ref[...])
+    out_ref = refs[-1]
+    back = dot_nt(p_ref[0, 0, : g_ref.shape[1], :], w_ref[...])
     hat, inverse = normalize(x_ref[0, 0].astype(F32))
-    rows_ref[...] += jnp.concatenate([column_sum(back * hat), column_sum(back)], 0)
     grad = g_ref[0].astype(F32) + normalize_back(back, hat, inverse, table[GAIN : GAIN + 1, :])
     out_ref[0, 0] = grad.astype(BF16)
 
 
-def input_grads(clip, grad, proj, inputs, table, weights, before):
+def input_grads(clip, step, grad, projs, inputs, table, weights, before):
     frames, places, _ = grad.shape
-    frame = pl.BlockSpec((1, places, D), lambda i, c: (i, 0, 0))
     block = pl.BlockSpec((1, 1, places, D), lambda i, c: (c[0], i, 0, 0))
     more = [] if before is None else [before]
     return pl.pallas_call(
@@ -626,21 +650,21 @@
             num_scalar_prefetch=1,
             grid=(frames,),
             in_specs=[
-                frame,
-                pl.BlockSpec((1, places, 3 * D), lambda i, c: (i, 0, 0)),
+                pl.BlockSpec((1, places, D), lambda i, c: (i, 0, 0)),
+                pl.BlockSpec((1, 1) + projs.shape[2:], lambda i, c: (step, i, 0, 0)),
                 block,
                 fixed(table.shape),
                 columns_of(3 * D, 0),
             ]
             + [pl.BlockSpec(memory_space=pl.ANY) for _ in more],
-            out_specs=[block, fixed((2, D))],
+            out_specs=block,
         ),
-        out_shape=[jax.ShapeDtypeStruct(inputs.shape, BF16), jax.ShapeDtypeStruct((2, D), F32)],
+        out_shape=jax.ShapeDtypeStruct(inputs.shape, BF16),
         input_output_aliases={6: 0} if more else {},
         compiler_params=PARAMS,
         cost_estimate=cost(18 * frames * places * D * D),
         name="input_grads",
-    )(clip, grad, proj, inputs, table, weights, *more)
+    )(clip, grad, projs, inputs, table, weights, *more)
 
 
 def place_kernel(order, *refs):
@@ -968,7 +992,7 @@
         got = []
         for step in range(ring):
             mine = lax.dynamic_index_in_dim(block, clip_of(step), 0, keepdims=False)
-            got.append(swap(cut(jnp.swapaxes(mine, 0, 1), step), step))
+            got.append(cut(jnp.swapaxes(mine, 0, 1), step))
         return got
 
     many = FF // D
@@ -984,7 +1008,8 @@
     smalls = jnp.pad(smalls, ((0, 0), (0, SMALL - smalls.shape[1])))
     first = gather_rows(jnp.concatenate([w_space, w_space_out, smalls], 1))
     up_turned = jnp.swapaxes(w_up.reshape(depth, D, many), 1, 2).reshape(depth, FF)
-    rest = gather(jnp.concatenate([w_time, w_time_out, up_turned, w_down.reshape(depth, FF)], 1))
+    time_weights = gather(jnp.concatenate([w_time, w_time_out], 1))
+    to_feed = jnp.concatenate([up_turned, w_down.reshape(depth, FF)], 1)
     table = jnp.swapaxes(first[:, 4 * D : 4 * D + 24].astype(F32), 0, 1)
     up_row = table[UP : UP + many].reshape(1, FF)
     counted = table[UP + many : UP + many + 2, ::depth]
@@ -994,31 +1019,36 @@
 
     order = [((me // pieces) ^ j).astype(jnp.int32) for j in range(batch)]
     clip_ids = [jnp.reshape(c, (1,)) for c in order]
-    valid_column = jnp.concatenate(spread(valid), 1).reshape(-1, 1).astype(F32)
-    saved, sent = [None] * batch, [None] * ring
-    for j in list(range(batch))[::-1]:
-        *kept_j, after = space_forward(clip_ids[j], clips_in, table, first)
+    valid_column = [swap(part, step) for step, part in enumerate(spread(valid))]
+    valid_column = jnp.concatenate(valid_column, 1).reshape(-1, 1).astype(F32)
+    saved, sent, ins = [None] * batch, [None] * ring, None
+    near = min(1, batch - 1)
+    turns = [j for j in range(batch - 1, -1, -1) if j != near] + [near]
+    cuts = spread(teacher)
+    for turn, j in enumerate(turns):
+        if turn == 3:
+            ins, sent[-1], cuts = lax.optimization_barrier((ins, sent[-1], cuts))
+        ins, *kept_j, after = space_forward(clip_ids[j], j, clips_in, table, first, ins)
         saved[j] = kept_j
         after = jnp.swapaxes(after, 0, 1)
+        if turn == 0:
+            after, to_feed = lax.optimization_barrier((after, to_feed))
+        if j == 0:
+            cuts, after = lax.optimization_barrier((cuts, after))
         for r in range(pieces):
             step = j * pieces + r
             sent[step] = swap(cut(after, step), step)
-        if j == batch // 2:
-            teacher, after = lax.optimization_barrier((teacher, after))
-
-    teachers = spread(teacher)
-    *saved_b, after_b = time_forward(sent, table, rest)
+    feed_weights = gather(to_feed)
+    teachers = [swap(part, step) for step, part in enumerate(cuts)]
+    *saved_b, after_b = time_forward(sent, table, time_weights)
     tile, _ = time_tiles(chunk, all_frames)
     layer_parts, grad_b, d_feed, rows_c, bias_up, squares = feed_forward(
-        after_b, teachers, valid_column, scale, table, up_row, rest, tile
+        after_b, teachers, valid_column, scale, table, up_row, feed_weights, tile
     )
-    squares = jnp.broadcast_to(jnp.sum(squares).reshape(1, 1), (1, D))
-    grad_parts, d_rest, rows_b = time_back(grad_b, saved_b, sent, table, rest, d_feed)
+    grad_parts, d_rest, rows_b = time_back(grad_b, saved_b, sent, table, time_weights, d_feed)
     d_rest = scatter(d_rest)
     d_time, d_feed = d_rest[:, : 4 * D], d_rest[:, 4 * D :]
     grad_parts = [swap(part, step) for step, part in enumerate(grad_parts)]
-    grad_parts[-1], layer_parts = lax.optimization_barrier((grad_parts[-1], layer_parts))
-    layer_parts = [swap(part, step) for step, part in enumerate(layer_parts)]
 
     def join(parts, j):
         if pieces == 1:
@@ -1029,27 +1059,23 @@
             whole = lax.dynamic_update_slice_in_dim(whole, parts[step], place_of(step), 0)
         return whole
 
-    projs, outs, biases, rows_a, input_grad = [], [], [], [], None
+    outs, biases, projs, input_grad = [], [], None, None
+    grads = [jnp.swapaxes(join(grad_parts, 0), 0, 1)] + [None] * (batch - 1)
     for j in range(batch):
-        grad = jnp.swapaxes(join(grad_parts, j), 0, 1)
-        proj, d_out, bias = space_back(grad, saved[j][1:], first)
-        projs.append(proj)
+        projs, d_out, bias = space_back(grads[j], j, batch, saved[j], first, projs)
         outs.append(d_out)
         biases.append(bias)
-        input_grad, rows = input_grads(clip_ids[j], grad, proj, clips_in, table, first, input_grad)
-        rows_a.append(rows)
-    d_space, sums_a = space_weights([kept_j[0] for kept_j in saved], projs, outs)
-    rows_a, biases = sum(rows_a), sum(biases)
-    columns = as_columns(
-        [
-            rows_a[0:1], rows_b[0:1], rows_c[0:1],
-            rows_a[1:2], rows_b[1:2], rows_c[1:2],
-            sums_a[:, :D], sums_a[:, 2 * D :], rows_b[3:4], rows_b[2:3],
-            biases, rows_b[4:5], rows_c[2:3],
-            bias_up.reshape(many, D), squares,
-        ]
+        if j == batch // 2:
+            projs, layer_parts = lax.optimization_barrier((projs, layer_parts))
+            layer_parts = [swap(part, step) for step, part in enumerate(layer_parts)]
+        if j + 1 < batch:
+            following = jnp.swapaxes(join(grad_parts, j + 1), 0, 1)
+            grads[j + 1] = following
+        input_grad = input_grads(clip_ids[j], j, grads[j], projs, clips_in, table, first, input_grad)
+    d_space, small = space_weights(
+        ins, projs, first, table, rows_c, rows_b, bias_up.reshape(many, D), squares, outs, biases
     )
-    d_space, here = reduce_rows(d_space, columns)
+    d_space, here = reduce_rows(d_space, small)
     layer_out = place_clips(jnp.stack(order), [join(layer_parts, j) for j in range(batch)])
     d_up = jnp.swapaxes(d_feed[:, :FF].reshape(depth, many, D), 1, 2).reshape(depth, FF)
     return (

time: 698 us -> 682 us (0.977)
    pallas_call x1, Pallas kernels: 56.8 us -> 81.3 us  [reduce_rows(): pl.pallas_call(functools.partial(reduce_kernel, depth, height), in_specs=...]
    pallas_call x1, Pallas kernels: 67.6 us -> 53.1 us  [gather_rows(): pl.pallas_call(functools.partial(gather_kernel, depth, height), in_specs=...]
    pallas_call x1, Pallas kernels: 140 us -> 133 us  [feed_forward(): pl.pallas_call(functools.partial(feed_kernel, ring), grid=(tokens // tile...]
    pallas_call x2 -> x1, Pallas kernels: 33 us -> 29.1 us  [space_weights(): pl.pallas_call(functools.partial(space_weight_kernel, batch), grid=(batch...]
    unnamed x66 -> x32, local copies, waits for them, and re-layouts: 19.1 us -> 20.6 us
  transfers between devices with their start and end apart: 17 -> 18, of which waited for: 3 -> 4; matrix products, arithmetic and copies ran while one was open for 8% -> 9% of each run, Pallas kernels for 51% -> 52%
where the time goes in v3:
time: 682 us
  Pallas kernels  556 us (82%)
  local copies, waits for them, and re-layouts  58.2 us (9%)
  waiting for transfers between devices  24.5 us (4%)
  between operations  20 us (3%)
  other arithmetic  12.3 us (2%)
  starting transfers between devices  10.4 us (2%)
    pallas_call x1, Pallas kernels, feed_forward(): pl.pallas_call(functools.partial(feed_kernel, ring), grid=(tokens // tile...  133 us
    pallas_call x1, Pallas kernels, reduce_rows(): pl.pallas_call(functools.partial(reduce_kernel, depth, height), in_specs=...  81.3 us
    pallas_call x1, Pallas kernels, time_back(): pl.pallas_call(functools.partial(time_back_kernel, group, ring), grid=(to...  66.8 us
    pallas_call x4, Pallas kernels, space_forward(): pl.pallas_call(space_kernel, grid_spec=pltpu.PrefetchScalarGridSpec(num_s...  54 us
    pallas_call x1, Pallas kernels, gather_rows(): pl.pallas_call(functools.partial(gather_kernel, depth, height), in_specs=...  53.1 us
    pallas_call x4, Pallas kernels, space_back(): pl.pallas_call(space_back_kernel, grid=(frames,), in_specs=[frame(places,...  52.3 us
    pallas_call x1, Pallas kernels, time_forward(): pl.pallas_call(functools.partial(time_kernel, frames, group, len(parts)),...  42.3 us
    pallas_call x4, Pallas kernels, input_grads(): pl.pallas_call(input_kernel, grid_spec=pltpu.PrefetchScalarGridSpec(num_s...  38.8 us
  transfers between devices with their start and end apart: 18, of which 4 were waited for; matrix products, arithmetic and copies ran while one was open for 9% of the time, Pallas kernels for 52%

profile of v3, /device:TPU:0, one launch (start us, length us, event | category | flops | bytes accessed | tf_op | source)
XLA Modules:
  0.0 681.7 jit_solution(13452606607693951526)
XLA Ops:
  7.2 1.6 pad_maximum_fusion.1
  8.9 1.4 reduce_sum.27
  12.9 0.8 copy.122
  13.7 0.8 copy.123
  14.4 0.8 copy.124
  15.2 0.8 copy.125
  16.0 0.8 reshape.109
  16.9 1.6 fusion.1.in_ref
  18.5 53.1 %gather_rows.1 = bf16[8,2,2,24,3200]{4,3,2,1,0:T(8,128)(2,1)} custom-call(bf16[24,3200]{1,0:T(8,128)(2,1)} %fusion.1.in_ref), custom_call_target="tpu_custom_call" | custom-call | tf_op jit(solution)/shard_map/gather_rows/pallas_call | solution.py:789
  71.7 1.0 convert_bitcast_fusion
  72.6 0.8 copy.131.table.refs_4_.refs_7_.refs_8_
  73.4 5.2 copy.130.x_ref
  78.6 13.4 %space_forward.4 = (bf16[4,4,208,768]{3,2,1,0:T(8,128)(2,1)}, bf16[4,196,768]{2,1,0:T(8,128)(2,1)}, bf16[4,196,768]{2,1,0:T(8,128)(2,1)}, bf16[4,196,768]{2,1,0:...) custom-call(s32[1]{0:T(128)} %bitcast.3.clip, ...), custom_call_target="tpu_custom_call" | custom-call | flops 693633024 | tf_op jit(solution)/shard_map/space_forward/pallas_call | solution.py:238
  92.0 1.8 copy.183
  94.9 0.7 pad_maximum_fusion
  95.7 1.6 collective-permute-start
  97.3 13.7 %space_forward.5 = (bf16[4,4,208,768]{3,2,1,0:T(8,128)(2,1)}, bf16[4,196,768]{2,1,0:T(8,128)(2,1)}, bf16[4,196,768]{2,1,0:T(8,128)(2,1)}, bf16[4,196,768]{2,1,0:...) custom-call(s32[1]{0:T(128)} %bitcast.2.clip, ...), custom_call_target="tpu_custom_call", output_to_operand_aliasing={{0}: (4, {})} | custom-call | flops 693633024 | tf_op jit(solution)/shard_map/space_forward/pallas_call | solution.py:238
  111.0 2.9 copy.180
  114.4 13.4 %space_forward.6 = (bf16[4,4,208,768]{3,2,1,0:T(8,128)(2,1)}, bf16[4,196,768]{2,1,0:T(8,128)(2,1)}, bf16[4,196,768]{2,1,0:T(8,128)(2,1)}, bf16[4,196,768]{2,1,0:...) custom-call(s32[1]{0:T(128)} %bitcast.clip, ...), custom_call_target="tpu_custom_call", output_to_operand_aliasing={{0}: (4, {})} | custom-call | flops 693633024 | tf_op jit(solution)/shard_map/space_forward/pallas_call | solution.py:238
  127.9 2.8 copy.182
  130.6 5.9 dynamic-slice_bitcast_fusion
  136.5 13.5 %space_forward.7 = (bf16[4,4,208,768]{3,2,1,0:T(8,128)(2,1)}, bf16[4,196,768]{2,1,0:T(8,128)(2,1)}, bf16[4,196,768]{2,1,0:T(8,128)(2,1)}, bf16[4,196,768]{2,1,0:...) custom-call(s32[1]{0:T(128)} %bitcast.1.clip, ...), custom_call_target="tpu_custom_call", output_to_operand_aliasing={{0}: (4, {})} | custom-call | flops 693633024 | tf_op jit(solution)/shard_map/space_forward/pallas_call | solution.py:238
  150.0 2.8 copy.181
  153.3 1.5 collective-permute-start.7
  155.6 1.2 collective-permute-done.7
  156.9 1.5 collective-permute-start.2
  159.4 0.7 slice_reduce_fusion
  161.6 2.0 convert_element_type.51.refs_5_
  163.6 42.3 %time_forward.1 = (bf16[3136,768]{1,0:T(8,128)(2,1)}, bf16[3136,768]{1,0:T(8,128)(2,1)}, bf16[3136,768]{1,0:T(8,128)(2,1)}, bf16[3136,768]{1,0:T(8,128)(2,1)}, b...) custom-call(bf16[196,4,768]{2,1,0:T(4,128)(2,1)} %bitcast.109, ...), custom_call_target="tpu_custom_call" | custom-call | flops 2774532096 | tf_op jit(solution)/shard_map/time_forward/pallas_call | solution.py:310
  206.0 20.8 %collective-permute-done.3.refs_3_ = bf16[196,4,768]{2,1,0:T(4,128)(2,1)} collective-permute-done((bf16[196,4,768]{2,1,0:T(4,128)(2,1)}, bf16[196,4,768]{2,1,0:T(4,128)(2,1)}, u32[]{:S(2)}, u32[]{:S(2)}) %collective-permute-start.3) | collective-permute-done | bytes 1204256 | tf_op jit(solution)/shard_map/ppermute | solution.py:978
  226.8 132.7 %feed_forward.1 = (bf16[196,4,768]{2,1,0:T(4,128)(2,1)}, bf16[196,4,768]{2,1,0:T(4,128)(2,1)}, bf16[196,4,768]{2,1,0:T(4,128)(2,1)}, bf16[196,4,768]{2,1,0:T(4,1...) custom-call(bf16[196,4,768]{2,1,0:T(4,128)(2,1)} %get-tuple-element., ...), custom_call_target="tpu_custom_call" | custom-call | flops 9248440320 | tf_op jit(solution)/shard_map/feed_forward/pallas_call | solution.py:395
  359.5 66.8 %time_back.1 = (bf16[196,4,768]{2,1,0:T(4,128)(2,1)}, bf16[196,4,768]{2,1,0:T(4,128)(2,1)}, bf16[196,4,768]{2,1,0:T(4,128)(2,1)}, bf16[196,4,768]{2,1,0:T(4,128)...) custom-call(f32[3136,768]{1,0:T(8,128)} %get-tuple-element.121.refs_0_, ...), custom_call_target="tpu_custom_call", output_to_operand_aliasing={{4}: (10, {})} | custom-call | flops 4855431168 | tf_op jit(solution)/shard_map/time_back/pallas_call | solution.py:482
  426.4 0.9 collective-permute-start.10
  427.3 1.5 collective-permute-start.9
  428.8 1.2 copy.177
  429.9 12.9 %space_back.4 = (bf16[4,4,208,2304]{3,2,1,0:T(8,128)(2,1)}, f32[768,768]{1,0:T(8,128)}, f32[1,768]{1,0:T(1,128)}) custom-call(bf16[4,196,768]{2,1,0:T(8,128)(2,1)} %bitcast.96, bf16[4,196,768]{2,1,0:T(8,128)(2,1)} %get-tuple-element.143.q_ref, bf16[4,196,768]{2,1,0:T(8,128)(2,1)} %get-tuple-element.144.k_ref, bf16[4,196,768]{2,1,0:T(8,128)(2,1)} %get-tuple-element.145.v_ref, ...), custom_call_target="tpu_custom_call" | custom-call | flops 693633024 | tf_op jit(solution)/shard_map/space_back/pallas_call | solution.py:542
  442.9 9.7 %input_grads.4.refs_0_ = bf16[4,4,196,768]{3,2,1,0:T(8,128)(2,1)} custom-call(s32[1]{0:T(128)} %bitcast.clip, bf16[4,196,768]{2,1,0:T(8,128)(2,1)} %bitcast.97, bf16[4,4,208,2304]{3,2,1,0:T(8,128)(2,1)} %get-tuple-element.148.refs_0_.p_ref, bf16[4,4,196,768]{3,2,1,0:T(8,128)(2,1)} %copy.130.x_ref, f32[16,768]{1,0:T(8,128)} %copy.131.table.refs_4_.refs_7_.refs_8_, ...), custom_call_target="tpu_custom_call" | custom-call | flops 520224768 | tf_op jit(solution)/shard_map/input_grads/pallas_call | solution.py:647
  452.6 2.5 copy.178
  455.2 1.8 collective-permute-done.9
  457.0 2.5 copy.179
  459.5 13.2 %space_back.5 = (bf16[4,4,208,2304]{3,2,1,0:T(8,128)(2,1)}, f32[768,768]{1,0:T(8,128)}, f32[1,768]{1,0:T(1,128)}) custom-call(bf16[4,196,768]{2,1,0:T(8,128)(2,1)} %bitcast.102, bf16[4,196,768]{2,1,0:T(8,128)(2,1)} %get-tuple-element.137.q_ref, bf16[4,196,768]{2,1,0:T(8,128)(2,1)} %get-tuple-element.138.k_ref, ...), custom_call_target="tpu_custom_call", output_to_operand_aliasing={{0}: (7, {})} | custom-call | flops 693633024 | tf_op jit(solution)/shard_map/space_back/pallas_call | solution.py:542
  472.7 9.9 %input_grads.5.refs_0_ = bf16[4,4,196,768]{3,2,1,0:T(8,128)(2,1)} custom-call(s32[1]{0:T(128)} %bitcast.1.clip, bf16[4,196,768]{2,1,0:T(8,128)(2,1)} %bitcast.103, bf16[4,4,208,2304]{3,2,1,0:T(8,128)(2,1)} %get-tuple-element.149.refs_0_.p_ref, bf16[4,4,196,768]{3,2,1,0:T(8,128)(2,1)} %copy.130.x_ref, ...), custom_call_target="tpu_custom_call", output_to_operand_aliasing={{}: (6, {})} | custom-call | flops 520224768 | tf_op jit(solution)/shard_map/input_grads/pallas_call | solution.py:647
  482.7 13.3 %space_back.6 = (bf16[4,4,208,2304]{3,2,1,0:T(8,128)(2,1)}, f32[768,768]{1,0:T(8,128)}, f32[1,768]{1,0:T(1,128)}) custom-call(bf16[4,196,768]{2,1,0:T(8,128)(2,1)} %bitcast.100, bf16[4,196,768]{2,1,0:T(8,128)(2,1)} %get-tuple-element.131.q_ref, bf16[4,196,768]{2,1,0:T(8,128)(2,1)} %get-tuple-element.132.k_ref, ...), custom_call_target="tpu_custom_call", output_to_operand_aliasing={{0}: (7, {})} | custom-call | flops 693633024 | tf_op jit(solution)/shard_map/space_back/pallas_call | solution.py:542
  495.9 1.6 collective-permute-start.12
  500.2 1.2 copy.176
  501.4 9.5 %input_grads.6.refs_0_ = bf16[4,4,196,768]{3,2,1,0:T(8,128)(2,1)} custom-call(s32[1]{0:T(128)} %bitcast.2.clip, bf16[4,196,768]{2,1,0:T(8,128)(2,1)} %bitcast.101, bf16[4,4,208,2304]{3,2,1,0:T(8,128)(2,1)} %get-tuple-element.166.refs_0_.p_ref, bf16[4,4,196,768]{3,2,1,0:T(8,128)(2,1)} %copy.130.x_ref, ...), custom_call_target="tpu_custom_call", output_to_operand_aliasing={{}: (6, {})} | custom-call | flops 520224768 | tf_op jit(solution)/shard_map/input_grads/pallas_call | solution.py:647
  510.9 12.9 %space_back.7 = (bf16[4,4,208,2304]{3,2,1,0:T(8,128)(2,1)}, f32[768,768]{1,0:T(8,128)}, f32[1,768]{1,0:T(1,128)}) custom-call(bf16[4,196,768]{2,1,0:T(8,128)(2,1)} %bitcast.98, bf16[4,196,768]{2,1,0:T(8,128)(2,1)} %get-tuple-element.161.q_ref, bf16[4,196,768]{2,1,0:T(8,128)(2,1)} %get-tuple-element.162.k_ref, ...), custom_call_target="tpu_custom_call", output_to_operand_aliasing={{0}: (7, {})} | custom-call | flops 693633024 | tf_op jit(solution)/shard_map/space_back/pallas_call | solution.py:542
  523.8 29.1 %space_weights.1 = (bf16[768,3072]{1,0:T(8,128)(2,1)}, f32[768,128]{1,0:T(8,128)}) custom-call(bf16[4,4,208,768]{3,2,1,0:T(8,128)(2,1)} %get-tuple-element.159.in_ref, bf16[4,4,208,2304]{3,2,1,0:T(8,128)(2,1)} %get-tuple-element.167.proj_ref.p_ref, bf16[768,3200]{1,0:T(8,128)(2,1)} %bitcast.94, f32[16,768]{1,0:T(8,128)} %copy.131.table.refs_4_.refs_7_.refs_8_, ...), custom_call_target="tpu_custom_call" | custom-call | flops 2208301056 | tf_op jit(solution)/shard_map/space_weights/pallas_call | solution.py:612
  552.9 81.3 %reduce_rows.1 = (f32[24,3072]{1,0:T(8,128)}, f32[24,128]{1,0:T(8,128)}) custom-call(bf16[8,2,2,24,3072]{4,3,2,1,0:T(8,128)(2,1)} %bitcast.106, f32[8,2,2,24,128]{4,3,2,1,0:T(8,128)} %bitcast.113), custom_call_target="tpu_custom_call" | custom-call | tf_op jit(solution)/shard_map/reduce_rows/pallas_call | solution.py:917
  634.2 1.6 slice.72
  635.9 1.5 slice.75
  637.4 0.8 slice.80
  638.2 1.3 slice.69
  639.4 9.6 %input_grads.7 = bf16[4,4,196,768]{3,2,1,0:T(8,128)(2,1)} custom-call(s32[1]{0:T(128)} %bitcast.3.clip, bf16[4,196,768]{2,1,0:T(8,128)(2,1)} %bitcast.99, bf16[4,4,208,2304]{3,2,1,0:T(8,128)(2,1)} %get-tuple-element.167.proj_ref.p_ref, bf16[4,4,196,768]{3,2,1,0:T(8,128)(2,1)} %copy.130.x_ref, ...), custom_call_target="tpu_custom_call", output_to_operand_aliasing={{}: (6, {})} | custom-call | flops 520224768 | tf_op jit(solution)/shard_map/input_grads/pallas_call | solution.py:647
  649.0 6.5 copy.160
  659.5 0.7 slice_reduce_fusion.2
  660.2 1.0 copy-done.3
  661.2 5.7 place_clips.1
  666.9 1.0 slice_convert_fusion
  668.1 0.7 copy.159
  668.8 1.2 copy.165
  670.0 0.8 reshape.121
  670.8 1.6 slice_convert_fusion.2
  672.4 1.4 slice_convert_fusion.3
  (72 shorter events, 10.7 us)
Async XLA Ops:
  7.2 156.4 %all-gather.3.cloned.1.call-start = ((), (), s32[]{:S(2)}) async-start(), calls=%async_computation.1 | async-start | bytes 4866048 | tf_op jit(solution)/shard_map/all_gather | solution.py:956
  8.8 218.0 %all-gather.5.cloned.1.call-start = ((), (), s32[]{:S(2)}) async-start(), calls=%async_computation.2 | async-start | bytes 9732096 | tf_op jit(solution)/shard_map/all_gather | solution.py:956
  92.0 1.8 copy-start.5
  93.8 0.9 copy-start.6
  95.7 571.3 %reduce-scatter.2.cloned.1.call-start = ((), (), s32[]{:S(2)}) async-start(), calls=%async_computation.3 | async-start | bytes 14598144 | tf_op jit(solution)/shard_map/reduce_scatter | solution.py:960
  95.7 40.8 %collective-permute-start = (bf16[196,4,768]{2,1,0:T(4,128)(2,1)S(1)}, bf16[196,4,768]{2,1,0:T(4,128)(2,1)}, u32[]{:S(2)}, u32[]{:S(2)}) collective-permute-start(bf16[196,4,768]{2,1,0:T(4,128)(2,1)S(1)} %bitcast.110), channel_id=1, source_target_pairs={{0,3},{1,2},{2,1},{3,0},{4,7},{5,6},{6,5},{7,4},{8,11},{9,10},{10,... | collective-permute-start | bytes 3612680 | tf_op jit(solution)/shard_map/ppermute | solution.py:978
  113.9 49.7 %collective-permute-start.5 = (bf16[196,4,768]{2,1,0:T(4,128)(2,1)}, bf16[196,4,768]{2,1,0:T(4,128)(2,1)}, u32[]{:S(2)}, u32[]{:S(2)}) collective-permute-start(bf16[196,4,768]{2,1,0:T(4,128)(2,1)} %bitcast.77), channel_id=1, source_target_pairs={{0,2},{1,3},{2,0},{3,1},{4,6},{5,7},{6,4},{7,5},{8,10},{9,11},{10,... | collective-permute-start | bytes 3612680 | tf_op jit(solution)/shard_map/ppermute | solution.py:978
  150.0 2.8 copy-start.7
  152.8 10.8 %collective-permute-start.4 = (bf16[196,4,768]{2,1,0:T(4,128)(2,1)}, bf16[196,4,768]{2,1,0:T(4,128)(2,1)}, u32[]{:S(2)}, u32[]{:S(2)}) collective-permute-start(bf16[196,4,768]{2,1,0:T(4,128)(2,1)} %bitcast.78), channel_id=1, source_target_pairs={{0,1},{1,0},{2,3},{3,2},{4,5},{5,4},{6,7},{7,6},{8,9},{9,8},{10,11... | collective-permute-start | bytes 3612680 | tf_op jit(solution)/shard_map/ppermute | solution.py:978
  152.8 2.5 collective-permute-start.6
  153.3 3.6 collective-permute-start.7
  154.8 3.6 collective-permute-start.8
  155.3 50.6 %collective-permute-start.1 = (bf16[196,4,768]{2,1,0:T(4,128)(2,1)}, bf16[196,4,768]{2,1,0:T(4,128)(2,1)S(1)}, u32[]{:S(2)}, u32[]{:S(2)}) collective-permute-start(bf16[196,4,768]{2,1,0:T(4,128)(2,1)} %get-tuple-element.111), channel_id=1, source_target_pairs={{0,1},{1,0},{2,3},{3,2},{4,5},{5,4},{6,7},{7,6},{8,9},{9,8},{10,11... | collective-permute-start | bytes 3612680 | tf_op jit(solution)/shard_map/ppermute | solution.py:978
  156.9 49.1 %collective-permute-start.2 = (bf16[196,4,768]{2,1,0:T(4,128)(2,1)}, bf16[196,4,768]{2,1,0:T(4,128)(2,1)S(1)}, u32[]{:S(2)}, u32[]{:S(2)}) collective-permute-start(bf16[196,4,768]{2,1,0:T(4,128)(2,1)} %get-tuple-element.112), channel_id=1, source_target_pairs={{0,2},{1,3},{2,0},{3,1},{4,6},{5,7},{6,4},{7,5},{8,10},{9,11},{10,... | collective-permute-start | bytes 3612680 | tf_op jit(solution)/shard_map/ppermute | solution.py:978
  158.4 68.4 %collective-permute-start.3 = (bf16[196,4,768]{2,1,0:T(4,128)(2,1)}, bf16[196,4,768]{2,1,0:T(4,128)(2,1)}, u32[]{:S(2)}, u32[]{:S(2)}) collective-permute-start(bf16[196,4,768]{2,1,0:T(4,128)(2,1)} %get-tuple-element.113), channel_id=1, source_target_pairs={{0,3},{1,2},{2,1},{3,0},{4,7},{5,6},{6,5},{7,4},{8,11},{9,10},{10,... | collective-permute-start | bytes 3612680 | tf_op jit(solution)/shard_map/ppermute | solution.py:978
  205.9 20.9 %copy-start = (bf16[196,4,768]{2,1,0:T(4,128)(2,1)}, bf16[196,4,768]{2,1,0:T(4,128)(2,1)S(1)}, u32[]{:S(2)}) copy-start(bf16[196,4,768]{2,1,0:T(4,128)(2,1)S(1)} %collective-permute-done.1.refs_1_) | copy-start | bytes 3612676
  205.9 20.9 %copy-start.1 = (bf16[196,4,768]{2,1,0:T(4,128)(2,1)}, bf16[196,4,768]{2,1,0:T(4,128)(2,1)S(1)}, u32[]{:S(2)}) copy-start(bf16[196,4,768]{2,1,0:T(4,128)(2,1)S(1)} %collective-permute-done.2.refs_2_) | copy-start | bytes 3612676
  426.4 2.4 copy-start.2
  426.4 26.2 %collective-permute-start.10 = (bf16[196,4,768]{2,1,0:T(4,128)(2,1)}, bf16[196,4,768]{2,1,0:T(4,128)(2,1)}, u32[]{:S(2)}, u32[]{:S(2)}) collective-permute-start(bf16[196,4,768]{2,1,0:T(4,128)(2,1)} %get-tuple-element.136), channel_id=1, source_target_pairs={{0,1},{1,0},{2,3},{3,2},{4,5},{5,4},{6,7},{7,6},{8,9},{9,8},{10,11... | collective-permute-start | bytes 3612680 | tf_op jit(solution)/shard_map/ppermute | solution.py:978
  427.3 29.7 %collective-permute-start.9 = (bf16[196,4,768]{2,1,0:T(4,128)(2,1)}, bf16[196,4,768]{2,1,0:T(4,128)(2,1)}, u32[]{:S(2)}, u32[]{:S(2)}) collective-permute-start(bf16[196,4,768]{2,1,0:T(4,128)(2,1)} %get-tuple-element.130), channel_id=1, source_target_pairs={{0,2},{1,3},{2,0},{3,1},{4,6},{5,7},{6,4},{7,5},{8,10},{9,11},{10,... | collective-permute-start | bytes 3612680 | tf_op jit(solution)/shard_map/ppermute | solution.py:978
  428.8 71.4 %collective-permute-start.14 = (bf16[196,4,768]{2,1,0:T(4,128)(2,1)}, bf16[196,4,768]{2,1,0:T(4,128)(2,1)S(1)}, u32[]{:S(2)}, u32[]{:S(2)}) collective-permute-start(bf16[196,4,768]{2,1,0:T(4,128)(2,1)} %get-tuple-element.160), channel_id=1, source_target_pairs={{0,3},{1,2},{2,1},{3,0},{4,7},{5,6},{6,5},{7,4},{8,11},{9,10},{10,... | collective-permute-start | bytes 3612680 | tf_op jit(solution)/shard_map/ppermute | solution.py:978
  482.7 16.3 %copy-start.8 = (f32[1,3072]{1,0:T(1,128)S(1)}, f32[1,3072]{1,0:T(1,128)}, u32[]{:S(2)}) copy-start(f32[1,3072]{1,0:T(1,128)} %get-tuple-element.170) | copy-start | bytes 36868
  495.9 164.2 %collective-permute-start.11 = (bf16[196,4,768]{2,1,0:T(4,128)(2,1)}, bf16[196,4,768]{2,1,0:T(4,128)(2,1)S(1)}, u32[]{:S(2)}, u32[]{:S(2)}) collective-permute-start(bf16[196,4,768]{2,1,0:T(4,128)(2,1)} %get-tuple-element.156), channel_id=1, source_target_pairs={{0,1},{1,0},{2,3},{3,2},{4,5},{5,4},{6,7},{7,6},{8,9},{9,8},{10,11... | collective-permute-start | bytes 3612680 | tf_op jit(solution)/shard_map/ppermute | solution.py:978
  495.9 164.2 %collective-permute-start.12 = (bf16[196,4,768]{2,1,0:T(4,128)(2,1)}, bf16[196,4,768]{2,1,0:T(4,128)(2,1)}, u32[]{:S(2)}, u32[]{:S(2)}) collective-permute-start(bf16[196,4,768]{2,1,0:T(4,128)(2,1)} %get-tuple-element.157), channel_id=1, source_target_pairs={{0,2},{1,3},{2,0},{3,1},{4,6},{5,7},{6,4},{7,5},{8,10},{9,11},{10,... | collective-permute-start | bytes 3612680 | tf_op jit(solution)/shard_map/ppermute | solution.py:978
  497.5 162.7 %collective-permute-start.13 = (bf16[196,4,768]{2,1,0:T(4,128)(2,1)}, bf16[196,4,768]{2,1,0:T(4,128)(2,1)}, u32[]{:S(2)}, u32[]{:S(2)}) collective-permute-start(bf16[196,4,768]{2,1,0:T(4,128)(2,1)} %get-tuple-element.158), channel_id=1, source_target_pairs={{0,3},{1,2},{2,1},{3,0},{4,7},{5,6},{6,5},{7,4},{8,11},{9,10},{10,... | collective-permute-start | bytes 3612680 | tf_op jit(solution)/shard_map/ppermute | solution.py:978
  649.0 6.5 copy-start.4
  660.2 1.1 copy-start.3
Sparse Core Ops, SparseCore 0:
  11.5 83.1 all-gather.2
  98.2 115.6 all-gather.4
  426.5 214.5 reduce-scatter.1

commit v4 on v3

--- a/solution.py
+++ b/solution.py
@@ -372,7 +372,7 @@
     @pl.when(step == last)
     def _():
         moves = []
-        for source, start in ((d_up, 4 * D), (d_down, 4 * D + FF)):
+        for source, start in ((d_up, 0), (d_down, FF)):
             moves += [(source.at[:, c], d_ref.at[:, start + c.start : start + c.stop]) for c in chunks]
         flush(moves, stage, sems)
 
@@ -410,7 +410,7 @@
         out_shape=[jax.ShapeDtypeStruct(t.shape, BF16) for t in teachers]
         + [
             jax.ShapeDtypeStruct((tokens, D), F32),
-            jax.ShapeDtypeStruct((D, 4 * D + 2 * FF), BF16),
+            jax.ShapeDtypeStruct((D, 2 * FF), BF16),
             jax.ShapeDtypeStruct((3, D), F32),
             jax.ShapeDtypeStruct((1, FF), F32),
             jax.ShapeDtypeStruct((1, D), F32),
@@ -432,7 +432,7 @@
 
 
 def time_back_kernel(group, ring, *refs):
-    (g_ref, a_ref, in_ref, q_ref, k_ref, v_ref, mix_ref, p_ref, table, w_ref), refs = refs[:10], refs[11:]
+    (g_ref, a_ref, in_ref, q_ref, k_ref, v_ref, mix_ref, p_ref, table, w_ref), refs = refs[:10], refs[10:]
     outs, refs = refs[:ring], refs[ring:]
     d_ref, rows_ref, grad_mix, grad_proj, d_proj, d_out, stage, sems, scratch = refs
     step, last = pl.program_id(0), pl.num_programs(0) - 1
@@ -474,7 +474,7 @@
         flush(moves + [(d_out, d_ref.at[:, pl.ds(3 * D, D)])], stage, sems)
 
 
-def time_back(grad, saved, like, table, weights, matrix):
+def time_back(grad, saved, like, table, weights):
     ring, tokens = len(like), grad.shape[0]
     places, frames = like[0].shape[0], like[0].shape[1] * ring
     tile, group = time_tiles(places, frames)
@@ -487,12 +487,10 @@
             pl.BlockSpec((tile // group,) + kept(group), lambda i: (i, 0, 0, 0)),
             fixed(table.shape),
             columns_of(4 * D, 0),
-            pl.BlockSpec(memory_space=pl.ANY),
         ],
         out_specs=piece_specs(like, tile) + [pl.BlockSpec(memory_space=pl.ANY), fixed((5, D))],
         out_shape=[jax.ShapeDtypeStruct(t.shape, BF16) for t in like]
-        + [jax.ShapeDtypeStruct(matrix.shape, BF16), jax.ShapeDtypeStruct((5, D), F32)],
-        input_output_aliases={10: ring},
+        + [jax.ShapeDtypeStruct((D, 8 * D), BF16), jax.ShapeDtypeStruct((5, D), F32)],
         scratch_shapes=[
             pltpu.VMEM((tile, D), BF16),
             pltpu.VMEM((tile, 3 * D), BF16),
@@ -505,7 +503,7 @@
         compiler_params=PARAMS,
         cost_estimate=cost(42 * tokens * D * D),
         name="time_back",
-    )(grad, *saved, table, weights, matrix)
+    )(grad, *saved, table, weights)
     return outs, d_time, sums
 
 
@@ -567,7 +565,7 @@
 
 
 def space_weight_kernel(parts, in_ref, proj_ref, w_ref, table, c_ref, b_ref, up_ref, square_ref, *refs):
-    outs, biases, refs = refs[:parts], refs[parts : 2 * parts], refs[2 * parts :]
+    outs, biases, refs = refs[:parts], refs[parts : 2 * parts], refs[2 * parts + 1 :]
     d_ref, small_ref, d_proj, d_out, sums, rows, stage, sems = refs
     step, last = pl.program_id(0), pl.num_programs(0) - 1
     clear(step == 0, d_proj, sums, rows)
@@ -578,8 +576,8 @@
     @pl.when(step == last)
     def _():
         d_out[...] = sum(ref[...] for ref in outs)
-        moves = [(d_proj.at[:, pl.ds(c * D, D)], d_ref.at[:, pl.ds(c * D, D)]) for c in range(3)]
-        flush(moves + [(d_out, d_ref.at[:, pl.ds(3 * D, D)])], stage, sems)
+        moves = [(d_proj.at[:, pl.ds(c * D, D)], d_ref.at[:, pl.ds((4 + c) * D, D)]) for c in range(3)]
+        flush(moves + [(d_out, d_ref.at[:, pl.ds(7 * D, D)])], stage, sems)
         many = up_ref.shape[0]
         rows[1:2, :], rows[2:3, :] = b_ref[0:1, :], c_ref[0:1, :]
         rows[4:5, :], rows[5:6, :] = b_ref[1:2, :], c_ref[1:2, :]
@@ -602,7 +600,7 @@
         small_ref[...] = jnp.where(lane == 0, gain_grad, jnp.where(lane == 3, shift_grad, columns))
 
 
-def space_weights(ins, projs, weights, table, rows_c, rows_b, bias_up, squares, outs, biases):
+def space_weights(ins, projs, weights, table, rows_c, rows_b, bias_up, squares, outs, biases, matrix):
     batch, frames, full, _ = ins.shape
 
     def clip(width):
@@ -615,9 +613,11 @@
         in_specs=[clip(D), clip(3 * D), columns_of(3 * D, 0)]
         + [fixed(a.shape) for a in smalls]
         + [fixed((D, D))] * batch
-        + [fixed((1, D))] * batch,
+        + [fixed((1, D))] * batch
+        + [pl.BlockSpec(memory_space=pl.ANY)],
         out_specs=[pl.BlockSpec(memory_space=pl.ANY), fixed((D, SMALL))],
-        out_shape=[jax.ShapeDtypeStruct((D, 4 * D), BF16), jax.ShapeDtypeStruct((D, SMALL), F32)],
+        out_shape=[jax.ShapeDtypeStruct(matrix.shape, BF16), jax.ShapeDtypeStruct((D, SMALL), F32)],
+        input_output_aliases={8 + 2 * batch: 0},
         scratch_shapes=[
             pltpu.VMEM((D, 3 * D), F32),
             pltpu.VMEM((D, D), F32),
@@ -629,42 +629,7 @@
         compiler_params=PARAMS,
         cost_estimate=cost(18 * batch * frames * full * D * D),
         name="space_weights",
-    )(ins, projs, weights, *smalls, *outs, *biases)
-
-
-def input_kernel(clip, g_ref, p_ref, x_ref, table, w_ref, *refs):
-    out_ref = refs[-1]
-    back = dot_nt(p_ref[0, 0, : g_ref.shape[1], :], w_ref[...])
-    hat, inverse = normalize(x_ref[0, 0].astype(F32))
-    grad = g_ref[0].astype(F32) + normalize_back(back, hat, inverse, table[GAIN : GAIN + 1, :])
-    out_ref[0, 0] = grad.astype(BF16)
-
-
-def input_grads(clip, step, grad, projs, inputs, table, weights, before):
-    frames, places, _ = grad.shape
-    block = pl.BlockSpec((1, 1, places, D), lambda i, c: (c[0], i, 0, 0))
-    more = [] if before is None else [before]
-    return pl.pallas_call(
-        input_kernel,
-        grid_spec=pltpu.PrefetchScalarGridSpec(
-            num_scalar_prefetch=1,
-            grid=(frames,),
-            in_specs=[
-                pl.BlockSpec((1, places, D), lambda i, c: (i, 0, 0)),
-                pl.BlockSpec((1, 1) + projs.shape[2:], lambda i, c: (step, i, 0, 0)),
-                block,
-                fixed(table.shape),
-                columns_of(3 * D, 0),
-            ]
-            + [pl.BlockSpec(memory_space=pl.ANY) for _ in more],
-            out_specs=block,
-        ),
-        out_shape=jax.ShapeDtypeStruct(inputs.shape, BF16),
-        input_output_aliases={6: 0} if more else {},
-        compiler_params=PARAMS,
-        cost_estimate=cost(18 * frames * places * D * D),
-        name="input_grads",
-    )(clip, grad, projs, inputs, table, weights, *more)
+    )(ins, projs, weights, *smalls, *outs, *biases, matrix)
 
 
 def place_kernel(order, *refs):
@@ -804,7 +769,65 @@
     return out.reshape(-1, block.shape[1])
 
 
-def reduce_kernel(depth, height, part_ref, small_ref, out_ref, out_small, *refs):
+def turned(number, flips, size):
+    total, bit = 0, 1
+    while bit < size:
+        value = (number // bit) % 2
+        total = total + bit * (1 - value if flips & bit else value)
+        bit *= 2
+    return total
+
+
+def reduce_kernel(depth, height, many, batch, part_ref, small_ref, projs, x_ref, table, all_w, *refs):
+    grads, outs, refs = refs[:batch], refs[batch : batch + many], refs[batch + many :]
+    out_small, dx_ref, refs = refs[0], refs[1], refs[2:]
+    refs, (p_buf, g_buf, x_buf, o_buf, i_sems, o_sems, w_ref, w_sem) = refs[:-8], refs[-8:]
+    weights = pltpu.make_async_copy(all_w.at[:, pl.ds(0, 3 * D)], w_ref, w_sem)
+    weights.start()
+    frames, places = x_ref.shape[1], x_ref.shape[2]
+    group = lax.axis_index("frame") // (lax.axis_size("frame") // batch)
+
+    def input_grads(j):
+        clip = turned(group, j, batch)
+
+        def loads(f, slot):
+            return [
+                pltpu.make_async_copy(projs.at[j, f], p_buf.at[slot], i_sems.at[slot, 0]),
+                pltpu.make_async_copy(grads[j].at[f], g_buf.at[slot], i_sems.at[slot, 1]),
+                pltpu.make_async_copy(x_ref.at[clip, f], x_buf.at[slot], i_sems.at[slot, 2]),
+            ]
+
+        def store(f, slot):
+            return pltpu.make_async_copy(o_buf.at[slot], dx_ref.at[clip, f], o_sems.at[slot])
+
+        def one(f, carry):
+            slot = lax.rem(f, 2)
+
+            @pl.when(f + 1 < frames)
+            def _():
+                for copy in loads(f + 1, 1 - slot):
+                    copy.start()
+
+            for copy in loads(f, slot):
+                copy.wait()
+
+            @pl.when(f >= 2)
+            def _():
+                store(f - 2, slot).wait()
+
+            back = dot_nt(p_buf[slot, :places, :], w_ref[...])
+            hat, inverse = normalize(x_buf[slot].astype(F32))
+            grad = g_buf[slot].astype(F32) + normalize_back(back, hat, inverse, table[GAIN : GAIN + 1, :])
+            o_buf[slot] = grad.astype(BF16)
+            store(f, slot).start()
+            return carry
+
+        for copy in loads(0, 0):
+            copy.start()
+        lax.fori_loop(0, frames, one, 0)
+        for f in range(max(frames - 2, 0), frames):
+            store(f, f % 2).wait()
+
     own, from_core, to_x, from_x, to_z, from_z, to_y, from_y = refs[:8]
     low_core, low_to_x, low_x, low_to_z, low_z, low_to_y, low_y = refs[8:15]
     c_send, c_recv, x_send, x_recv, z_send, z_recv, y_send, y_recv = refs[15:23]
@@ -859,7 +882,10 @@
     for zz in range(depth):
         low_to_x[zz] = small_ref[2 * zz + 1 - x, :, core] + low_core[2 * zz + 1 - x]
     low_xc = start(remote(low_to_x, low_x, lx_send, lx_recv, x_device))
+    weights.wait()
     for n, d in enumerate(order):
+        for j in range(n * batch // depth, (n + 1) * batch // depth):
+            input_grads(j)
         mine[depth + n].wait()
         c_copies[depth + n].wait_recv()
         x_copies[n].wait_recv()
@@ -902,23 +928,29 @@
         yy, to = lax.rem(y + height - d, height), device(z, x, lax.rem(y + d, height), core)
         remote(to_y.at[d], from_y.at[yy], y_send.at[d], y_recv.at[yy], to).wait_recv()
         remote(low_to_y.at[d], low_y.at[yy], ly_send.at[d], ly_recv.at[yy], to).wait_recv()
-    out_ref[...] = over(from_y)
+    total, at = over(from_y), 0
+    for ref in outs:
+        ref[...] = total[:, at : at + ref.shape[1]]
+        at += ref.shape[1]
     out_small[...] = over(low_y)
     for copy in sent:
         copy.wait_send()
 
 
-def reduce_rows(block, small):
+def reduce_rows(block, small, widths, projs, grads, inputs, table, weights):
     clips, frames = lax.axis_size("clip"), lax.axis_size("frame")
     depth, height = clips // 2, frames // 2
     rows = block.shape[0] // (clips * frames)
     sems, tail, low = pltpu.SemaphoreType.DMA, (rows, block.shape[1]), (rows, small.shape[1])
     lead = (clips, height, 2)
+    hbm, vmem = pl.BlockSpec(memory_space=pl.ANY), pl.BlockSpec(memory_space=pltpu.VMEM)
+    frame = (2,) + inputs.shape[2:]
     return pl.pallas_call(
-        functools.partial(reduce_kernel, depth, height),
-        in_specs=[pl.BlockSpec(memory_space=pl.ANY), pl.BlockSpec(memory_space=pltpu.VMEM)],
-        out_specs=[pl.BlockSpec(memory_space=pltpu.VMEM)] * 2,
-        out_shape=[jax.ShapeDtypeStruct(tail, F32), jax.ShapeDtypeStruct(low, F32)],
+        functools.partial(reduce_kernel, depth, height, len(widths), len(grads)),
+        in_specs=[hbm, vmem, hbm, hbm, vmem, hbm] + [hbm] * len(grads),
+        out_specs=[vmem] * (len(widths) + 1) + [hbm],
+        out_shape=[jax.ShapeDtypeStruct((rows, width), F32) for width in (*widths, small.shape[1])]
+        + [jax.ShapeDtypeStruct(inputs.shape, BF16)],
         scratch_shapes=[
             pltpu.VMEM((2 * depth, height) + tail, BF16),
             pltpu.VMEM((2 * depth, height) + tail, BF16),
@@ -944,12 +976,19 @@
             sems((depth,)), sems((depth,)),
             sems((height,)), sems((height,)),
             sems((2 * depth,)),
+            pltpu.VMEM((2,) + projs.shape[2:], BF16),
+            pltpu.VMEM(frame, BF16),
+            pltpu.VMEM(frame, BF16),
+            pltpu.VMEM(frame, BF16),
+            sems((2, 3)), sems((2,)),
+            pltpu.VMEM((D, 3 * D), BF16),
+            sems,
         ],
         compiler_params=pltpu.CompilerParams(
             collective_id=1, has_side_effects=True, vmem_limit_bytes=60 << 20
         ),
         name="reduce_rows",
-    )(block.reshape(lead + tail), small.reshape(lead + low))
+    )(block.reshape(lead + tail), small.reshape(lead + low), projs, inputs, table, weights, *grads)
 
 
 def gather(block):
@@ -1033,7 +1072,7 @@
         after = jnp.swapaxes(after, 0, 1)
         if turn == 0:
             after, to_feed = lax.optimization_barrier((after, to_feed))
-        if j == 0:
+        if turn == 1:
             cuts, after = lax.optimization_barrier((cuts, after))
         for r in range(pieces):
             step = j * pieces + r
@@ -1045,9 +1084,8 @@
     layer_parts, grad_b, d_feed, rows_c, bias_up, squares = feed_forward(
         after_b, teachers, valid_column, scale, table, up_row, feed_weights, tile
     )
-    grad_parts, d_rest, rows_b = time_back(grad_b, saved_b, sent, table, time_weights, d_feed)
-    d_rest = scatter(d_rest)
-    d_time, d_feed = d_rest[:, : 4 * D], d_rest[:, 4 * D :]
+    d_feed = scatter(d_feed)
+    grad_parts, d_both, rows_b = time_back(grad_b, saved_b, sent, table, time_weights)
     grad_parts = [swap(part, step) for step, part in enumerate(grad_parts)]
 
     def join(parts, j):
@@ -1059,23 +1097,26 @@
             whole = lax.dynamic_update_slice_in_dim(whole, parts[step], place_of(step), 0)
         return whole
 
-    outs, biases, projs, input_grad = [], [], None, None
+    outs, biases, projs = [], [], None
     grads = [jnp.swapaxes(join(grad_parts, 0), 0, 1)] + [None] * (batch - 1)
     for j in range(batch):
         projs, d_out, bias = space_back(grads[j], j, batch, saved[j], first, projs)
         outs.append(d_out)
         biases.append(bias)
-        if j == batch // 2:
+        if j == batch - 1:
             projs, layer_parts = lax.optimization_barrier((projs, layer_parts))
             layer_parts = [swap(part, step) for step, part in enumerate(layer_parts)]
         if j + 1 < batch:
-            following = jnp.swapaxes(join(grad_parts, j + 1), 0, 1)
-            grads[j + 1] = following
-        input_grad = input_grads(clip_ids[j], j, grads[j], projs, clips_in, table, first, input_grad)
-    d_space, small = space_weights(
-        ins, projs, first, table, rows_c, rows_b, bias_up.reshape(many, D), squares, outs, biases
+            following = join(grad_parts, j + 1)
+            if j:
+                projs, following = lax.optimization_barrier((projs, following))
+            grads[j + 1] = jnp.swapaxes(following, 0, 1)
+    d_both, small = space_weights(
+        ins, projs, first, table, rows_c, rows_b, bias_up.reshape(many, D), squares, outs, biases, d_both
     )
-    d_space, here = reduce_rows(d_space, small)
+    d_time, d_time_out, d_space, d_space_out, here, input_grad = reduce_rows(
+        d_both, small, (3 * D, D, 3 * D, D), projs, grads, clips_in, table, first
+    )
     layer_out = place_clips(jnp.stack(order), [join(layer_parts, j) for j in range(batch)])
     d_up = jnp.swapaxes(d_feed[:, :FF].reshape(depth, many, D), 1, 2).reshape(depth, FF)
     return (
@@ -1084,13 +1125,13 @@
         input_grad,
         here[:, 0:3],
         here[:, 3:6],
-        d_space[:, : 3 * D],
+        d_space,
         here[:, 6:9],
         here[:, 9],
-        d_space[:, 3 * D : 4 * D],
+        d_space_out,
         here[:, 10:13],
-        d_time[:, : 3 * D].astype(F32),
-        d_time[:, 3 * D :].astype(F32),
+        d_time,
+        d_time_out,
         d_up.astype(F32),
         here[:, 13 : 13 + many].reshape(-1),
         d_feed[:, FF:].reshape(-1, D).astype(F32),

time: 682 us -> 677 us (level)
  waiting for transfers between devices: 24.5 us -> 56 us
  Pallas kernels: 556 us -> 528 us
    ppermute x15, waiting for transfers between devices: 24.5 us -> 56 us  [swap(): return lax.ppermute(block, 'frame', [(i, i ^ step) for i in range(ring)])]
    pallas_call x5 -> x1, Pallas kernels: 120 us -> 93.7 us  [reduce_rows(): pl.pallas_call(functools.partial(reduce_kernel, depth, height, len(widths...]
    unnamed x32 -> x60, local copies, waits for them, and re-layouts: 20.6 us -> 21 us
  transfers between devices with their start and end apart: 18 -> 18, of which waited for: 4 -> 4; matrix products, arithmetic and copies ran while one was open for 9% -> 8% of each run, Pallas kernels for 52% -> 59%
where the time goes in v4:
time: 677 us; the launch traced here: 676 us
  Pallas kernels  528 us (78%)
  waiting for transfers between devices  56 us (8%)
  local copies, waits for them, and re-layouts  52.1 us (8%)
  between operations  20.1 us (3%)
  starting transfers between devices  11.1 us (2%)
  other arithmetic  8.38 us (1%)
    pallas_call x1, Pallas kernels, feed_forward(): pl.pallas_call(functools.partial(feed_kernel, ring), grid=(tokens // tile...  133 us
    pallas_call x1, Pallas kernels, reduce_rows(): pl.pallas_call(functools.partial(reduce_kernel, depth, height, len(widths...  93.7 us
    pallas_call x1, Pallas kernels, time_back(): pl.pallas_call(functools.partial(time_back_kernel, group, ring), grid=(to...  66.8 us
    ppermute x15, waiting for transfers between devices, swap(): return lax.ppermute(block, 'frame', [(i, i ^ step) for i in range(ring)])  56 us
    pallas_call x4, Pallas kernels, space_forward(): pl.pallas_call(space_kernel, grid_spec=pltpu.PrefetchScalarGridSpec(num_s...  54.6 us
    pallas_call x1, Pallas kernels, gather_rows(): pl.pallas_call(functools.partial(gather_kernel, depth, height), in_specs=...  52.6 us
    pallas_call x4, Pallas kernels, space_back(): pl.pallas_call(space_back_kernel, grid=(frames,), in_specs=[frame(places,...  51.9 us
    pallas_call x1, Pallas kernels, time_forward(): pl.pallas_call(functools.partial(time_kernel, frames, group, len(parts)),...  41.4 us
  transfers between devices with their start and end apart: 18, of which 4 were waited for; matrix products, arithmetic and copies ran while one was open for 8% of the time, Pallas kernels for 59%

profile of v4, /device:TPU:0, one launch (start us, length us, event | category | flops | bytes accessed | tf_op | source)
XLA Modules:
  0.0 676.0 jit_solution(8607265495601122377)
XLA Ops:
  7.2 1.6 pad_maximum_fusion.1
  8.9 1.4 reduce_sum.27
  13.0 5.3 copy.115.x_ref
  19.0 0.7 fusion.1.in_ref
  19.6 52.6 %gather_rows.1 = bf16[8,2,2,24,3200]{4,3,2,1,0:T(8,128)(2,1)} custom-call(bf16[24,3200]{1,0:T(8,128)(2,1)} %fusion.1.in_ref), custom_call_target="tpu_custom_call" | custom-call | tf_op jit(solution)/shard_map/gather_rows/pallas_call | solution.py:754
  72.2 1.0 convert_bitcast_fusion
  73.2 0.8 copy.116.table.refs_4_.refs_7_.refs_8_
  74.0 13.5 %space_forward.4 = (bf16[4,4,208,768]{3,2,1,0:T(8,128)(2,1)}, bf16[4,196,768]{2,1,0:T(8,128)(2,1)}, bf16[4,196,768]{2,1,0:T(8,128)(2,1)}, bf16[4,196,768]{2,1,0:...) custom-call(s32[1]{0:T(128)} %bitcast.3.clip, ...), custom_call_target="tpu_custom_call" | custom-call | flops 693633024 | tf_op jit(solution)/shard_map/space_forward/pallas_call | solution.py:238
  87.4 1.8 copy.162
  90.3 0.7 pad_maximum_fusion
  91.1 1.6 collective-permute-start
  92.7 13.7 %space_forward.5 = (bf16[4,4,208,768]{3,2,1,0:T(8,128)(2,1)}, bf16[4,196,768]{2,1,0:T(8,128)(2,1)}, bf16[4,196,768]{2,1,0:T(8,128)(2,1)}, bf16[4,196,768]{2,1,0:...) custom-call(s32[1]{0:T(128)} %bitcast.2.clip, ...), custom_call_target="tpu_custom_call", output_to_operand_aliasing={{0}: (4, {})} | custom-call | flops 693633024 | tf_op jit(solution)/shard_map/space_forward/pallas_call | solution.py:238
  106.4 2.8 copy.161
  109.1 5.8 dynamic-slice_bitcast_fusion
  115.6 13.6 %space_forward.6 = (bf16[4,4,208,768]{3,2,1,0:T(8,128)(2,1)}, bf16[4,196,768]{2,1,0:T(8,128)(2,1)}, bf16[4,196,768]{2,1,0:T(8,128)(2,1)}, bf16[4,196,768]{2,1,0:...) custom-call(s32[1]{0:T(128)} %bitcast.clip, ...), custom_call_target="tpu_custom_call", output_to_operand_aliasing={{0}: (4, {})} | custom-call | flops 693633024 | tf_op jit(solution)/shard_map/space_forward/pallas_call | solution.py:238
  129.2 13.9 %space_forward.7 = (bf16[4,4,208,768]{3,2,1,0:T(8,128)(2,1)}, bf16[4,196,768]{2,1,0:T(8,128)(2,1)}, bf16[4,196,768]{2,1,0:T(8,128)(2,1)}, bf16[4,196,768]{2,1,0:...) custom-call(s32[1]{0:T(128)} %bitcast.1.clip, ...), custom_call_target="tpu_custom_call", output_to_operand_aliasing={{0}: (4, {})} | custom-call | flops 693633024 | tf_op jit(solution)/shard_map/space_forward/pallas_call | solution.py:238
  143.1 2.9 copy.159
  146.0 1.6 collective-permute-start.8
  148.1 3.4 collective-permute-done.8
  151.6 0.9 collective-permute-start.1
  152.4 1.5 collective-permute-start.2
  154.3 1.5 copy.160
  155.9 0.6 copy.146
  156.5 0.7 slice_reduce_fusion
  158.7 2.0 convert_element_type.43.refs_5_
  160.7 41.4 %time_forward.1 = (bf16[3136,768]{1,0:T(8,128)(2,1)}, bf16[3136,768]{1,0:T(8,128)(2,1)}, bf16[3136,768]{1,0:T(8,128)(2,1)}, bf16[3136,768]{1,0:T(8,128)(2,1)}, b...) custom-call(bf16[196,4,768]{2,1,0:T(4,128)(2,1)} %bitcast.107, ...), custom_call_target="tpu_custom_call" | custom-call | flops 2774532096 | tf_op jit(solution)/shard_map/time_forward/pallas_call | solution.py:310
  202.1 20.7 %collective-permute-done.3.refs_3_ = bf16[196,4,768]{2,1,0:T(4,128)(2,1)} collective-permute-done((bf16[196,4,768]{2,1,0:T(4,128)(2,1)}, bf16[196,4,768]{2,1,0:T(4,128)(2,1)}, u32[]{:S(2)}, u32[]{:S(2)}) %collective-permute-start.3) | collective-permute-done | bytes 1204256 | tf_op jit(solution)/shard_map/ppermute | solution.py:1017
  222.9 132.7 %feed_forward.1 = (bf16[196,4,768]{2,1,0:T(4,128)(2,1)}, bf16[196,4,768]{2,1,0:T(4,128)(2,1)}, bf16[196,4,768]{2,1,0:T(4,128)(2,1)}, bf16[196,4,768]{2,1,0:T(4,1...) custom-call(bf16[196,4,768]{2,1,0:T(4,128)(2,1)} %get-tuple-element., ...), custom_call_target="tpu_custom_call" | custom-call | flops 9248440320 | tf_op jit(solution)/shard_map/feed_forward/pallas_call | solution.py:395
  355.6 66.8 %time_back.1 = (bf16[196,4,768]{2,1,0:T(4,128)(2,1)}, bf16[196,4,768]{2,1,0:T(4,128)(2,1)}, bf16[196,4,768]{2,1,0:T(4,128)(2,1)}, bf16[196,4,768]{2,1,0:T(4,128)...) custom-call(f32[3136,768]{1,0:T(8,128)} %get-tuple-element.129.refs_0_, ...), custom_call_target="tpu_custom_call" | custom-call | flops 4855431168 | tf_op jit(solution)/shard_map/time_back/pallas_call | solution.py:482
  422.5 0.8 collective-permute-start.9
  423.3 1.5 collective-permute-start.10
  424.9 2.4 copy.157
  427.3 12.9 %space_back.4 = (bf16[4,4,208,2304]{3,2,1,0:T(8,128)(2,1)}, f32[768,768]{1,0:T(8,128)}, f32[1,768]{1,0:T(1,128)}) custom-call(bf16[4,196,768]{2,1,0:T(8,128)(2,1)} %bitcast.100, bf16[4,196,768]{2,1,0:T(8,128)(2,1)} %get-tuple-element.144.q_ref, bf16[4,196,768]{2,1,0:T(8,128)(2,1)} %get-tuple-element.145.k_ref, ...), custom_call_target="tpu_custom_call" | custom-call | flops 693633024 | tf_op jit(solution)/shard_map/space_back/pallas_call | solution.py:540
  440.2 1.2 copy.158
  441.4 13.0 %space_back.5 = (bf16[4,4,208,2304]{3,2,1,0:T(8,128)(2,1)}, f32[768,768]{1,0:T(8,128)}, f32[1,768]{1,0:T(1,128)}) custom-call(bf16[4,196,768]{2,1,0:T(8,128)(2,1)} %bitcast.94, bf16[4,196,768]{2,1,0:T(8,128)(2,1)} %get-tuple-element.138.q_ref, bf16[4,196,768]{2,1,0:T(8,128)(2,1)} %get-tuple-element.139.k_ref, ...), custom_call_target="tpu_custom_call", output_to_operand_aliasing={{0}: (7, {})} | custom-call | flops 693633024 | tf_op jit(solution)/shard_map/space_back/pallas_call | solution.py:540
  454.4 12.2 %collective-permute-done.10 = bf16[196,4,768]{2,1,0:T(4,128)(2,1)S(1)} collective-permute-done((bf16[196,4,768]{2,1,0:T(4,128)(2,1)}, bf16[196,4,768]{2,1,0:T(4,128)(2,1)S(1)}, u32[]{:S(2)}, u32[]{:S(2)}) %collective-permute-start.10) | collective-permute-done | bytes 1204256 | tf_op jit(solution)/shard_map/ppermute | solution.py:1017
  466.7 1.1 copy.156
  467.8 13.0 %space_back.6 = (bf16[4,4,208,2304]{3,2,1,0:T(8,128)(2,1)}, f32[768,768]{1,0:T(8,128)}, f32[1,768]{1,0:T(1,128)}) custom-call(bf16[4,196,768]{2,1,0:T(8,128)(2,1)} %bitcast.96, bf16[4,196,768]{2,1,0:T(8,128)(2,1)} %get-tuple-element.153.q_ref, bf16[4,196,768]{2,1,0:T(8,128)(2,1)} %get-tuple-element.154.k_ref, ...), custom_call_target="tpu_custom_call", output_to_operand_aliasing={{0}: (7, {})} | custom-call | flops 693633024 | tf_op jit(solution)/shard_map/space_back/pallas_call | solution.py:540
  480.8 19.5 %collective-permute-done.11 = bf16[196,4,768]{2,1,0:T(4,128)(2,1)S(1)} collective-permute-done((bf16[196,4,768]{2,1,0:T(4,128)(2,1)}, bf16[196,4,768]{2,1,0:T(4,128)(2,1)S(1)}, u32[]{:S(2)}, u32[]{:S(2)}) %collective-permute-start.11) | collective-permute-done | bytes 1204256 | tf_op jit(solution)/shard_map/ppermute | solution.py:1017
  500.3 1.2 copy.155
  501.5 13.0 %space_back.7 = (bf16[4,4,208,2304]{3,2,1,0:T(8,128)(2,1)}, f32[768,768]{1,0:T(8,128)}, f32[1,768]{1,0:T(1,128)}) custom-call(bf16[4,196,768]{2,1,0:T(8,128)(2,1)} %bitcast.98, bf16[4,196,768]{2,1,0:T(8,128)(2,1)} %get-tuple-element.162.q_ref, bf16[4,196,768]{2,1,0:T(8,128)(2,1)} %get-tuple-element.163.k_ref, ...), custom_call_target="tpu_custom_call", output_to_operand_aliasing={{0}: (7, {})} | custom-call | flops 693633024 | tf_op jit(solution)/shard_map/space_back/pallas_call | solution.py:540
  515.0 1.4 collective-permute-start.14
  517.5 0.7 reduce.7
  518.2 0.6 reshape.116.up_ref
  518.8 28.8 %space_weights.1 = (bf16[768,6144]{1,0:T(8,128)(2,1)}, f32[768,128]{1,0:T(8,128)}) custom-call(bf16[4,4,208,768]{3,2,1,0:T(8,128)(2,1)} %get-tuple-element.177.in_ref, bf16[4,4,208,2304]{3,2,1,0:T(8,128)(2,1)} %get-tuple-element.178.proj_ref.projs, bf16[768,3200]{1,0:T(8,128)(2,1)} %bitcast.91, ...), custom_call_target="tpu_custom_call", output_to_operand_aliasing={{0}: (16, {})} | custom-call | flops 2208301056 | tf_op jit(solution)/shard_map/space_weights/pallas_call | solution.py:610
  547.6 93.7 %reduce_rows.1 = (f32[24,2304]{1,0:T(8,128)}, f32[24,768]{1,0:T(8,128)}, f32[24,2304]{1,0:T(8,128)}, f32[24,768]{1,0:T(8,128)}, f32[24,128]{1,0:T(8,128)}, /*index=5*/bf16[4,4,196,768]{3,2,1,0:T(8,128)(2,1)}) custom-call(bf16[8,2,2,24,6144]{4,3,2,1,0:T(8,128)(2,1)} %bitcast.93, f32[8,2,2,24,128]{4,3,2,1,0:T(8,128)} %bitcast.110, ...), custom_call_target="tpu_custom_call" | custom-call | tf_op jit(solution)/shard_map/reduce_rows/pallas_call | solution.py:948
  641.3 1.3 slice.51
  642.6 0.8 slice.58
  644.0 6.5 copy.139
  650.6 0.7 copy.140
  651.2 0.7 copy.141
  651.9 0.7 copy.142
  652.5 0.7 copy.143
  653.8 0.7 slice_reduce_fusion.2
  654.5 1.0 copy-done.2
  655.9 5.7 place_clips.1
  661.6 1.0 slice_convert_fusion
  662.8 0.7 copy.138
  663.5 1.2 copy.144
  664.7 0.8 reshape.121
  665.5 0.7 copy.174
  666.2 0.6 copy.175
  666.8 0.7 copy.176
  667.5 0.6 copy.177
  (92 shorter events, 6.5 us)
Async XLA Ops:
  7.2 153.6 %all-gather.3.cloned.1.call-start = ((), (), s32[]{:S(2)}) async-start(), calls=%async_computation.1 | async-start | bytes 4866048 | tf_op jit(solution)/shard_map/all_gather | solution.py:995
  8.8 214.1 %all-gather.5.cloned.1.call-start = ((), (), s32[]{:S(2)}) async-start(), calls=%async_computation.2 | async-start | bytes 9732096 | tf_op jit(solution)/shard_map/all_gather | solution.py:995
  12.9 5.3 copy-start.15
  12.9 5.4 copy-start.16
  12.9 5.5 copy-start.17
  12.9 5.6 copy-start.18
  12.9 5.7 copy-start.19
  12.9 6.0 copy-start.9
  12.9 6.0 copy-start.13
  87.4 1.8 copy-start.8
  87.4 1.9 copy-start.7
  91.1 570.6 %reduce-scatter.2.cloned.1.call-start = ((), (), s32[]{:S(2)}) async-start(), calls=%async_computation.3 | async-start | bytes 9732096 | tf_op jit(solution)/shard_map/reduce_scatter | solution.py:999
  91.1 38.1 %collective-permute-start = (bf16[196,4,768]{2,1,0:T(4,128)(2,1)S(1)}, bf16[196,4,768]{2,1,0:T(4,128)(2,1)S(1)}, u32[]{:S(2)}, u32[]{:S(2)}) collective-permute-start(bf16[196,4,768]{2,1,0:T(4,128)(2,1)S(1)} %bitcast.106), channel_id=1, source_target_pairs={{0,3},{1,2},{2,1},{3,0},{4,7},{5,6},{6,5},{7,4},{8,11},{9,10},{10,... | collective-permute-start | bytes 3612680 | tf_op jit(solution)/shard_map/ppermute | solution.py:1017
  115.0 45.7 %collective-permute-start.5 = (bf16[196,4,768]{2,1,0:T(4,128)(2,1)}, bf16[196,4,768]{2,1,0:T(4,128)(2,1)}, u32[]{:S(2)}, u32[]{:S(2)}) collective-permute-start(bf16[196,4,768]{2,1,0:T(4,128)(2,1)} %bitcast.79), channel_id=1, source_target_pairs={{0,2},{1,3},{2,0},{3,1},{4,6},{5,7},{6,4},{7,5},{8,10},{9,11},{10,... | collective-permute-start | bytes 3612680 | tf_op jit(solution)/shard_map/ppermute | solution.py:1017
  129.2 13.9 %copy-start.20 = (bf16[196,4,768]{2,1,0:T(4,128)(2,1)}, bf16[196,4,768]{2,1,0:T(4,128)(2,1)S(1)}, u32[]{:S(2)}) copy-start(bf16[196,4,768]{2,1,0:T(4,128)(2,1)S(1)} %collective-permute-done.refs_3_) | copy-start | bytes 3612676
  143.1 2.9 copy-start.12
  143.1 11.2 %copy-start = (bf16[4,196,768]{2,1,0:T(8,128)(2,1)S(1)}, bf16[4,196,768]{2,1,0:T(8,128)(2,1)}, u32[]{:S(2)}) copy-start(bf16[4,196,768]{2,1,0:T(8,128)(2,1)} %get-tuple-element.122) | copy-start | bytes 3612676
  146.0 14.8 %collective-permute-start.4 = (bf16[196,4,768]{2,1,0:T(4,128)(2,1)}, bf16[196,4,768]{2,1,0:T(4,128)(2,1)}, u32[]{:S(2)}, u32[]{:S(2)}) collective-permute-start(bf16[196,4,768]{2,1,0:T(4,128)(2,1)} %bitcast.77), channel_id=1, source_target_pairs={{0,1},{1,0},{2,3},{3,2},{4,5},{5,4},{6,7},{7,6},{8,9},{9,8},{10,11... | collective-permute-start | bytes 3612680 | tf_op jit(solution)/shard_map/ppermute | solution.py:1017
  146.0 5.6 collective-permute-start.8
  147.6 4.9 collective-permute-start.7
  148.1 5.9 collective-permute-start.6
  151.6 50.6 %collective-permute-start.1 = (bf16[196,4,768]{2,1,0:T(4,128)(2,1)}, bf16[196,4,768]{2,1,0:T(4,128)(2,1)S(1)}, u32[]{:S(2)}, u32[]{:S(2)}) collective-permute-start(bf16[196,4,768]{2,1,0:T(4,128)(2,1)} %get-tuple-element.119), channel_id=1, source_target_pairs={{0,1},{1,0},{2,3},{3,2},{4,5},{5,4},{6,7},{7,6},{8,9},{9,8},{10,11... | collective-permute-start | bytes 3612680 | tf_op jit(solution)/shard_map/ppermute | solution.py:1017
  152.4 49.7 %collective-permute-start.2 = (bf16[196,4,768]{2,1,0:T(4,128)(2,1)}, bf16[196,4,768]{2,1,0:T(4,128)(2,1)}, u32[]{:S(2)}, u32[]{:S(2)}) collective-permute-start(bf16[196,4,768]{2,1,0:T(4,128)(2,1)} %get-tuple-element.120), channel_id=1, source_target_pairs={{0,2},{1,3},{2,0},{3,1},{4,6},{5,7},{6,4},{7,5},{8,10},{9,11},{10,... | collective-permute-start | bytes 3612680 | tf_op jit(solution)/shard_map/ppermute | solution.py:1017
  154.0 68.9 %collective-permute-start.3 = (bf16[196,4,768]{2,1,0:T(4,128)(2,1)}, bf16[196,4,768]{2,1,0:T(4,128)(2,1)}, u32[]{:S(2)}, u32[]{:S(2)}) collective-permute-start(bf16[196,4,768]{2,1,0:T(4,128)(2,1)} %get-tuple-element.121), channel_id=1, source_target_pairs={{0,3},{1,2},{2,1},{3,0},{4,7},{5,6},{6,5},{7,4},{8,11},{9,10},{10,... | collective-permute-start | bytes 3612680 | tf_op jit(solution)/shard_map/ppermute | solution.py:1017
  202.1 20.8 %copy-start.1 = (bf16[196,4,768]{2,1,0:T(4,128)(2,1)}, bf16[196,4,768]{2,1,0:T(4,128)(2,1)S(1)}, u32[]{:S(2)}) copy-start(bf16[196,4,768]{2,1,0:T(4,128)(2,1)S(1)} %collective-permute-done.1.refs_1_) | copy-start | bytes 3612676
  422.5 17.7 %collective-permute-start.9 = (bf16[196,4,768]{2,1,0:T(4,128)(2,1)}, bf16[196,4,768]{2,1,0:T(4,128)(2,1)S(1)}, u32[]{:S(2)}, u32[]{:S(2)}) collective-permute-start(bf16[196,4,768]{2,1,0:T(4,128)(2,1)} %get-tuple-element.137), channel_id=1, source_target_pairs={{0,1},{1,0},{2,3},{3,2},{4,5},{5,4},{6,7},{7,6},{8,9},{9,8},{10,11... | collective-permute-start | bytes 3612680 | tf_op jit(solution)/shard_map/ppermute | solution.py:1017
  423.3 43.4 %collective-permute-start.10 = (bf16[196,4,768]{2,1,0:T(4,128)(2,1)}, bf16[196,4,768]{2,1,0:T(4,128)(2,1)S(1)}, u32[]{:S(2)}, u32[]{:S(2)}) collective-permute-start(bf16[196,4,768]{2,1,0:T(4,128)(2,1)} %get-tuple-element.151), channel_id=1, source_target_pairs={{0,2},{1,3},{2,0},{3,1},{4,6},{5,7},{6,4},{7,5},{8,10},{9,11},{10,... | collective-permute-start | bytes 3612680 | tf_op jit(solution)/shard_map/ppermute | solution.py:1017
  424.9 75.5 %collective-permute-start.11 = (bf16[196,4,768]{2,1,0:T(4,128)(2,1)}, bf16[196,4,768]{2,1,0:T(4,128)(2,1)S(1)}, u32[]{:S(2)}, u32[]{:S(2)}) collective-permute-start(bf16[196,4,768]{2,1,0:T(4,128)(2,1)} %get-tuple-element.160), channel_id=1, source_target_pairs={{0,3},{1,2},{2,1},{3,0},{4,7},{5,6},{6,5},{7,4},{8,11},{9,10},{10,... | collective-permute-start | bytes 3612680 | tf_op jit(solution)/shard_map/ppermute | solution.py:1017
  501.5 16.0 %copy-start.14 = (f32[1,3072]{1,0:T(1,128)S(1)}, f32[1,3072]{1,0:T(1,128)}, u32[]{:S(2)}) copy-start(f32[1,3072]{1,0:T(1,128)} %get-tuple-element.181) | copy-start | bytes 36868
  514.5 140.0 %collective-permute-start.12 = (bf16[196,4,768]{2,1,0:T(4,128)(2,1)}, bf16[196,4,768]{2,1,0:T(4,128)(2,1)S(1)}, u32[]{:S(2)}, u32[]{:S(2)}) collective-permute-start(bf16[196,4,768]{2,1,0:T(4,128)(2,1)} %get-tuple-element.174), channel_id=1, source_target_pairs={{0,1},{1,0},{2,3},{3,2},{4,5},{5,4},{6,7},{7,6},{8,9},{9,8},{10,11... | collective-permute-start | bytes 3612680 | tf_op jit(solution)/shard_map/ppermute | solution.py:1017
  515.0 139.5 %collective-permute-start.13 = (bf16[196,4,768]{2,1,0:T(4,128)(2,1)}, bf16[196,4,768]{2,1,0:T(4,128)(2,1)S(1)}, u32[]{:S(2)}, u32[]{:S(2)}) collective-permute-start(bf16[196,4,768]{2,1,0:T(4,128)(2,1)} %get-tuple-element.175), channel_id=1, source_target_pairs={{0,2},{1,3},{2,0},{3,1},{4,6},{5,7},{6,4},{7,5},{8,10},{9,11},{10,... | collective-permute-start | bytes 3612680 | tf_op jit(solution)/shard_map/ppermute | solution.py:1017
  515.0 139.5 %collective-permute-start.14 = (bf16[196,4,768]{2,1,0:T(4,128)(2,1)}, bf16[196,4,768]{2,1,0:T(4,128)(2,1)}, u32[]{:S(2)}, u32[]{:S(2)}) collective-permute-start(bf16[196,4,768]{2,1,0:T(4,128)(2,1)} %get-tuple-element.176), channel_id=1, source_target_pairs={{0,3},{1,2},{2,1},{3,0},{4,7},{5,6},{6,5},{7,4},{8,11},{9,10},{10,... | collective-permute-start | bytes 3612680 | tf_op jit(solution)/shard_map/ppermute | solution.py:1017
  644.0 6.5 copy-start.4
  654.5 1.0 copy-start.2
  654.5 1.4 copy-start.3
  663.5 2.0 copy-start.6
  663.5 2.7 copy-start.11
  663.5 3.3 copy-start.5
  664.7 2.8 copy-start.10
Sparse Core Ops, SparseCore 0:
  11.5 84.7 all-gather.2
  99.8 109.6 all-gather.4
  355.8 169.6 reduce-scatter.1

commit v5 on v4

--- a/solution.py
+++ b/solution.py
@@ -564,16 +564,40 @@
 SMALL = 128
 
 
-def space_weight_kernel(parts, in_ref, proj_ref, w_ref, table, c_ref, b_ref, up_ref, square_ref, *refs):
-    outs, biases, refs = refs[:parts], refs[parts : 2 * parts], refs[2 * parts + 1 :]
-    d_ref, small_ref, d_proj, d_out, sums, rows, stage, sems = refs
-    step, last = pl.program_id(0), pl.num_programs(0) - 1
-    clear(step == 0, d_proj, sums, rows)
+def space_part_kernel(in_ref, proj_ref, d_proj, sums):
+    clear(pl.program_id(0) == 0, d_proj, sums)
     proj = proj_ref[0].reshape(-1, 3 * D)
     d_proj[...] += dot_tn(in_ref[0].reshape(-1, D), proj)
     sums[...] += column_sum(proj.astype(F32))
 
-    @pl.when(step == last)
+
+def space_part(ins, projs):
+    batch, frames, full, _ = ins.shape
+
+    def clip(width):
+        return pl.BlockSpec((1, frames, full, width), lambda i: (i, 0, 0, 0))
+
+    return pl.pallas_call(
+        space_part_kernel,
+        grid=(batch - 1,),
+        in_specs=[clip(D), clip(3 * D)],
+        out_specs=[fixed((D, 3 * D)), fixed((1, 3 * D))],
+        out_shape=[jax.ShapeDtypeStruct((D, 3 * D), F32), jax.ShapeDtypeStruct((1, 3 * D), F32)],
+        compiler_params=PARAMS,
+        cost_estimate=cost(18 * (batch - 1) * frames * full * D * D),
+        name="space_part",
+    )(ins, projs)
+
+
+def space_weight_kernel(parts, in_ref, proj_ref, d_before, sums_before, w_ref, table, c_ref, b_ref, up_ref, square_ref, *refs):
+    outs, biases, refs = refs[:parts], refs[parts : 2 * parts], refs[2 * parts + 1 :]
+    d_ref, small_ref, d_proj, d_out, sums, rows, stage, sems = refs
+    rows[...] = jnp.zeros_like(rows)
+    proj = proj_ref[0].reshape(-1, 3 * D)
+    d_proj[...] = d_before[...] + dot_tn(in_ref[0].reshape(-1, D), proj)
+    sums[...] = sums_before[...] + column_sum(proj.astype(F32))
+
+    @pl.when(pl.program_id(0) == 0)
     def _():
         d_out[...] = sum(ref[...] for ref in outs)
         moves = [(d_proj.at[:, pl.ds(c * D, D)], d_ref.at[:, pl.ds((4 + c) * D, D)]) for c in range(3)]
@@ -600,24 +624,24 @@
         small_ref[...] = jnp.where(lane == 0, gain_grad, jnp.where(lane == 3, shift_grad, columns))
 
 
-def space_weights(ins, projs, weights, table, rows_c, rows_b, bias_up, squares, outs, biases, matrix):
+def space_weights(ins, projs, before, weights, table, rows_c, rows_b, bias_up, squares, outs, biases, matrix):
     batch, frames, full, _ = ins.shape
 
     def clip(width):
-        return pl.BlockSpec((1, frames, full, width), lambda i: (i, 0, 0, 0))
+        return pl.BlockSpec((1, frames, full, width), lambda i: (batch - 1, 0, 0, 0))
 
     smalls = [table, rows_c, rows_b, bias_up, squares]
     return pl.pallas_call(
         functools.partial(space_weight_kernel, batch),
-        grid=(batch,),
-        in_specs=[clip(D), clip(3 * D), columns_of(3 * D, 0)]
+        grid=(1,),
+        in_specs=[clip(D), clip(3 * D), fixed((D, 3 * D)), fixed((1, 3 * D)), columns_of(3 * D, 0)]
         + [fixed(a.shape) for a in smalls]
         + [fixed((D, D))] * batch
         + [fixed((1, D))] * batch
         + [pl.BlockSpec(memory_space=pl.ANY)],
         out_specs=[pl.BlockSpec(memory_space=pl.ANY), fixed((D, SMALL))],
         out_shape=[jax.ShapeDtypeStruct(matrix.shape, BF16), jax.ShapeDtypeStruct((D, SMALL), F32)],
-        input_output_aliases={8 + 2 * batch: 0},
+        input_output_aliases={10 + 2 * batch: 0},
         scratch_shapes=[
             pltpu.VMEM((D, 3 * D), F32),
             pltpu.VMEM((D, D), F32),
@@ -627,9 +651,9 @@
             pltpu.SemaphoreType.DMA((2,)),
         ],
         compiler_params=PARAMS,
-        cost_estimate=cost(18 * batch * frames * full * D * D),
+        cost_estimate=cost(18 * frames * full * D * D),
         name="space_weights",
-    )(ins, projs, weights, *smalls, *outs, *biases, matrix)
+    )(ins, projs, *before, weights, *smalls, *outs, *biases, matrix)
 
 
 def place_kernel(order, *refs):
@@ -1100,6 +1124,9 @@
     outs, biases, projs = [], [], None
     grads = [jnp.swapaxes(join(grad_parts, 0), 0, 1)] + [None] * (batch - 1)
     for j in range(batch):
+        if j == batch - 1:
+            before = space_part(ins, projs)
+            projs, *before = lax.optimization_barrier((projs, *before))
         projs, d_out, bias = space_back(grads[j], j, batch, saved[j], first, projs)
         outs.append(d_out)
         biases.append(bias)
@@ -1112,7 +1139,7 @@
                 projs, following = lax.optimization_barrier((projs, following))
             grads[j + 1] = jnp.swapaxes(following, 0, 1)
     d_both, small = space_weights(
-        ins, projs, first, table, rows_c, rows_b, bias_up.reshape(many, D), squares, outs, biases, d_both
+        ins, projs, before, first, table, rows_c, rows_b, bias_up.reshape(many, D), squares, outs, biases, d_both
     )
     d_time, d_time_out, d_space, d_space_out, here, input_grad = reduce_rows(
         d_both, small, (3 * D, D, 3 * D, D), projs, grads, clips_in, table, first

time: 677 us -> 682 us (level)
  Pallas kernels: 528 us -> 535 us
    pallas_call x1 -> x2, Pallas kernels: 28.8 us -> 34.6 us  [the longest x1 17.5 us: space_part(): pl.pallas_call(space_part_kernel, grid=(batch - 1,), in_specs=[clip(D), c...]
  transfers between devices with their start and end apart: 18 -> 18, of which waited for: 4 -> 4; matrix products, arithmetic and copies ran while one was open for 8% -> 7% of each run, Pallas kernels for 59% -> 59%
where the time goes in v5:
time: 682 us
  Pallas kernels  535 us (78%)
  waiting for transfers between devices  55.6 us (8%)
  local copies, waits for them, and re-layouts  52.1 us (8%)
  between operations  20.2 us (3%)
  starting transfers between devices  11 us (2%)
  other arithmetic  8.44 us (1%)
    pallas_call x1, Pallas kernels, feed_forward(): pl.pallas_call(functools.partial(feed_kernel, ring), grid=(tokens // tile...  133 us
    pallas_call x1, Pallas kernels, reduce_rows(): pl.pallas_call(functools.partial(reduce_kernel, depth, height, len(widths...  93.7 us
    pallas_call x1, Pallas kernels, time_back(): pl.pallas_call(functools.partial(time_back_kernel, group, ring), grid=(to...  66.9 us
    ppermute x15, waiting for transfers between devices, swap(): return lax.ppermute(block, 'frame', [(i, i ^ step) for i in range(ring)])  55.6 us
    pallas_call x4, Pallas kernels, space_forward(): pl.pallas_call(space_kernel, grid_spec=pltpu.PrefetchScalarGridSpec(num_s...  54.8 us
    pallas_call x4, Pallas kernels, space_back(): pl.pallas_call(space_back_kernel, grid=(frames,), in_specs=[frame(places,...  52.4 us
    pallas_call x1, Pallas kernels, gather_rows(): pl.pallas_call(functools.partial(gather_kernel, depth, height), in_specs=...  52.4 us
    pallas_call x1, Pallas kernels, time_forward(): pl.pallas_call(functools.partial(time_kernel, frames, group, len(parts)),...  41.7 us
  transfers between devices with their start and end apart: 18, of which 4 were waited for; matrix products, arithmetic and copies ran while one was open for 7% of the time, Pallas kernels for 59%

profile of v5, /device:TPU:0, one launch (start us, length us, event | category | flops | bytes accessed | tf_op | source)
XLA Modules:
  0.0 682.3 jit_solution(11488083798707905340)
XLA Ops:
  7.2 1.6 pad_maximum_fusion.1
  8.9 1.4 reduce_sum.27
  13.0 5.3 copy.115.x_ref
  19.0 0.7 fusion.1.in_ref
  19.7 52.4 %gather_rows.1 = bf16[8,2,2,24,3200]{4,3,2,1,0:T(8,128)(2,1)} custom-call(bf16[24,3200]{1,0:T(8,128)(2,1)} %fusion.1.in_ref), custom_call_target="tpu_custom_call" | custom-call | tf_op jit(solution)/shard_map/gather_rows/pallas_call | solution.py:778
  72.1 1.0 convert_bitcast_fusion
  73.0 0.8 copy.116.table.refs_4_.refs_7_.refs_8_
  73.8 13.5 %space_forward.4 = (bf16[4,4,208,768]{3,2,1,0:T(8,128)(2,1)}, bf16[4,196,768]{2,1,0:T(8,128)(2,1)}, bf16[4,196,768]{2,1,0:T(8,128)(2,1)}, bf16[4,196,768]{2,1,0:...) custom-call(s32[1]{0:T(128)} %bitcast.3.clip, ...), custom_call_target="tpu_custom_call" | custom-call | flops 693633024 | tf_op jit(solution)/shard_map/space_forward/pallas_call | solution.py:238
  87.2 1.8 copy.162
  90.1 0.7 pad_maximum_fusion
  90.9 1.6 collective-permute-start
  92.5 13.8 %space_forward.5 = (bf16[4,4,208,768]{3,2,1,0:T(8,128)(2,1)}, bf16[4,196,768]{2,1,0:T(8,128)(2,1)}, bf16[4,196,768]{2,1,0:T(8,128)(2,1)}, bf16[4,196,768]{2,1,0:...) custom-call(s32[1]{0:T(128)} %bitcast.2.clip, ...), custom_call_target="tpu_custom_call", output_to_operand_aliasing={{0}: (4, {})} | custom-call | flops 693633024 | tf_op jit(solution)/shard_map/space_forward/pallas_call | solution.py:238
  106.3 2.8 copy.161
  109.1 5.8 dynamic-slice_bitcast_fusion
  115.5 13.6 %space_forward.6 = (bf16[4,4,208,768]{3,2,1,0:T(8,128)(2,1)}, bf16[4,196,768]{2,1,0:T(8,128)(2,1)}, bf16[4,196,768]{2,1,0:T(8,128)(2,1)}, bf16[4,196,768]{2,1,0:...) custom-call(s32[1]{0:T(128)} %bitcast.clip, ...), custom_call_target="tpu_custom_call", output_to_operand_aliasing={{0}: (4, {})} | custom-call | flops 693633024 | tf_op jit(solution)/shard_map/space_forward/pallas_call | solution.py:238
  129.1 13.9 %space_forward.7 = (bf16[4,4,208,768]{3,2,1,0:T(8,128)(2,1)}, bf16[4,196,768]{2,1,0:T(8,128)(2,1)}, bf16[4,196,768]{2,1,0:T(8,128)(2,1)}, bf16[4,196,768]{2,1,0:...) custom-call(s32[1]{0:T(128)} %bitcast.1.clip, ...), custom_call_target="tpu_custom_call", output_to_operand_aliasing={{0}: (4, {})} | custom-call | flops 693633024 | tf_op jit(solution)/shard_map/space_forward/pallas_call | solution.py:238
  143.0 2.9 copy.159
  145.9 1.6 collective-permute-start.8
  148.1 3.4 collective-permute-done.8
  151.4 0.8 collective-permute-start.1
  152.3 1.6 collective-permute-start.2
  154.1 1.5 copy.160
  156.4 0.7 slice_reduce_fusion
  158.5 2.1 convert_element_type.43.refs_5_
  160.6 41.7 %time_forward.1 = (bf16[3136,768]{1,0:T(8,128)(2,1)}, bf16[3136,768]{1,0:T(8,128)(2,1)}, bf16[3136,768]{1,0:T(8,128)(2,1)}, bf16[3136,768]{1,0:T(8,128)(2,1)}, b...) custom-call(bf16[196,4,768]{2,1,0:T(4,128)(2,1)} %bitcast.107, ...), custom_call_target="tpu_custom_call" | custom-call | flops 2774532096 | tf_op jit(solution)/shard_map/time_forward/pallas_call | solution.py:310
  202.3 20.4 %collective-permute-done.3.refs_3_ = bf16[196,4,768]{2,1,0:T(4,128)(2,1)} collective-permute-done((bf16[196,4,768]{2,1,0:T(4,128)(2,1)}, bf16[196,4,768]{2,1,0:T(4,128)(2,1)}, u32[]{:S(2)}, u32[]{:S(2)}) %collective-permute-start.3) | collective-permute-done | bytes 1204256 | tf_op jit(solution)/shard_map/ppermute | solution.py:1041
  222.7 132.7 %feed_forward.1 = (bf16[196,4,768]{2,1,0:T(4,128)(2,1)}, bf16[196,4,768]{2,1,0:T(4,128)(2,1)}, bf16[196,4,768]{2,1,0:T(4,128)(2,1)}, bf16[196,4,768]{2,1,0:T(4,1...) custom-call(bf16[196,4,768]{2,1,0:T(4,128)(2,1)} %get-tuple-element., ...), custom_call_target="tpu_custom_call" | custom-call | flops 9248440320 | tf_op jit(solution)/shard_map/feed_forward/pallas_call | solution.py:395
  355.5 66.9 %time_back.1 = (bf16[196,4,768]{2,1,0:T(4,128)(2,1)}, bf16[196,4,768]{2,1,0:T(4,128)(2,1)}, bf16[196,4,768]{2,1,0:T(4,128)(2,1)}, bf16[196,4,768]{2,1,0:T(4,128)...) custom-call(f32[3136,768]{1,0:T(8,128)} %get-tuple-element.134.refs_0_, ...), custom_call_target="tpu_custom_call" | custom-call | flops 4855431168 | tf_op jit(solution)/shard_map/time_back/pallas_call | solution.py:482
  422.4 0.8 collective-permute-start.9
  423.2 1.5 collective-permute-start.10
  424.7 2.4 copy.157
  427.2 12.9 %space_back.4 = (bf16[4,4,208,2304]{3,2,1,0:T(8,128)(2,1)}, f32[768,768]{1,0:T(8,128)}, f32[1,768]{1,0:T(1,128)}) custom-call(bf16[4,196,768]{2,1,0:T(8,128)(2,1)} %bitcast.100, bf16[4,196,768]{2,1,0:T(8,128)(2,1)} %get-tuple-element.149.q_ref, bf16[4,196,768]{2,1,0:T(8,128)(2,1)} %get-tuple-element.150.k_ref, ...), custom_call_target="tpu_custom_call" | custom-call | flops 693633024 | tf_op jit(solution)/shard_map/space_back/pallas_call | solution.py:540
  440.1 1.2 copy.158
  441.3 13.2 %space_back.5 = (bf16[4,4,208,2304]{3,2,1,0:T(8,128)(2,1)}, f32[768,768]{1,0:T(8,128)}, f32[1,768]{1,0:T(1,128)}) custom-call(bf16[4,196,768]{2,1,0:T(8,128)(2,1)} %bitcast.94, bf16[4,196,768]{2,1,0:T(8,128)(2,1)} %get-tuple-element.143.q_ref, bf16[4,196,768]{2,1,0:T(8,128)(2,1)} %get-tuple-element.144.k_ref, ...), custom_call_target="tpu_custom_call", output_to_operand_aliasing={{0}: (7, {})} | custom-call | flops 693633024 | tf_op jit(solution)/shard_map/space_back/pallas_call | solution.py:540
  454.5 12.4 %collective-permute-done.10 = bf16[196,4,768]{2,1,0:T(4,128)(2,1)S(1)} collective-permute-done((bf16[196,4,768]{2,1,0:T(4,128)(2,1)}, bf16[196,4,768]{2,1,0:T(4,128)(2,1)S(1)}, u32[]{:S(2)}, u32[]{:S(2)}) %collective-permute-start.10) | collective-permute-done | bytes 1204256 | tf_op jit(solution)/shard_map/ppermute | solution.py:1041
  466.9 1.2 copy.156
  468.0 13.1 %space_back.6 = (bf16[4,4,208,2304]{3,2,1,0:T(8,128)(2,1)}, f32[768,768]{1,0:T(8,128)}, f32[1,768]{1,0:T(1,128)}) custom-call(bf16[4,196,768]{2,1,0:T(8,128)(2,1)} %bitcast.96, bf16[4,196,768]{2,1,0:T(8,128)(2,1)} %get-tuple-element.158.q_ref, bf16[4,196,768]{2,1,0:T(8,128)(2,1)} %get-tuple-element.159.k_ref, ...), custom_call_target="tpu_custom_call", output_to_operand_aliasing={{0}: (7, {})} | custom-call | flops 693633024 | tf_op jit(solution)/shard_map/space_back/pallas_call | solution.py:540
  481.1 19.4 %collective-permute-done.11 = bf16[196,4,768]{2,1,0:T(4,128)(2,1)S(1)} collective-permute-done((bf16[196,4,768]{2,1,0:T(4,128)(2,1)}, bf16[196,4,768]{2,1,0:T(4,128)(2,1)S(1)}, u32[]{:S(2)}, u32[]{:S(2)}) %collective-permute-start.11) | collective-permute-done | bytes 1204256 | tf_op jit(solution)/shard_map/ppermute | solution.py:1041
  500.5 1.1 copy.155
  501.7 17.5 %space_part.1 = (f32[768,2304]{1,0:T(8,128)}, f32[1,2304]{1,0:T(1,128)}) custom-call(bf16[4,4,208,768]{3,2,1,0:T(8,128)(2,1)} %get-tuple-element.173.in_ref, bf16[4,4,208,2304]{3,2,1,0:T(8,128)(2,1)} %get-tuple-element.176.proj_ref.refs_0_), custom_call_target="tpu_custom_call" | custom-call | flops 1656225792 | tf_op jit(solution)/shard_map/space_part/pallas_call | solution.py:580
  519.2 13.2 %space_back.7 = (bf16[4,4,208,2304]{3,2,1,0:T(8,128)(2,1)}, f32[768,768]{1,0:T(8,128)}, f32[1,768]{1,0:T(1,128)}) custom-call(bf16[4,196,768]{2,1,0:T(8,128)(2,1)} %bitcast.98, bf16[4,196,768]{2,1,0:T(8,128)(2,1)} %get-tuple-element.167.q_ref, bf16[4,196,768]{2,1,0:T(8,128)(2,1)} %get-tuple-element.168.k_ref, ...), custom_call_target="tpu_custom_call", output_to_operand_aliasing={{0}: (7, {})} | custom-call | flops 693633024 | tf_op jit(solution)/shard_map/space_back/pallas_call | solution.py:540
  532.9 1.4 collective-permute-start.14
  534.3 0.7 pad_add_fusion.order
  535.5 0.7 reduce.7
  536.8 17.0 %space_weights.1 = (bf16[768,6144]{1,0:T(8,128)(2,1)}, f32[768,128]{1,0:T(8,128)}) custom-call(bf16[4,4,208,768]{3,2,1,0:T(8,128)(2,1)} %get-tuple-element.173.in_ref, bf16[4,4,208,2304]{3,2,1,0:T(8,128)(2,1)} %get-tuple-element.186.proj_ref.projs, f32[768,2304]{1,0:T(8,128)} %get-tuple-element.187.d_before, ...), custom_call_target="tpu_custom_call", output_to_operand_aliasing={{0}: (18, {})} | custom-call | flops 552075264 | tf_op jit(solution)/shard_map/space_weights/pallas_call | solution.py:634
  553.8 93.7 %reduce_rows.1 = (f32[24,2304]{1,0:T(8,128)}, f32[24,768]{1,0:T(8,128)}, f32[24,2304]{1,0:T(8,128)}, f32[24,768]{1,0:T(8,128)}, f32[24,128]{1,0:T(8,128)}, /*index=5*/bf16[4,4,196,768]{3,2,1,0:T(8,128)(2,1)}) custom-call(bf16[8,2,2,24,6144]{4,3,2,1,0:T(8,128)(2,1)} %bitcast.93, f32[8,2,2,24,128]{4,3,2,1,0:T(8,128)} %bitcast.110, ...), custom_call_target="tpu_custom_call" | custom-call | tf_op jit(solution)/shard_map/reduce_rows/pallas_call | solution.py:972
  647.6 1.3 slice.51
  648.8 0.8 slice.58
  650.3 6.5 copy.139
  656.8 0.7 copy.140
  657.5 0.7 copy.141
  658.1 0.7 copy.142
  658.8 0.7 copy.143
  660.1 0.7 slice_reduce_fusion.2
  660.8 1.0 copy-done.2
  662.1 5.7 place_clips.1
  667.9 1.0 slice_convert_fusion
  669.0 0.7 copy.138
  669.8 1.2 copy.144
  671.0 0.8 reshape.121
  671.8 0.7 copy.174
  672.4 0.6 copy.175
  673.1 0.7 copy.176
  673.8 0.6 copy.177
  (93 shorter events, 7.1 us)
Async XLA Ops:
  7.2 153.4 %all-gather.3.cloned.1.call-start = ((), (), s32[]{:S(2)}) async-start(), calls=%async_computation.1 | async-start | bytes 4866048 | tf_op jit(solution)/shard_map/all_gather | solution.py:1019
  8.8 213.9 %all-gather.5.cloned.1.call-start = ((), (), s32[]{:S(2)}) async-start(), calls=%async_computation.2 | async-start | bytes 9732096 | tf_op jit(solution)/shard_map/all_gather | solution.py:1019
  12.9 5.4 copy-start.15
  12.9 5.4 copy-start.16
  12.9 5.5 copy-start.17
  12.9 5.6 copy-start.18
  12.9 5.7 copy-start.19
  12.9 6.0 copy-start.9
  12.9 6.0 copy-start.13
  87.2 1.8 copy-start.8
  87.2 1.9 copy-start.7
  90.9 577.0 %reduce-scatter.2.cloned.1.call-start = ((), (), s32[]{:S(2)}) async-start(), calls=%async_computation.3 | async-start | bytes 9732096 | tf_op jit(solution)/shard_map/reduce_scatter | solution.py:1023
  90.9 38.2 %collective-permute-start = (bf16[196,4,768]{2,1,0:T(4,128)(2,1)S(1)}, bf16[196,4,768]{2,1,0:T(4,128)(2,1)S(1)}, u32[]{:S(2)}, u32[]{:S(2)}) collective-permute-start(bf16[196,4,768]{2,1,0:T(4,128)(2,1)S(1)} %bitcast.106), channel_id=1, source_target_pairs={{0,3},{1,2},{2,1},{3,0},{4,7},{5,6},{6,5},{7,4},{8,11},{9,10},{10,... | collective-permute-start | bytes 3612680 | tf_op jit(solution)/shard_map/ppermute | solution.py:1041
  114.9 45.7 %collective-permute-start.5 = (bf16[196,4,768]{2,1,0:T(4,128)(2,1)}, bf16[196,4,768]{2,1,0:T(4,128)(2,1)}, u32[]{:S(2)}, u32[]{:S(2)}) collective-permute-start(bf16[196,4,768]{2,1,0:T(4,128)(2,1)} %bitcast.79), channel_id=1, source_target_pairs={{0,2},{1,3},{2,0},{3,1},{4,6},{5,7},{6,4},{7,5},{8,10},{9,11},{10,... | collective-permute-start | bytes 3612680 | tf_op jit(solution)/shard_map/ppermute | solution.py:1041
  129.1 13.9 %copy-start.20 = (bf16[196,4,768]{2,1,0:T(4,128)(2,1)}, bf16[196,4,768]{2,1,0:T(4,128)(2,1)S(1)}, u32[]{:S(2)}) copy-start(bf16[196,4,768]{2,1,0:T(4,128)(2,1)S(1)} %collective-permute-done.refs_3_) | copy-start | bytes 3612676
  143.0 2.9 copy-start.12
  143.0 11.1 %copy-start = (bf16[4,196,768]{2,1,0:T(8,128)(2,1)S(1)}, bf16[4,196,768]{2,1,0:T(8,128)(2,1)}, u32[]{:S(2)}) copy-start(bf16[4,196,768]{2,1,0:T(8,128)(2,1)} %get-tuple-element.127) | copy-start | bytes 3612676
  145.9 14.7 %collective-permute-start.4 = (bf16[196,4,768]{2,1,0:T(4,128)(2,1)}, bf16[196,4,768]{2,1,0:T(4,128)(2,1)}, u32[]{:S(2)}, u32[]{:S(2)}) collective-permute-start(bf16[196,4,768]{2,1,0:T(4,128)(2,1)} %bitcast.77), channel_id=1, source_target_pairs={{0,1},{1,0},{2,3},{3,2},{4,5},{5,4},{6,7},{7,6},{8,9},{9,8},{10,11... | collective-permute-start | bytes 3612680 | tf_op jit(solution)/shard_map/ppermute | solution.py:1041
  145.9 5.5 collective-permute-start.8
  147.5 4.8 collective-permute-start.7
  148.0 5.8 collective-permute-start.6
  151.4 50.8 %collective-permute-start.1 = (bf16[196,4,768]{2,1,0:T(4,128)(2,1)}, bf16[196,4,768]{2,1,0:T(4,128)(2,1)S(1)}, u32[]{:S(2)}, u32[]{:S(2)}) collective-permute-start(bf16[196,4,768]{2,1,0:T(4,128)(2,1)} %get-tuple-element.124), channel_id=1, source_target_pairs={{0,1},{1,0},{2,3},{3,2},{4,5},{5,4},{6,7},{7,6},{8,9},{9,8},{10,11... | collective-permute-start | bytes 3612680 | tf_op jit(solution)/shard_map/ppermute | solution.py:1041
  152.3 50.0 %collective-permute-start.2 = (bf16[196,4,768]{2,1,0:T(4,128)(2,1)}, bf16[196,4,768]{2,1,0:T(4,128)(2,1)}, u32[]{:S(2)}, u32[]{:S(2)}) collective-permute-start(bf16[196,4,768]{2,1,0:T(4,128)(2,1)} %get-tuple-element.125), channel_id=1, source_target_pairs={{0,2},{1,3},{2,0},{3,1},{4,6},{5,7},{6,4},{7,5},{8,10},{9,11},{10,... | collective-permute-start | bytes 3612680 | tf_op jit(solution)/shard_map/ppermute | solution.py:1041
  153.8 68.9 %collective-permute-start.3 = (bf16[196,4,768]{2,1,0:T(4,128)(2,1)}, bf16[196,4,768]{2,1,0:T(4,128)(2,1)}, u32[]{:S(2)}, u32[]{:S(2)}) collective-permute-start(bf16[196,4,768]{2,1,0:T(4,128)(2,1)} %get-tuple-element.126), channel_id=1, source_target_pairs={{0,3},{1,2},{2,1},{3,0},{4,7},{5,6},{6,5},{7,4},{8,11},{9,10},{10,... | collective-permute-start | bytes 3612680 | tf_op jit(solution)/shard_map/ppermute | solution.py:1041
  202.3 20.4 %copy-start.1 = (bf16[196,4,768]{2,1,0:T(4,128)(2,1)}, bf16[196,4,768]{2,1,0:T(4,128)(2,1)S(1)}, u32[]{:S(2)}) copy-start(bf16[196,4,768]{2,1,0:T(4,128)(2,1)S(1)} %collective-permute-done.1.refs_1_) | copy-start | bytes 3612676
  422.4 17.7 %collective-permute-start.9 = (bf16[196,4,768]{2,1,0:T(4,128)(2,1)}, bf16[196,4,768]{2,1,0:T(4,128)(2,1)S(1)}, u32[]{:S(2)}, u32[]{:S(2)}) collective-permute-start(bf16[196,4,768]{2,1,0:T(4,128)(2,1)} %get-tuple-element.142), channel_id=1, source_target_pairs={{0,1},{1,0},{2,3},{3,2},{4,5},{5,4},{6,7},{7,6},{8,9},{9,8},{10,11... | collective-permute-start | bytes 3612680 | tf_op jit(solution)/shard_map/ppermute | solution.py:1041
  423.2 43.7 %collective-permute-start.10 = (bf16[196,4,768]{2,1,0:T(4,128)(2,1)}, bf16[196,4,768]{2,1,0:T(4,128)(2,1)S(1)}, u32[]{:S(2)}, u32[]{:S(2)}) collective-permute-start(bf16[196,4,768]{2,1,0:T(4,128)(2,1)} %get-tuple-element.156), channel_id=1, source_target_pairs={{0,2},{1,3},{2,0},{3,1},{4,6},{5,7},{6,4},{7,5},{8,10},{9,11},{10,... | collective-permute-start | bytes 3612680 | tf_op jit(solution)/shard_map/ppermute | solution.py:1041
  424.7 75.8 %collective-permute-start.11 = (bf16[196,4,768]{2,1,0:T(4,128)(2,1)}, bf16[196,4,768]{2,1,0:T(4,128)(2,1)S(1)}, u32[]{:S(2)}, u32[]{:S(2)}) collective-permute-start(bf16[196,4,768]{2,1,0:T(4,128)(2,1)} %get-tuple-element.165), channel_id=1, source_target_pairs={{0,3},{1,2},{2,1},{3,0},{4,7},{5,6},{6,5},{7,4},{8,11},{9,10},{10,... | collective-permute-start | bytes 3612680 | tf_op jit(solution)/shard_map/ppermute | solution.py:1041
  519.2 16.3 %copy-start.14 = (f32[1,3072]{1,0:T(1,128)S(1)}, f32[1,3072]{1,0:T(1,128)}, u32[]{:S(2)}) copy-start(f32[1,3072]{1,0:T(1,128)} %get-tuple-element.191) | copy-start | bytes 36868
  532.4 128.3 %collective-permute-start.12 = (bf16[196,4,768]{2,1,0:T(4,128)(2,1)}, bf16[196,4,768]{2,1,0:T(4,128)(2,1)S(1)}, u32[]{:S(2)}, u32[]{:S(2)}) collective-permute-start(bf16[196,4,768]{2,1,0:T(4,128)(2,1)} %get-tuple-element.183), channel_id=1, source_target_pairs={{0,1},{1,0},{2,3},{3,2},{4,5},{5,4},{6,7},{7,6},{8,9},{9,8},{10,11... | collective-permute-start | bytes 3612680 | tf_op jit(solution)/shard_map/ppermute | solution.py:1041
  532.6 128.2 %collective-permute-start.13 = (bf16[196,4,768]{2,1,0:T(4,128)(2,1)}, bf16[196,4,768]{2,1,0:T(4,128)(2,1)S(1)}, u32[]{:S(2)}, u32[]{:S(2)}) collective-permute-start(bf16[196,4,768]{2,1,0:T(4,128)(2,1)} %get-tuple-element.184), channel_id=1, source_target_pairs={{0,2},{1,3},{2,0},{3,1},{4,6},{5,7},{6,4},{7,5},{8,10},{9,11},{10,... | collective-permute-start | bytes 3612680 | tf_op jit(solution)/shard_map/ppermute | solution.py:1041
  532.9 127.8 %collective-permute-start.14 = (bf16[196,4,768]{2,1,0:T(4,128)(2,1)}, bf16[196,4,768]{2,1,0:T(4,128)(2,1)}, u32[]{:S(2)}, u32[]{:S(2)}) collective-permute-start(bf16[196,4,768]{2,1,0:T(4,128)(2,1)} %get-tuple-element.185), channel_id=1, source_target_pairs={{0,3},{1,2},{2,1},{3,0},{4,7},{5,6},{6,5},{7,4},{8,11},{9,10},{10,... | collective-permute-start | bytes 3612680 | tf_op jit(solution)/shard_map/ppermute | solution.py:1041
  650.3 6.5 copy-start.4
  660.7 1.0 copy-start.2
  660.8 1.4 copy-start.3
  669.8 2.0 copy-start.6
  669.8 2.7 copy-start.11
  669.8 3.3 copy-start.5
  671.0 2.8 copy-start.10
Sparse Core Ops, SparseCore 0:
  11.5 84.7 all-gather.2
  99.8 109.7 all-gather.4
  355.6 170.2 reduce-scatter.1
